TPU v7x, 512 devices: a whole 4x4x16 slice. The times are simulated.
512 devices in a mesh: rep: 16 (over x, y), fsdp: 32 (over z, core).
Axes of the slice: x: 4, y: 4, z: 16, core: 2. Of those that a mesh axis runs over, the one named last changes fastest.
Arguments:
- grads: bfloat16 [16, 4096, 5120], P('rep', 'fsdp'), may hold values from -6 to 6
- errors: bfloat16 [16, 4096, 5120], P('rep', 'fsdp'), may hold values from -4 to 4
- q_start: float32 [64, 5120], replicated, may hold values from -6 to 6
Outputs:
- new_errors: bfloat16 [16, 4096, 5120], P('rep', 'fsdp')
- factor_q: float32 [64, 5120], replicated
All inputs are finite; a program needn't handle non-finite values.
Results may differ from a plain program's by a relative error of at most 0.001.
Values sent between devices are 32-bit elements; how exact they have to be, the bound alone decides.
No kernel may reach another device: no remote copies, remote signals or barrier semaphores. Data moves between devices by JAX's collectives and lax.ppermute only.
A program may use at most 64 MiB of HBM per device.

v0:
```python
import jax
import jax.numpy as jnp
from jax import lax
from jax.sharding import PartitionSpec as P

ITERS = 3


def cholesky_step(left, gram):
    lower = jnp.linalg.cholesky(gram)
    return lax.linalg.triangular_solve(lower, left, left_side=False, lower=True, transpose_a=True)


def inner_gram(left):
    return jnp.dot(
        left.T, left, precision=lax.Precision.HIGHEST, preferred_element_type=jnp.float32
    )


def body(grads, errors, q_start):
    merged = grads[0].astype(jnp.float32) + errors[0].astype(jnp.float32)
    row_count = merged.shape[0]
    scale = 1.0 / lax.axis_size("rep")
    factor_q = q_start
    basis = jnp.zeros((row_count, q_start.shape[0]), jnp.float32)
    for step in range(ITERS):
        local_left = lax.dot_general(
            merged,
            factor_q,
            (((1,), (1,)), ((), ())),
            precision=lax.Precision.HIGHEST,
            preferred_element_type=jnp.float32,
        )
        summed_left = lax.psum(local_left, "rep")
        basis = summed_left
        for turn in range(2):
            gram = lax.psum(inner_gram(basis), "fsdp")
            basis = cholesky_step(basis, gram)
        partial_right = lax.dot_general(
            basis,
            merged,
            (((0,), (0,)), ((), ())),
            precision=lax.Precision.HIGHEST,
            preferred_element_type=jnp.float32,
        )
        total_right = lax.psum(partial_right, ("rep", "fsdp"))
        factor_q = total_right * scale
    product = jnp.dot(
        basis, factor_q, precision=lax.Precision.HIGHEST, preferred_element_type=jnp.float32
    )
    new_errors = (merged - product).astype(jnp.bfloat16)
    return (new_errors[None], factor_q)


def solution(mesh):
    placed = (P("rep", "fsdp", None), P("rep", "fsdp", None), P())
    return jax.shard_map(
        body, mesh=mesh, in_specs=placed, out_specs=(P("rep", "fsdp", None), P()), check_vma=False
    )
```

profile of v0, /device:TPU:1, one launch (start us, length us, event | category | flops | bytes accessed | tf_op | source)
XLA Modules:
  0.0 2273.6 jit_solution(3520358346742440806)
XLA Ops:
  8.5 4.7 fusion.12
  13.2 61.6 %psum.84 = f32[128,64]{0,1:T(8,128)S(1)} all-reduce(f32[128,64]{0,1:T(8,128)S(1)} %fusion.12), channel_id=1, replica_groups=mesh['rep'=16,'fsdp'=32] {'rep'}, use_global_device_ids=true, to_apply=%region_0.0 | all-reduce | flops 8192 | bytes 65536 | tf_op jit(solution)/shard_map/psum | solution.py:34
  75.0 107.6 %psum.85 = f32[64,64]{0,1:T(8,128)S(1)} all-reduce(f32[64,64]{0,1:T(8,128)S(1)} %fusion.48), channel_id=1, replica_groups=mesh['rep'=16,'fsdp'=32] {'fsdp'}, use_global_device_ids=true, to_apply=%region_1.0 | all-reduce | flops 4096 | bytes 32768 | tf_op jit(solution)/shard_map/psum | solution.py:37
  182.7 5.8 cholesky.104
  189.9 4.9 custom-call.10
  195.3 90.0 %psum.86 = f32[64,64]{0,1:T(8,128)S(1)} all-reduce(f32[64,64]{0,1:T(8,128)S(1)} %fusion.49), channel_id=1, replica_groups=mesh['rep'=16,'fsdp'=32] {'fsdp'}, use_global_device_ids=true, to_apply=%region_4.7 | all-reduce | flops 4096 | bytes 32768 | tf_op jit(solution)/shard_map/psum | solution.py:37
  285.4 5.8 cholesky.115
  292.6 4.9 custom-call.11
  297.7 4.2 fusion.10
  302.0 463.5 %all-reduce.4.cloned.1.call-done = f32[64,5120]{1,0:T(8,128)} async-done(((f32[64,5120]{1,0:T(8,128)}), f32[64,5120]{1,0:T(8,128)}) %all-reduce.4.cloned.1.call-update) | async-done | bytes 1310736 | tf_op jit(solution)/shard_map/psum | solution.py:46
  765.5 4.6 fusion.8
  770.1 59.5 %psum.88 = f32[128,64]{0,1:T(8,128)S(1)} all-reduce(f32[128,64]{0,1:T(8,128)S(1)} %fusion.8), channel_id=1, replica_groups=mesh['rep'=16,'fsdp'=32] {'rep'}, use_global_device_ids=true, to_apply=%region_6.9 | all-reduce | flops 8192 | bytes 65536 | tf_op jit(solution)/shard_map/psum | solution.py:34
  829.9 99.9 %psum.89 = f32[64,64]{0,1:T(8,128)S(1)} all-reduce(f32[64,64]{0,1:T(8,128)S(1)} %fusion.50), channel_id=1, replica_groups=mesh['rep'=16,'fsdp'=32] {'fsdp'}, use_global_device_ids=true, to_apply=%region_7.10 | all-reduce | flops 4096 | bytes 32768 | tf_op jit(solution)/shard_map/psum | solution.py:37
  929.9 5.8 cholesky.126
  937.1 4.9 custom-call.12
  942.4 90.0 %psum.90 = f32[64,64]{0,1:T(8,128)S(1)} all-reduce(f32[64,64]{0,1:T(8,128)S(1)} %fusion.51), channel_id=1, replica_groups=mesh['rep'=16,'fsdp'=32] {'fsdp'}, use_global_device_ids=true, to_apply=%region_8.11 | all-reduce | flops 4096 | bytes 32768 | tf_op jit(solution)/shard_map/psum | solution.py:37
  1032.5 5.8 cholesky.137
  1039.7 4.9 custom-call.13
  1044.9 4.2 fusion.6
  1049.1 464.6 %all-reduce.6.cloned.1.call-done = f32[64,5120]{1,0:T(8,128)} async-done(((f32[64,5120]{1,0:T(8,128)}), f32[64,5120]{1,0:T(8,128)}) %all-reduce.6.cloned.1.call-update) | async-done | bytes 1310736 | tf_op jit(solution)/shard_map/psum | solution.py:46
  1513.7 4.6 fusion.4
  1518.3 59.6 %psum.92 = f32[128,64]{0,1:T(8,128)S(1)} all-reduce(f32[128,64]{0,1:T(8,128)S(1)} %fusion.4), channel_id=1, replica_groups=mesh['rep'=16,'fsdp'=32] {'rep'}, use_global_device_ids=true, to_apply=%region_10.13 | all-reduce | flops 8192 | bytes 65536 | tf_op jit(solution)/shard_map/psum | solution.py:34
  1578.1 99.7 %psum.93 = f32[64,64]{0,1:T(8,128)S(1)} all-reduce(f32[64,64]{0,1:T(8,128)S(1)} %fusion.52), channel_id=1, replica_groups=mesh['rep'=16,'fsdp'=32] {'fsdp'}, use_global_device_ids=true, to_apply=%region_11.14 | all-reduce | flops 4096 | bytes 32768 | tf_op jit(solution)/shard_map/psum | solution.py:37
  1677.9 5.8 cholesky.148
  1685.1 4.9 custom-call.14
  1690.4 90.2 %psum.94 = f32[64,64]{0,1:T(8,128)S(1)} all-reduce(f32[64,64]{0,1:T(8,128)S(1)} %fusion.53), channel_id=1, replica_groups=mesh['rep'=16,'fsdp'=32] {'fsdp'}, use_global_device_ids=true, to_apply=%region_12.15 | all-reduce | flops 4096 | bytes 32768 | tf_op jit(solution)/shard_map/psum | solution.py:37
  1780.8 5.8 cholesky.159
  1788.0 4.9 custom-call.15
  1793.1 4.2 fusion.2
  1797.3 464.5 %all-reduce.8.cloned.1.call-done = f32[64,5120]{1,0:T(8,128)} async-done(((f32[64,5120]{1,0:T(8,128)}), f32[64,5120]{1,0:T(8,128)}) %all-reduce.8.cloned.1.call-update) | async-done | bytes 1310736 | tf_op jit(solution)/shard_map/psum | solution.py:46
  2261.8 1.5 broadcast_multiply_fusion
  2263.6 3.5 fusion.1
  (56 shorter events, 12.7 us)
Async XLA Ops:
  7.2 1.3 copy-start
  7.2 758.3 %all-reduce.4.cloned.1.call-start = ((), (), s32[]{:S(2)}) async-start(), calls=%async_computation | async-start | bytes 2621440 | tf_op jit(solution)/shard_map/psum | solution.py:46
  8.5 289.2 %copy-start.1 = (bf16[1,128,5120]{2,1,0:T(8,128)(2,1)S(1)}, bf16[1,128,5120]{2,1,0:T(8,128)(2,1)}, u32[]{:S(2)}) copy-start(bf16[1,128,5120]{2,1,0:T(8,128)(2,1)} %param.7) | copy-start | bytes 3932164
  301.9 1211.8 %all-reduce.6.cloned.1.call-start = ((), (), s32[]{:S(2)}) async-start(), calls=%async_computation.1 | async-start | bytes 2621440 | tf_op jit(solution)/shard_map/psum | solution.py:46
  1049.1 1212.8 %all-reduce.8.cloned.1.call-start = ((), (), s32[]{:S(2)}) async-start(), calls=%async_computation.2 | async-start | bytes 2621440 | tf_op jit(solution)/shard_map/psum | solution.py:46
  2261.8 1.7 copy-start.2
  2263.6 3.5 copy-start.3
Sparse Core Ops, SparseCore 0:
  302.0 463.4 all-reduce.3
  1049.2 464.5 all-reduce.5
  1797.4 464.3 all-reduce.7
where the time goes:
time: 2270 us
  waiting for transfers between devices  1390 us (61%)
  blocking collectives  758 us (33%)
  other arithmetic  74 us (3%)
  matrix products  32.6 us (1%)
    psum x3, waiting for transfers between devices, body(): total_right = lax.psum(partial_right, ('rep', 'fsdp'))  1390 us
    psum x6, blocking collectives, body(): gram = lax.psum(inner_gram(basis), 'fsdp')  578 us
    psum x3, blocking collectives, body(): summed_left = lax.psum(local_left, 'rep')  181 us
  transfers between devices with their start and end apart: 3, of which 3 were waited for; matrix products, arithmetic and copies ran while one was open for 0% of the time, Pallas kernels for 0%

commit v1 on v0

v1 whole, which is shorter than its diff:
```python
import jax
import jax.numpy as jnp
from jax import lax
from jax.experimental import pallas as pl
from jax.experimental.pallas import tpu as pltpu
from jax.sharding import Mesh, PartitionSpec as P

ITERS = 3
F32 = jnp.float32
BF16 = jnp.bfloat16
LANES = 128
VMEM = 56 * 1024 * 1024
NT = (((1,), (1,)), ((), ()))
NN = (((1,), (0,)), ((), ()))


def dot(a, b, dims):
    return lax.dot_general(a, b, dims, preferred_element_type=F32)


def split2(x):
    high = x.astype(BF16)
    return high, (x - high.astype(F32)).astype(BF16)


def split3(x):
    high = x.astype(BF16)
    rest = x - high.astype(F32)
    mid = rest.astype(BF16)
    return high, mid, (rest - mid.astype(F32)).astype(BF16)


def params():
    return pltpu.CompilerParams(vmem_limit_bytes=VMEM)


def start_kernel(grads, errors, q_start, out):
    reps, tall, rows = out.shape
    rank, width = q_start.shape
    cut = width // reps
    extra = rank // reps
    left = jnp.zeros((2 * rank, rows), F32)
    for i in range(reps // 2):
        span = pl.ds(2 * cut * i, 2 * cut)
        g, e = grads[:, span], errors[:, span]
        turned = (g.astype(F32) + e.astype(F32)).T
        out[2 * i, :cut, :] = turned[:cut]
        out[2 * i + 1, :cut, :] = turned[cut:]
        high, low = split2(q_start[:, span])
        both = jnp.concatenate([high, low], axis=0)
        left = left + (dot(both, g, NT) + dot(both, e, NT))
    left = left[:rank] + left[rank:]
    for i in range(reps):
        out[i, cut : cut + extra, :] = left[extra * i : extra * (i + 1)]
        out[i, cut + extra :, :] = jnp.zeros((tall - cut - extra, rows), F32)


def start(grads, errors, q_start, reps):
    rows, width = grads.shape
    tall = width // reps + 8
    return pl.pallas_call(
        start_kernel,
        out_shape=jax.ShapeDtypeStruct((reps, tall, rows), F32),
        compiler_params=params(),
        name="start",
    )(grads, errors, q_start)


def parts_kernel(flag, own, other, high, low):
    first = flag[0] == 0
    for core in range(2):
        x = jnp.where(first, own[0], other[0]) if core == 0 else jnp.where(first, other[0], own[0])
        high[core], low[core] = split2(x)


def parts(flag, own, other):
    length, cut, rows = own.shape
    piece = pl.BlockSpec((1, cut, rows), lambda j: (j, 0, 0))
    result = pl.BlockSpec((2, cut, rows), lambda j: (0, 0, j))
    shape = jax.ShapeDtypeStruct((2, cut, length * rows), BF16)
    return pl.pallas_call(
        parts_kernel,
        grid=(length,),
        in_specs=[pl.BlockSpec(memory_space=pltpu.SMEM), piece, piece],
        out_specs=[result, result],
        out_shape=[shape, shape],
        compiler_params=params(),
        name="parts",
    )(flag, own, other)


def inverse_factor(gram_twice):
    rank, wide = gram_twice.shape
    step = 8
    count = rank // step
    row = lax.broadcasted_iota(jnp.int32, (step, wide), 0)
    col = lax.broadcasted_iota(jnp.int32, (step, wide), 1)
    a = []
    for b in range(count):
        unit = (col == row + (rank + b * step)).astype(F32)
        a.append(jnp.where(col < rank, gram_twice[b * step : (b + 1) * step], unit))
    for k in range(rank):
        block, inside = divmod(k, step)
        line = a[block][inside : inside + 1, :]
        line = line * (1.0 / line[:, k : k + 1])
        for b in range(block, count):
            factor = a[b][:, k : k + 1]
            if b == block:
                factor = jnp.where(row[:, :1] > inside, factor, 0.0)
            a[b] = a[b] - factor * line
    done = []
    for b in range(count):
        diagonal = jnp.sum(jnp.where(col == row + b * step, a[b], 0.0), axis=1, keepdims=True)
        done.append(jnp.where(col < rank, 0.0, a[b] * lax.rsqrt(diagonal)))
    w = jnp.concatenate(done, axis=0)
    return w + pltpu.roll(w, rank, 1)


def gram_of(held, chunk):
    rank = held.shape[0] // 4
    total = jnp.zeros((3 * rank, 4 * rank), F32)
    for at in range(0, held.shape[1], chunk):
        x = held[:, at : at + chunk]
        total = total + dot(x[: 3 * rank], x, NT)
    total = total[:rank] + (total[rank : 2 * rank] + total[2 * rank :])
    near, far = total[:, : 2 * rank], total[:, 2 * rank :]
    return near + pltpu.roll(near, rank, 1) + far


def put(held, at, x):
    rank, n = x.shape
    high, mid, low = split3(x)
    span = slice(at, at + n)
    held[:rank, span] = high
    held[rank : 2 * rank, span] = mid
    held[2 * rank : 3 * rank, span] = low
    held[3 * rank :, span] = low


def weights(w):
    rank = w.shape[0]
    col = lax.broadcasted_iota(jnp.int32, w.shape, 1)
    once = jnp.where(col < rank, w, 0.0)
    wide = jnp.concatenate([w, once], axis=1)
    return jnp.concatenate(split3(wide), axis=0)


def right_of(held, high, low, chunk):
    rank = held.shape[0] // 4
    cut, half = high.shape[1:]
    one = jnp.zeros((2 * rank, cut), F32)
    two = jnp.zeros((rank, cut), F32)
    for core in range(2):
        for at in range(0, half, chunk):
            x = held[: 2 * rank, core * half + at : core * half + at + chunk]
            one = one + dot(x, high[core, :, at : at + chunk], NT)
            two = two + dot(x[:rank], low[core, :, at : at + chunk], NT)
    return one[:rank] + (one[rank:] + two)


def orth_and_right(flag, own, other, high, low, held):
    length, rank, rows = own.shape
    chunk = 512
    first = flag[0] == 0
    for core in range(2):
        for j in range(length):
            x = jnp.where(first, own[j], other[j]) if core == 0 else jnp.where(first, other[j], own[j])
            put(held, (core * length + j) * rows, x)
    left = weights(inverse_factor(gram_of(held, chunk)))
    for at in range(0, held.shape[1], chunk):
        y = dot(left, held[:, at : at + chunk], NN)
        put(held, at, y[:rank] + (y[rank : 2 * rank] + y[2 * rank :]))
    second = inverse_factor(gram_of(held, chunk))
    right = right_of(held, high, low, chunk)
    right = jnp.dot(second[:, :rank], right, precision=lax.Precision.HIGHEST, preferred_element_type=F32)
    return second, right


def step_kernel(scale, flag, mine, own, other, high, low, out, held):
    length, rank, rows = own.shape
    _, right = orth_and_right(flag, own, other, high, low, held)
    q_high, q_low = split2(right * scale)
    both = jnp.concatenate([q_high, q_low], axis=0)
    core = mine[0]
    for j in range(length):
        span = slice(j * rows, (j + 1) * rows)
        one = dot(both, high[core, :, span], NN)
        out[j] = one[:rank] + (one[rank:] + dot(q_high, low[core, :, span], NN))


def last_kernel(scale, flag, place, own, other, high, low, out, basis, held):
    length, rank, rows = own.shape
    second, right = orth_and_right(flag, own, other, high, low, held)
    out[:, : right.shape[1]] = right * scale
    out[:, right.shape[1] :] = jnp.zeros((rank, out.shape[1] - right.shape[1]), F32)
    at = pl.multiple_of(place[0] * rows, rows)
    y = dot(weights(second), held[:, pl.ds(at, rows)], NN)
    basis[...] = y[:rank] + (y[rank : 2 * rank] + y[2 * rank :])


def iterate(scale, flag, index, own, other, high, low, last):
    length, rank, rows = own.shape
    cut = high.shape[1]
    if last:
        wide = -(-cut // LANES) * LANES
        out_shape = [jax.ShapeDtypeStruct((rank, wide), F32), jax.ShapeDtypeStruct((rank, rows), F32)]
    else:
        out_shape = jax.ShapeDtypeStruct((length, rank, rows), F32)
    kernel = last_kernel if last else step_kernel
    smem = pl.BlockSpec(memory_space=pltpu.SMEM)
    vmem = pl.BlockSpec(memory_space=pltpu.VMEM)
    return pl.pallas_call(
        lambda *refs: kernel(scale, *refs),
        in_specs=[smem, smem, vmem, vmem, vmem, vmem],
        out_shape=out_shape,
        scratch_shapes=[pltpu.VMEM((4 * rank, 2 * length * rows), BF16)],
        compiler_params=params(),
        name="last" if last else "step",
    )(flag, index, own, other, high, low)


def finish_kernel(flag, grads, errors, own, other, basis, new_errors, factor_q):
    rank, wide = basis.shape[0], own.shape[2]
    half = own.shape[1]
    cut = factor_q.shape[1] // 2
    first = flag[0] == 0
    top = jnp.where(first, own[...], other[...])
    low = jnp.where(first, other[...], own[...])
    a = jnp.concatenate([top[0], low[0]], axis=0)
    b = pltpu.roll(jnp.concatenate([top[1], low[1]], axis=0), cut % LANES, 1)
    whole = cut // LANES * LANES
    lane = lax.broadcasted_iota(jnp.int32, (rank, LANES), 1)
    seam = jnp.where(lane < cut % LANES, a[:, whole:], b[:, :LANES])
    q = jnp.concatenate([a[:, :whole], seam, b[:, LANES:]], axis=1)
    factor_q[...] = q
    q_high, q_low = split2(q)
    b_high, b_low = split2(basis[...].T)
    left = jnp.concatenate([b_high, b_high, b_low], axis=1)
    product = dot(left, jnp.concatenate([q_high, q_low, q_high], axis=0), NN)
    merged = grads[...].astype(F32) + errors[...].astype(F32)
    new_errors[...] = (merged - product).astype(BF16)


def finish(flag, grads, errors, own, other, basis):
    rows, width = grads.shape
    reps, half, wide = own.shape
    rank = basis.shape[0]
    block = 2 * width // reps
    cols = pl.BlockSpec((rows, block), lambda i: (0, i))
    pair = pl.BlockSpec((2, half, wide), lambda i: (i, 0, 0))
    return pl.pallas_call(
        finish_kernel,
        grid=(reps // 2,),
        in_specs=[
            pl.BlockSpec(memory_space=pltpu.SMEM),
            cols,
            cols,
            pair,
            pair,
            pl.BlockSpec((rank, rows), lambda i: (0, 0)),
        ],
        out_specs=[cols, pl.BlockSpec((rank, block), lambda i: (0, i))],
        out_shape=[jax.ShapeDtypeStruct((rows, width), BF16), jax.ShapeDtypeStruct((rank, width), F32)],
        compiler_params=params(),
        name="finish",
    )(flag, grads, errors, own, other, basis)


def exchange(chunks, axis):
    return lax.all_to_all(chunks, axis, 0, 0)


def gather(block, axis, count):
    return exchange(jnp.broadcast_to(block[None], (count,) + block.shape), axis)


def swap_cores(block):
    return lax.ppermute(block, "core", [(0, 1), (1, 0)])


def body(grads, errors, q_start):
    grads, errors = grads[0], errors[0]
    rows, width = grads.shape
    rank = q_start.shape[0]
    reps, length = lax.axis_size("rep"), lax.axis_size("z")
    core, place = lax.axis_index("core"), lax.axis_index("z")
    cut, extra = width // reps, rank // reps
    scale = 1.0 / reps
    flag = core.reshape(1).astype(jnp.int32)
    zero = jnp.zeros((1,), jnp.int32)

    block = jnp.sum(exchange(start(grads, errors, q_start, reps), "rep"), axis=0)
    own_total = lax.all_gather(block[:cut], "z")
    high, low = parts(flag, own_total, swap_cores(own_total))

    piece = block[cut : cut + extra]
    along = gather(piece, ("z", "core"), 2 * length).reshape(2 * length * extra, rows)
    left = gather(along, "rep", reps).reshape(reps, length, 2, extra, rows)
    left = left.transpose(2, 1, 0, 3, 4).reshape(2, length, rank, rows)
    own, other, order = left[0], left[1], zero
    for step in range(ITERS - 1):
        partial = iterate(scale, order, flag, own, other, high, low, False)
        own = gather(jnp.sum(exchange(partial, "rep"), axis=0), "rep", reps)
        other, order = swap_cores(own), flag
    at = (core * length + place).reshape(1).astype(jnp.int32)
    part_q, basis = iterate(scale, order, at, own, other, high, low, True)
    half = lax.dynamic_slice_in_dim(part_q, core * (rank // 2), rank // 2, 0)
    own_q = gather(half, "rep", reps)
    new_errors, factor_q = finish(flag, grads, errors, own_q, swap_cores(own_q), basis)
    return new_errors[None], factor_q


def solution(mesh):
    reps, count = mesh.devices.shape
    split = Mesh(mesh.devices.reshape(reps, count // 2, 2), ("rep", "z", "core"))
    placed = P("rep", ("z", "core"), None)
    return jax.shard_map(
        body, mesh=split, in_specs=(placed, placed, P()), out_specs=(placed, P()), check_vma=False
    )
```

time: 2270 us -> 357 us (0.16)
  waiting for transfers between devices: 1390 us -> 90.6 us
  blocking collectives: 758 us -> 128 us
  Pallas kernels: 0 us -> 80.9 us
  other arithmetic: 74 us -> 0.2 us
  starting transfers between devices: 0.12 us -> 33.9 us
  matrix products: 32.6 us -> 0 us
    psum x3 -> x0, waiting for transfers between devices: 1390 us -> none  [body(): total_right = lax.psum(partial_right, ('rep', 'fsdp'))]
    psum x9 -> x0, blocking collectives: 758 us -> none  [the longest x6 578 us: body(): gram = lax.psum(inner_gram(basis), 'fsdp')]
    all_to_all x0 -> x7, blocking collectives: none -> 128 us  [exchange(): return lax.all_to_all(chunks, axis, 0, 0)]
    pallas_call x0 -> x6, Pallas kernels: none -> 80.9 us  [the longest x3 57.7 us: iterate(): pl.pallas_call(lambda *refs: kernel(scale, *refs), in_specs=[smem, smem,...]
    another operation x30 -> x0, other arithmetic: 72.4 us -> none  [the longest x18 39.1 us: cholesky_step(): lower = jnp.linalg.cholesky(gram)]
    all_gather x0 -> x1, waiting for transfers between devices: none -> 70.9 us  [body(): own_total = lax.all_gather(block[:cut], 'z')]
    dot_general x13 -> x0, matrix products: 31.1 us -> none  [the longest x3 14 us: body(): lax.dot_general(merged, factor_q, (((1,), (1,)), ((), ())), precision=lax...]
    ppermute x0 -> x4, starting transfers between devices: none -> 27.3 us  [swap_cores(): return lax.ppermute(block, 'core', [(0, 1), (1, 0)])]
  transfers between devices with their start and end apart: 3 -> 6, of which waited for: 3 -> 5; matrix products, arithmetic and copies ran while one was open for 0% -> 1% of each run, Pallas kernels for 0% -> 0%
where the time goes in v1:
time: 357 us; the launch traced here: 356 us
  blocking collectives  128 us (36%)
  waiting for transfers between devices  90.6 us (25%)
  Pallas kernels  80.9 us (23%)
  starting transfers between devices  33.9 us (9%)
  between operations  14.1 us (4%)
  local copies, waits for them, and re-layouts  7.95 us (2%)
    all_to_all x7, blocking collectives, exchange(): return lax.all_to_all(chunks, axis, 0, 0)  128 us
    all_gather x1, waiting for transfers between devices, body(): own_total = lax.all_gather(block[:cut], 'z')  70.9 us
    pallas_call x3, Pallas kernels, iterate(): pl.pallas_call(lambda *refs: kernel(scale, *refs), in_specs=[smem, smem,...  57.7 us
    ppermute x4, starting transfers between devices, swap_cores(): return lax.ppermute(block, 'core', [(0, 1), (1, 0)])  27.3 us
    all_to_all x1, waiting for transfers between devices, exchange(): return lax.all_to_all(chunks, axis, 0, 0)  15 us
    pallas_call x1, Pallas kernels, parts(): pl.pallas_call(parts_kernel, grid=(length,), in_specs=[pl.BlockSpec(memor...  11.1 us
    pallas_call x1, Pallas kernels, finish(): pl.pallas_call(finish_kernel, grid=(reps // 2,), in_specs=[pl.BlockSpec(m...  7.31 us
  transfers between devices with their start and end apart: 6, of which 5 were waited for; matrix products, arithmetic and copies ran while one was open for 1% of the time, Pallas kernels for 0%

profile of v1, /device:TPU:1, one launch (start us, length us, event | category | flops | bytes accessed | tf_op | source)
XLA Modules:
  0.0 355.6 jit_solution(13426127446470019403)
XLA Ops:
  7.2 4.7 %start.1 = f32[16,328,128]{2,1,0:T(8,128)} custom-call(bf16[128,5120]{1,0:T(8,128)(2,1)} %bitcast.12, bf16[128,5120]{1,0:T(8,128)(2,1)} %bitcast.14, f32[64,5120]{1,0:T(8,128)} %q_start.1), custom_call_target="tpu_custom_call" | custom-call | tf_op jit(solution)/shard_map/start/pallas_call | solution.py:61
  11.9 39.1 %all_to_all.40 = f32[16,328,128]{2,1,0:T(8,128)S(1)} all-to-all(f32[16,328,128]{2,1,0:T(8,128)} %start.1), channel_id=1, replica_groups=mesh['rep'=16,'z'=16,'core'=2] {'rep'}, dimensions={0} | all-to-all | bytes 5373952 | tf_op jit(solution)/shard_map/all_to_all | solution.py:270
  51.2 0.7 slice.21
  51.9 70.9 %all-gather.3.cloned.1.call-done = f32[5120,128]{1,0:T(8,128)} async-done(((f32[320,128]{1,0:T(8,128)}), f32[5120,128]{1,0:T(8,128)}) %all-gather.3.cloned.1.call-update) | async-done | bytes 2621456 | tf_op jit(solution)/shard_map/all_gather | solution.py:293
  122.7 11.5 %collective-permute-start = (f32[16,320,128]{2,1,0:T(8,128)}, f32[16,320,128]{2,1,0:T(8,128)}, u32[]{:S(2)}, u32[]{:S(2)}) collective-permute-start(f32[16,320,128]{2,1,0:T(8,128)} %bitcast.17), channel_id=1, source_target_pairs={{0,1},{1,0},{2,3},{3,2},{4,5},{5,4},{6,7},{7,6},{8,9},{9,8},{10,11... | collective-permute-start | bytes 7864328 | tf_op jit(solution)/shard_map/ppermute | solution.py:278
  134.3 20.4 %all_to_all.41 = f32[32,4,128]{2,1,0:T(4,128)S(1)} all-to-all(f32[32,4,128]{2,1,0:T(4,128)S(1)} %broadcast_in_dim.14), channel_id=1, replica_groups=mesh['rep'=16,'z'=16,'core'=2] {'z','core'}, dimensions={0} | all-to-all | bytes 131072 | tf_op jit(solution)/shard_map/all_to_all | solution.py:270
  154.7 1.1 broadcast_in_dim.16
  155.8 6.5 %all-to-all-start.2 = ((f32[16,128,128]{2,1,0:T(8,128)}), f32[16,128,128]{2,1,0:T(8,128)S(1)}, u32[]{:S(2)}, u32[]{:S(2)}) async-start(f32[16,128,128]{2,1,0:T(8,128)} %broadcast_in_dim.16), calls=%async_computation.2 | async-start | bytes 2097152 | tf_op jit(solution)/shard_map/all_to_all | solution.py:270
  162.3 15.0 %all-to-all-done.2 = f32[16,128,128]{2,1,0:T(8,128)S(1)} async-done(((f32[16,128,128]{2,1,0:T(8,128)}), f32[16,128,128]{2,1,0:T(8,128)S(1)}, u32[]{:S(2)}, u32[]{:S(2)}) %all-to-all-start.2) | async-done | bytes 1048608 | tf_op jit(solution)/shard_map/all_to_all | solution.py:270
  177.3 0.6 copy.7
  178.0 1.0 copy.8
  179.0 1.0 copy.9
  180.0 11.1 %parts.1 = (bf16[2,320,2048]{2,1,0:T(8,128)(2,1)}, bf16[2,320,2048]{2,1,0:T(8,128)(2,1)}) custom-call(s32[1]{0:T(128)} %bitcast.flag.refs_1_.refs_0_, f32[16,320,128]{2,1,0:T(8,128)} %bitcast.18, f32[16,320,128]{2,1,0:T(8,128)} %collective-permute-done.other), custom_call_target="tpu_custom_call" | custom-call | tf_op jit(solution)/shard_map/parts/pallas_call | solution.py:81
  191.2 19.7 %step.2 = f32[16,64,128]{2,1,0:T(8,128)} custom-call(s32[1]{0:T(128)} %constant.5.clone.1.refs_0_, s32[1]{0:T(128)} %bitcast.flag.refs_1_.refs_0_, f32[16,64,128]{2,1,0:T(8,128)} %bitcast.19, f32[16,64,128]{2,1,0:T(8,128)} %bitcast.20, bf16[2,320,2048]{2,1,0:T(8,128)(2,1)} %get-tuple-element.8.refs_4_, bf16[2,320,2048]{2,1,0:T(8,128)(2,1)} %get-tuple-element.9.refs_5_), custom_call_target="tpu_custom_call" | custom-call | tf_op jit(solution)/shard_map/step/pallas_call | solution.py:212
  210.9 13.5 %all_to_all.42 = f32[16,64,128]{2,1,0:T(8,128)S(1)} all-to-all(f32[16,64,128]{2,1,0:T(8,128)} %step.2), channel_id=1, replica_groups=mesh['rep'=16,'z'=16,'core'=2] {'rep'}, dimensions={0} | all-to-all | bytes 1048576 | tf_op jit(solution)/shard_map/all_to_all | solution.py:270
  224.5 12.0 %all_to_all.43.refs_2_ = f32[16,64,128]{2,1,0:T(8,128)S(1)} all-to-all(f32[16,64,128]{2,1,0:T(8,128)S(1)} %broadcast_in_dim.17), channel_id=1, replica_groups=mesh['rep'=16,'z'=16,'core'=2] {'rep'}, dimensions={0} | all-to-all | bytes 1048576 | tf_op jit(solution)/shard_map/all_to_all | solution.py:270
  236.4 6.7 %collective-permute-start.1 = (f32[16,64,128]{2,1,0:T(8,128)S(1)}, f32[16,64,128]{2,1,0:T(8,128)S(1)}, u32[]{:S(2)}, u32[]{:S(2)}) collective-permute-start(f32[16,64,128]{2,1,0:T(8,128)S(1)} %all_to_all.43.refs_2_), channel_id=1, source_target_pairs={{0,1},{1,0},{2,3},{3,2},{4,5},{5,4},{6,7},{7,6},{8,9},{9,8},{10,11... | collective-permute-start | bytes 1572872 | tf_op jit(solution)/shard_map/ppermute | solution.py:278
  243.2 1.3 collective-permute-done.1.refs_3_
  244.5 0.8 copy-done.4
  245.3 19.7 %step.3 = f32[16,64,128]{2,1,0:T(8,128)} custom-call(s32[1]{0:T(128)} %bitcast.flag.refs_1_.refs_0_, s32[1]{0:T(128)} %bitcast.flag.refs_1_.refs_0_, f32[16,64,128]{2,1,0:T(8,128)} %copy-done.1, f32[16,64,128]{2,1,0:T(8,128)} %copy-done.4, bf16[2,320,2048]{2,1,0:T(8,128)(2,1)} %get-tuple-element.8.refs_4_, bf16[2,320,2048]{2,1,0:T(8,128)(2,1)} %get-tuple-element.9.refs_5_), custom_call_target="tpu_custom_call" | custom-call | tf_op jit(solution)/shard_map/step/pallas_call | solution.py:212
  265.0 13.8 %all_to_all.44 = f32[16,64,128]{2,1,0:T(8,128)S(1)} all-to-all(f32[16,64,128]{2,1,0:T(8,128)} %step.3), channel_id=1, replica_groups=mesh['rep'=16,'z'=16,'core'=2] {'rep'}, dimensions={0} | all-to-all | bytes 1048576 | tf_op jit(solution)/shard_map/all_to_all | solution.py:270
  278.9 12.9 %all_to_all.45.refs_2_ = f32[16,64,128]{2,1,0:T(8,128)S(1)} all-to-all(f32[16,64,128]{2,1,0:T(8,128)S(1)} %broadcast_in_dim.18), channel_id=1, replica_groups=mesh['rep'=16,'z'=16,'core'=2] {'rep'}, dimensions={0} | all-to-all | bytes 1048576 | tf_op jit(solution)/shard_map/all_to_all | solution.py:270
  291.8 5.4 %collective-permute-start.2 = (f32[16,64,128]{2,1,0:T(8,128)S(1)}, f32[16,64,128]{2,1,0:T(8,128)S(1)}, u32[]{:S(2)}, u32[]{:S(2)}) collective-permute-start(f32[16,64,128]{2,1,0:T(8,128)S(1)} %all_to_all.45.refs_2_), channel_id=1, source_target_pairs={{0,1},{1,0},{2,3},{3,2},{4,5},{5,4},{6,7},{7,6},{8,9},{9,8},{10,11... | collective-permute-start | bytes 1572872 | tf_op jit(solution)/shard_map/ppermute | solution.py:278
  297.2 1.5 collective-permute-done.2.refs_3_
  298.7 0.8 copy-done.5
  299.5 18.2 %last.1 = (f32[64,384]{1,0:T(8,128)}, f32[64,128]{1,0:T(8,128)}) custom-call(s32[1]{0:T(128)} %bitcast.flag.refs_1_.refs_0_, s32[1]{0:T(128)} %bitcast.3.refs_1_, f32[16,64,128]{2,1,0:T(8,128)} %copy-done.2, f32[16,64,128]{2,1,0:T(8,128)} %copy-done.5, bf16[2,320,2048]{2,1,0:T(8,128)(2,1)} %get-tuple-element.8.refs_4_, ...), custom_call_target="tpu_custom_call" | custom-call | tf_op jit(solution)/shard_map/last/pallas_call | solution.py:212
  317.8 0.8 constant_dynamic-slice_fusion
  318.7 16.3 %all_to_all.46.own = f32[16,32,384]{2,1,0:T(8,128)S(1)} all-to-all(f32[16,32,384]{2,1,0:T(8,128)S(1)} %broadcast_in_dim.19), channel_id=1, replica_groups=mesh['rep'=16,'z'=16,'core'=2] {'rep'}, dimensions={0} | all-to-all | bytes 1572864 | tf_op jit(solution)/shard_map/all_to_all | solution.py:270
  334.9 3.7 %collective-permute-start.3 = (f32[16,32,384]{2,1,0:T(8,128)S(1)}, f32[16,32,384]{2,1,0:T(8,128)S(1)}, u32[]{:S(2)}, u32[]{:S(2)}) collective-permute-start(f32[16,32,384]{2,1,0:T(8,128)S(1)} %all_to_all.46.own), channel_id=1, source_target_pairs={{0,1},{1,0},{2,3},{3,2},{4,5},{5,4},{6,7},{7,6},{8,9},{9,8},{10,11... | collective-permute-start | bytes 2359304 | tf_op jit(solution)/shard_map/ppermute | solution.py:278
  338.6 1.9 collective-permute-done.3.other
  340.5 0.9 copy-done.3
  341.4 7.3 %finish.1 = (bf16[128,5120]{1,0:T(8,128)(2,1)}, f32[64,5120]{1,0:T(8,128)}) custom-call(s32[1]{0:T(128)} %bitcast.flag.refs_1_.refs_0_, bf16[128,5120]{1,0:T(8,128)(2,1)} %bitcast.13, bf16[128,5120]{1,0:T(8,128)(2,1)} %bitcast.15, f32[16,32,384]{2,1,0:T(8,128)} %copy-done, f32[16,32,384]{2,1,0:T(8,128)} %copy-done.3, f32[64,128]{1,0:T(8,128)} %get-tuple-element.11.basis), custom_call_target="tpu_custom_call" | custom-call | tf_op jit(solution)/shard_map/finish/pallas_call | solution.py:251
  (21 shorter events, 0.6 us)
Async XLA Ops:
  7.2 115.6 %all-gather.3.cloned.1.call-start = ((), (), s32[]{:S(2)}) async-start(), calls=%async_computation.8 | async-start | bytes 2785280 | tf_op jit(solution)/shard_map/all_gather | solution.py:293
  122.7 57.3 %collective-permute-start = (f32[16,320,128]{2,1,0:T(8,128)}, f32[16,320,128]{2,1,0:T(8,128)}, u32[]{:S(2)}, u32[]{:S(2)}) collective-permute-start(f32[16,320,128]{2,1,0:T(8,128)} %bitcast.17), channel_id=1, source_target_pairs={{0,1},{1,0},{2,3},{3,2},{4,5},{5,4},{6,7},{7,6},{8,9},{9,8},{10,11... | collective-permute-start | bytes 7864328 | tf_op jit(solution)/shard_map/ppermute | solution.py:278
  155.8 21.5 %all-to-all-start.2 = ((f32[16,128,128]{2,1,0:T(8,128)}), f32[16,128,128]{2,1,0:T(8,128)S(1)}, u32[]{:S(2)}, u32[]{:S(2)}) async-start(f32[16,128,128]{2,1,0:T(8,128)} %broadcast_in_dim.16), calls=%async_computation.2 | async-start | bytes 2097152 | tf_op jit(solution)/shard_map/all_to_all | solution.py:270
  236.4 8.1 %copy-start.1 = (f32[16,64,128]{2,1,0:T(8,128)}, f32[16,64,128]{2,1,0:T(8,128)S(1)}, u32[]{:S(2)}) copy-start(f32[16,64,128]{2,1,0:T(8,128)S(1)} %all_to_all.43.refs_2_) | copy-start | bytes 1572868
  236.4 8.1 %collective-permute-start.1 = (f32[16,64,128]{2,1,0:T(8,128)S(1)}, f32[16,64,128]{2,1,0:T(8,128)S(1)}, u32[]{:S(2)}, u32[]{:S(2)}) collective-permute-start(f32[16,64,128]{2,1,0:T(8,128)S(1)} %all_to_all.43.refs_2_), channel_id=1, source_target_pairs={{0,1},{1,0},{2,3},{3,2},{4,5},{5,4},{6,7},{7,6},{8,9},{9,8},{10,11... | collective-permute-start | bytes 1572872 | tf_op jit(solution)/shard_map/ppermute | solution.py:278
  244.5 0.8 copy-start.4
  291.8 6.9 %copy-start.2 = (f32[16,64,128]{2,1,0:T(8,128)}, f32[16,64,128]{2,1,0:T(8,128)S(1)}, u32[]{:S(2)}) copy-start(f32[16,64,128]{2,1,0:T(8,128)S(1)} %all_to_all.45.refs_2_) | copy-start | bytes 1572868
  291.8 6.9 %collective-permute-start.2 = (f32[16,64,128]{2,1,0:T(8,128)S(1)}, f32[16,64,128]{2,1,0:T(8,128)S(1)}, u32[]{:S(2)}, u32[]{:S(2)}) collective-permute-start(f32[16,64,128]{2,1,0:T(8,128)S(1)} %all_to_all.45.refs_2_), channel_id=1, source_target_pairs={{0,1},{1,0},{2,3},{3,2},{4,5},{5,4},{6,7},{7,6},{8,9},{9,8},{10,11... | collective-permute-start | bytes 1572872 | tf_op jit(solution)/shard_map/ppermute | solution.py:278
  298.7 0.8 copy-start.5
  334.9 5.6 %copy-start = (f32[16,32,384]{2,1,0:T(8,128)}, f32[16,32,384]{2,1,0:T(8,128)S(1)}, u32[]{:S(2)}) copy-start(f32[16,32,384]{2,1,0:T(8,128)S(1)} %all_to_all.46.own) | copy-start | bytes 2359300
  334.9 5.6 %collective-permute-start.3 = (f32[16,32,384]{2,1,0:T(8,128)S(1)}, f32[16,32,384]{2,1,0:T(8,128)S(1)}, u32[]{:S(2)}, u32[]{:S(2)}) collective-permute-start(f32[16,32,384]{2,1,0:T(8,128)S(1)} %all_to_all.46.own), channel_id=1, source_target_pairs={{0,1},{1,0},{2,3},{3,2},{4,5},{5,4},{6,7},{7,6},{8,9},{9,8},{10,11... | collective-permute-start | bytes 2359304 | tf_op jit(solution)/shard_map/ppermute | solution.py:278
  340.5 0.9 copy-start.3
Sparse Core Ops, SparseCore 0:
  52.0 70.6 all-gather.2

commit v2 on v1

v2 whole, which is shorter than its diff:
```python
import functools

import jax
import jax.numpy as jnp
from jax import lax
from jax.experimental import pallas as pl
from jax.experimental.pallas import tpu as pltpu
from jax.sharding import Mesh, PartitionSpec as P

ITERS = 3
F32 = jnp.float32
BF16 = jnp.bfloat16
LANES = 128
VMEM = 20 * 1024 * 1024
SMEM_SPEC = pl.BlockSpec(memory_space=pltpu.SMEM)
VMEM_SPEC = pl.BlockSpec(memory_space=pltpu.VMEM)
HBM_SPEC = pl.BlockSpec(memory_space=pltpu.HBM)
NT = (((1,), (1,)), ((), ()))
NN = (((1,), (0,)), ((), ()))


def dot(a, b, dims):
    return lax.dot_general(a, b, dims, preferred_element_type=F32)


def split2(x):
    high = x.astype(BF16)
    return high, (x - high.astype(F32)).astype(BF16)


def split3(x):
    high = x.astype(BF16)
    rest = x - high.astype(F32)
    mid = rest.astype(BF16)
    return high, mid, (rest - mid.astype(F32)).astype(BF16)


def params(limit=VMEM):
    return pltpu.CompilerParams(vmem_limit_bytes=limit)


def start_kernel(grads, errors, q_start, out, g_held, e_held, q_held, sems):
    reps, tall, rows = out.shape
    rank, width = q_start.shape
    cut = width // reps
    extra = rank // reps
    spans = [pl.ds(2 * cut * i, 2 * cut) for i in range(reps // 2)]
    loads = []
    for i, span in enumerate(spans):
        pairs = ((grads, g_held), (errors, e_held), (q_start, q_held))
        loads.append(
            [pltpu.make_async_copy(x.at[:, span], y.at[:, span], sems.at[k, i]) for k, (x, y) in enumerate(pairs)]
        )
        for load in loads[-1]:
            load.start()
    left = jnp.zeros((2 * rank, rows), F32)
    for i, span in enumerate(spans):
        for load in loads[i]:
            load.wait()
        g, e = g_held[:, span], e_held[:, span]
        turned = (g.astype(F32) + e.astype(F32)).T
        out[2 * i, :cut, :] = turned[:cut]
        out[2 * i + 1, :cut, :] = turned[cut:]
        high, low = split2(q_held[:, span])
        both = jnp.concatenate([high, low], axis=0)
        left = left + (dot(both, g, NT) + dot(both, e, NT))
    left = left[:rank] + left[rank:]
    for i in range(reps):
        out[i, cut : cut + extra, :] = left[extra * i : extra * (i + 1)]
        out[i, cut + extra :, :] = jnp.zeros((tall - cut - extra, rows), F32)


def start(grads, errors, q_start, reps):
    rows, width = grads.shape
    tall = width // reps + 8
    return pl.pallas_call(
        start_kernel,
        in_specs=[HBM_SPEC] * 3,
        out_specs=VMEM_SPEC,
        out_shape=jax.ShapeDtypeStruct((reps, tall, rows), F32),
        scratch_shapes=[
            pltpu.VMEM(grads.shape, BF16),
            pltpu.VMEM(errors.shape, BF16),
            pltpu.VMEM(q_start.shape, F32),
            pltpu.SemaphoreType.DMA((3, reps // 2)),
        ],
        compiler_params=params(3 * VMEM),
        name="start",
    )(grads, errors, q_start)


def inverse_factor(gram_twice):
    rank, wide = gram_twice.shape
    step = 8
    count = rank // step
    row = lax.broadcasted_iota(jnp.int32, (step, wide), 0)
    col = lax.broadcasted_iota(jnp.int32, (step, wide), 1)
    a = []
    for b in range(count):
        unit = (col == row + (rank + b * step)).astype(F32)
        a.append(jnp.where(col < rank, gram_twice[b * step : (b + 1) * step], unit))

    def spread(x, k):
        return jnp.broadcast_to(x[:, k : k + 1], (step, wide))

    def line_of(x, j):
        return jnp.broadcast_to(x[j : j + 1, :], (step, wide))

    done = []
    for p in range(count):
        panel = a[p]
        f = [spread(panel, p * step + j) for j in range(step)]
        pivots = jnp.ones((step, wide), F32)
        lines, weight = [], []
        for j in range(step):
            pivot = line_of(f[j], j)
            inverse = 1.0 / pivot
            below = jnp.where(row > j, f[j], 0.0)
            line = line_of(panel, j) * inverse
            panel = panel - below * line
            ahead = {}
            for t in range(j + 1, step):
                ahead[t] = line_of(f[t], j) * inverse
                f[t] = f[t] - below * ahead[t]
            pivots = jnp.where(row == j, pivot, pivots)
            lines.append(line)
            weight.append(ahead)
        done.append(jnp.where(col < rank, 0.0, panel * lax.rsqrt(pivots)))
        for b in range(p + 1, count):
            g = [spread(a[b], p * step + j) for j in range(step)]
            for j in range(step):
                for t in range(j + 1, step):
                    g[t] = g[t] - g[j] * weight[j][t]
                a[b] = a[b] - g[j] * lines[j]
    w = jnp.concatenate(done, axis=0)
    return w + pltpu.roll(w, rank, 1)


def gram_of(held, chunk):
    rank = held.shape[0] // 4
    total = jnp.zeros((3 * rank, 4 * rank), F32)
    for at in range(0, held.shape[1], chunk):
        x = held[:, at : at + chunk]
        total = total + dot(x[: 3 * rank], x, NT)
    total = total[:rank] + (total[rank : 2 * rank] + total[2 * rank :])
    near, far = total[:, : 2 * rank], total[:, 2 * rank :]
    return near + pltpu.roll(near, rank, 1) + far


def put(held, at, x):
    rank, n = x.shape
    high, mid, low = split3(x)
    span = pl.ds(at, n)
    held[:rank, span] = high
    held[rank : 2 * rank, span] = mid
    held[2 * rank : 3 * rank, span] = low
    held[3 * rank :, span] = low


def weights(w):
    rank = w.shape[0]
    col = lax.broadcasted_iota(jnp.int32, w.shape, 1)
    once = jnp.where(col < rank, w, 0.0)
    wide = jnp.concatenate([w, once], axis=1)
    return jnp.concatenate(split3(wide), axis=0)


CHUNK = 512


def right_of(held, high, low):
    rank = held.shape[0] // 4
    cut, n = high.shape
    one = jnp.zeros((2 * rank, cut), F32)
    two = jnp.zeros((rank, cut), F32)
    for at in range(0, n, CHUNK):
        x = held[: 2 * rank, at : at + CHUNK]
        one = one + dot(x, high[:, at : at + CHUNK], NT)
        two = two + dot(x[:rank], low[:, at : at + CHUNK], NT)
    return one[:rank] + (one[rank:] + two)


def planes(info, length, mine):
    upward = info[1] == (0 if mine else 1)
    columns = 2 * LANES

    def at(j):
        plane = lax.rem(info[0] + jnp.where(upward, length - j, 1 + j), length)
        return pl.multiple_of(plane * columns, columns)

    return at


def orthonormal(info, own, other, held):
    length = own.shape[0]
    for mine, blocks in ((True, own), (False, other)):
        at = planes(info, length, mine)
        for j in range(length // 2):
            put(held, at(j), jnp.concatenate([blocks[2 * j], blocks[2 * j + 1]], axis=1))
    left = weights(inverse_factor(gram_of(held, CHUNK)))
    for at in range(0, held.shape[1], CHUNK):
        y = dot(left, held[:, at : at + CHUNK], NN)
        put(held, at, y[: y.shape[0] // 3] + (y[y.shape[0] // 3 : 2 * y.shape[0] // 3] + y[2 * y.shape[0] // 3 :]))
    return inverse_factor(gram_of(held, CHUNK))


def right_factor(scale, second, held, high, low):
    left = second[:, : second.shape[0]] * scale
    right = right_of(held, high, low)
    return jnp.dot(left, right, precision=lax.Precision.HIGHEST, preferred_element_type=F32)


def next_left(info, q, high, low, out):
    length, rank, rows = out.shape
    q_high, q_low = split2(q)
    both = jnp.concatenate([q_high, q_low], axis=0)
    at = planes(info, length, True)
    for j in range(length // 2):
        span = pl.ds(at(j), 2 * rows)
        one = dot(both, high[:, span], NN)
        x = one[:rank] + (one[rank:] + dot(q_high, low[:, span], NN))
        out[2 * j] = x[:, :rows]
        out[2 * j + 1] = x[:, rows:]


def first_kernel(scale, info, own, other, total, total_other, out, high_out, low_out, held, high, low, sems):
    length = own.shape[0]
    for mine, blocks in ((True, total), (False, total_other)):
        at = planes(info, length, mine)
        core = info[1] if mine else 1 - info[1]
        for j in range(length // 2):
            for stream in range(2):
                side = core if stream == 0 else 1 - core
                span = pl.ds(pl.multiple_of(at(j) + side * LANES, LANES), LANES)
                high[:, span], low[:, span] = split2(blocks[j, stream])
    stores = [
        pltpu.make_async_copy(high, high_out, sems.at[0]),
        pltpu.make_async_copy(low, low_out, sems.at[1]),
    ]
    for store in stores:
        store.start()
    second = orthonormal(info, own, other, held)
    next_left(info, right_factor(scale, second, held, high, low), high, low, out)
    for store in stores:
        store.wait()


def load_parts(high_in, low_in, high, low, sems):
    loads = [
        pltpu.make_async_copy(high_in, high, sems.at[0]),
        pltpu.make_async_copy(low_in, low, sems.at[1]),
    ]
    for load in loads:
        load.start()
    return loads


def step_kernel(scale, info, own, other, high_in, low_in, out, held, high, low, sems):
    loads = load_parts(high_in, low_in, high, low, sems)
    second = orthonormal(info, own, other, held)
    for load in loads:
        load.wait()
    next_left(info, right_factor(scale, second, held, high, low), high, low, out)


def last_kernel(scale, info, own, other, high_in, low_in, out, basis, held, high, low, sems):
    loads = load_parts(high_in, low_in, high, low, sems)
    length, rank, rows = own.shape
    second = orthonormal(info, own, other, held)
    for load in loads:
        load.wait()
    q = right_factor(scale, second, held, high, low)
    half = rank // 2
    quarter = half // 2
    rest = jnp.concatenate([q[:, 2 * LANES :], jnp.zeros_like(q[:, 2 * LANES :])], axis=1)
    for core in range(2):
        span = slice(core * half, (core + 1) * half)
        out[core, :half] = q[span, :LANES]
        out[core, half : 2 * half] = q[span, LANES : 2 * LANES]
        tail = rest[span]
        out[core, 2 * half :] = tail[:quarter] + pltpu.roll(tail[quarter:], LANES // 2, 1)
    at = pl.multiple_of((2 * info[0] + info[1]) * rows, rows)
    y = dot(weights(second), held[:, pl.ds(at, rows)], NN)
    basis[...] = y[:rank] + (y[rank : 2 * rank] + y[2 * rank :])


def scratch(length, rank, cut):
    n = 2 * length * LANES
    return [pltpu.VMEM((4 * rank, n), BF16)], [pltpu.VMEM((cut, n), BF16)] * 2


def first(scale, info, own, other, total, total_other):
    length, rank, rows = own.shape
    cut = total.shape[2]
    held, both = scratch(length, rank, cut)
    whole = jax.ShapeDtypeStruct((cut, 2 * length * rows), BF16)
    return pl.pallas_call(
        functools.partial(first_kernel, scale),
        in_specs=[SMEM_SPEC] + [VMEM_SPEC] * 4,
        out_specs=[VMEM_SPEC, HBM_SPEC, HBM_SPEC],
        out_shape=[jax.ShapeDtypeStruct(own.shape, F32), whole, whole],
        scratch_shapes=held + both + [pltpu.SemaphoreType.DMA((2,))],
        compiler_params=params(),
        name="first",
    )(info, own, other, total, total_other)


def step(scale, info, own, other, high, low):
    length, rank, rows = own.shape
    held, both = scratch(length, rank, high.shape[0])
    return pl.pallas_call(
        functools.partial(step_kernel, scale),
        in_specs=[SMEM_SPEC, VMEM_SPEC, VMEM_SPEC, HBM_SPEC, HBM_SPEC],
        out_shape=jax.ShapeDtypeStruct(own.shape, F32),
        scratch_shapes=held + both + [pltpu.SemaphoreType.DMA((2,))],
        compiler_params=params(),
        name="step",
    )(info, own, other, high, low)


def last(scale, info, own, other, high, low):
    length, rank, rows = own.shape
    held, both = scratch(length, rank, high.shape[0])
    shapes = [(2, 5 * rank // 4, LANES), (rank, rows)]
    return pl.pallas_call(
        functools.partial(last_kernel, scale),
        in_specs=[SMEM_SPEC, VMEM_SPEC, VMEM_SPEC, HBM_SPEC, HBM_SPEC],
        out_shape=[jax.ShapeDtypeStruct(x, F32) for x in shapes],
        scratch_shapes=held + both + [pltpu.SemaphoreType.DMA((2,))],
        compiler_params=params(),
        name="last",
    )(info, own, other, high, low)


def columns_of(top, low):
    half = top.shape[0] * 2 // 5
    quarter = half // 2
    lane = lax.broadcasted_iota(jnp.int32, (quarter, LANES), 1)
    blocks = []
    for x in (top, low):
        tail = x[2 * half :]
        upper = jnp.where(lane < LANES // 2, tail, 0.0)
        lower = jnp.where(lane < LANES // 2, pltpu.roll(tail, LANES // 2, 1), 0.0)
        blocks.append((x[:half], x[half : 2 * half], jnp.concatenate([upper, lower], axis=0)))
    return [jnp.concatenate([a, b], axis=0) for a, b in zip(*blocks)]


def finish_kernel(flag, grads, errors, own, other, basis, new_errors, factor_q):
    first_core = flag[0] == 0
    turned = basis[...].T
    b_high, b_low = split2(turned)
    left = jnp.concatenate([b_high, b_high, b_low], axis=1)
    wide = 5 * LANES
    lane = lax.broadcasted_iota(jnp.int32, (basis.shape[0], LANES), 1)
    for i in range(own.shape[0] // 2):
        even, odd = [
            columns_of(jnp.where(first_core, own[j], other[j]), jnp.where(first_core, other[j], own[j]))
            for j in (2 * i, 2 * i + 1)
        ]
        turn = [pltpu.roll(x, LANES // 2, 1) for x in odd]
        low_lane = lane < LANES // 2
        q = jnp.concatenate(
            [
                even[0],
                even[1],
                jnp.where(low_lane, even[2], turn[0]),
                jnp.where(low_lane, turn[0], turn[1]),
                jnp.where(low_lane, turn[1], turn[2]),
            ],
            axis=1,
        )
        span = slice(i * wide, (i + 1) * wide)
        factor_q[:, span] = q
        q_high, q_low = split2(q)
        product = dot(left, jnp.concatenate([q_high, q_low, q_high], axis=0), NN)
        merged = grads[:, span].astype(F32) + errors[:, span].astype(F32)
        new_errors[:, span] = (merged - product).astype(BF16)


def finish(flag, grads, errors, own, other, basis):
    rows, width = grads.shape
    reps, tall, lanes = own.shape
    rank = basis.shape[0]
    steps = 4
    cols = pl.BlockSpec((rows, width // steps), lambda i: (0, i))
    piece = pl.BlockSpec((reps // steps, tall, lanes), lambda i: (i, 0, 0))
    return pl.pallas_call(
        finish_kernel,
        grid=(steps,),
        in_specs=[SMEM_SPEC, cols, cols, piece, piece, pl.BlockSpec((rank, rows), lambda i: (0, 0))],
        out_specs=[cols, pl.BlockSpec((rank, width // steps), lambda i: (0, i))],
        out_shape=[jax.ShapeDtypeStruct((rows, width), BF16), jax.ShapeDtypeStruct((rank, width), F32)],
        compiler_params=params(),
        name="finish",
    )(flag, grads, errors, own, other, basis)


def exchange(chunks, axis):
    return lax.all_to_all(chunks, axis, 0, 0)


def gather(block, axis, count):
    return exchange(jnp.broadcast_to(block[None], (count,) + block.shape), axis)


def swap_cores(block):
    return lax.ppermute(block, "core", [(0, 1), (1, 0)])


def ring(block, length):
    half = length // 2
    up = [(2 * i, 2 * ((i + 1) % length)) for i in range(length)]
    down = [(2 * i + 1, 2 * ((i - 1) % length) + 1) for i in range(length)]
    blocks = [block]
    for s in range(half):
        blocks.append(lax.ppermute(blocks[-1], ("z", "core"), up + down if s < half - 1 else down))
    return blocks


def body(grads, errors, q_start):
    grads, errors = grads[0], errors[0]
    rows, width = grads.shape
    rank = q_start.shape[0]
    reps, length = lax.axis_size("rep"), lax.axis_size("z")
    core, place = lax.axis_index("core"), lax.axis_index("z")
    cut, extra = width // reps, rank // reps
    scale = 1.0 / reps
    flag = core.reshape(1).astype(jnp.int32)
    info = jnp.stack([place, core]).astype(jnp.int32)

    block = jnp.sum(exchange(start(grads, errors, q_start, reps), "rep"), axis=0)
    streams = ring(block, length), ring(swap_cores(block), length)
    held = jnp.stack(
        [jnp.stack([jnp.where(core == 0, x[j], x[j + 1]) for x in streams]) for j in range(length // 2)]
    )
    total = held[:, :, :cut]
    piece = held[:, :, cut : cut + extra]
    piece = jnp.where(core == 0, piece, piece[:, ::-1]).reshape(length * extra, rows)
    own = gather(piece, "rep", reps).reshape(reps, length, extra, rows)
    own = own.transpose(1, 0, 2, 3).reshape(length, rank, rows)
    partial, high, low = first(scale, info, own, swap_cores(own), total, swap_cores(total))
    for turn in range(ITERS - 1):
        own = gather(jnp.sum(exchange(partial, "rep"), axis=0), "rep", reps)
        if turn < ITERS - 2:
            partial = step(scale, info, own, swap_cores(own), high, low)
    part_q, basis = last(scale, info, own, swap_cores(own), high, low)
    own_q = gather(lax.dynamic_index_in_dim(part_q, core, 0, False), "rep", reps)
    new_errors, factor_q = finish(flag, grads, errors, own_q, swap_cores(own_q), basis)
    return new_errors[None], factor_q


def solution(mesh):
    reps, count = mesh.devices.shape
    split = Mesh(mesh.devices.reshape(reps, count // 2, 2), ("rep", "z", "core"))
    placed = P("rep", ("z", "core"), None)
    return jax.shard_map(
        body, mesh=split, in_specs=(placed, placed, P()), out_specs=(placed, P()), check_vma=False
    )
```

time: 357 us -> 276 us (0.77)
  waiting for transfers between devices: 90.6 us -> 9.6 us
  starting transfers between devices: 33.9 us -> 91.1 us
  Pallas kernels: 80.9 us -> 44.9 us
  between operations: 14.1 us -> 1.15 us
  blocking collectives: 128 us -> 120 us
    all_gather x1 -> x0, waiting for transfers between devices: 70.9 us -> none  [body(): own_total = lax.all_gather(block[:cut], 'z')]
    ppermute x0 -> x16, starting transfers between devices: none -> 65 us  [ring(): lax.ppermute(blocks[-1], ('z', 'core'), up + down if s < half - 1 else down)]
    pallas_call x6 -> x5, Pallas kernels: 80.9 us -> 44.9 us  [the longest x1 12.4 us: last(): pl.pallas_call(functools.partial(last_kernel, scale), in_specs=[SMEM_SPEC...]
    all_to_all x1 -> x0, waiting for transfers between devices: 15 us -> none  [exchange(): return lax.all_to_all(chunks, axis, 0, 0)]
    all_to_all x7, blocking collectives: 128 us -> 120 us  [exchange(): return lax.all_to_all(chunks, axis, 0, 0)]
    all_to_all x1 -> x0, starting transfers between devices: 6.53 us -> none  [exchange(): return lax.all_to_all(chunks, axis, 0, 0)]
    unnamed x12 -> x14, local copies, waits for them, and re-layouts: 2.51 us -> 6.73 us
    ppermute x4 -> x6, starting transfers between devices: 27.3 us -> 26.1 us  [swap_cores(): return lax.ppermute(block, 'core', [(0, 1), (1, 0)])]
  transfers between devices with their start and end apart: 6 -> 22, of which waited for: 5 -> 5; matrix products, arithmetic and copies ran while one was open for 1% -> 0% of each run, Pallas kernels for 0% -> 0%
where the time goes in v2:
time: 276 us; the launch traced here: 275 us
  blocking collectives  120 us (43%)
  starting transfers between devices  91.1 us (33%)
  Pallas kernels  44.9 us (16%)
  waiting for transfers between devices  9.6 us (3%)
  local copies, waits for them, and re-layouts  7.7 us (3%)
    all_to_all x7, blocking collectives, exchange(): return lax.all_to_all(chunks, axis, 0, 0)  120 us
    ppermute x16, starting transfers between devices, ring(): lax.ppermute(blocks[-1], ('z', 'core'), up + down if s < half - 1 else down)  65 us
    ppermute x6, starting transfers between devices, swap_cores(): return lax.ppermute(block, 'core', [(0, 1), (1, 0)])  26.1 us
    pallas_call x1, Pallas kernels, last(): pl.pallas_call(functools.partial(last_kernel, scale), in_specs=[SMEM_SPEC...  12.4 us
    pallas_call x1, Pallas kernels, step(): pl.pallas_call(functools.partial(step_kernel, scale), in_specs=[SMEM_SPEC...  12.3 us
    pallas_call x1, Pallas kernels, first(): pl.pallas_call(functools.partial(first_kernel, scale), in_specs=[SMEM_SPE...  12.2 us
    unnamed x14, local copies, waits for them, and re-layouts  6.73 us
    ppermute x6, waiting for transfers between devices, swap_cores(): return lax.ppermute(block, 'core', [(0, 1), (1, 0)])  6.21 us
  transfers between devices with their start and end apart: 22, of which 5 were waited for; matrix products, arithmetic and copies ran while one was open for 0% of the time, Pallas kernels for 0%

profile of v2, /device:TPU:1, one launch (start us, length us, event | category | flops | bytes accessed | tf_op | source)
XLA Modules:
  0.0 274.7 jit_solution(9062802715001554177)
XLA Ops:
  0.6 5.0 %start.1 = f32[16,328,128]{2,1,0:T(8,128)} custom-call(bf16[128,5120]{1,0:T(8,128)(2,1)} %bitcast.76, bf16[128,5120]{1,0:T(8,128)(2,1)} %bitcast.78, f32[64,5120]{1,0:T(8,128)} %q_start.1), custom_call_target="tpu_custom_call" | custom-call | tf_op jit(solution)/shard_map/start/pallas_call | solution.py:76
  5.6 39.2 %all_to_all.35 = f32[16,328,128]{2,1,0:T(8,128)S(1)} all-to-all(f32[16,328,128]{2,1,0:T(8,128)} %start.1), channel_id=1, replica_groups=mesh['rep'=16,'z'=16,'core'=2] {'rep'}, dimensions={0} | all-to-all | bytes 5373952 | tf_op jit(solution)/shard_map/all_to_all | solution.py:399
  44.9 6.0 %collective-permute-start.1 = (f32[328,128]{1,0:T(8,128)S(1)}, f32[328,128]{1,0:T(8,128)S(1)}, u32[]{:S(2)}, u32[]{:S(2)}) collective-permute-start(f32[328,128]{1,0:T(8,128)S(1)} %reduce_sum.27), channel_id=1, source_target_pairs={{0,1},{1,0},{2,3},{3,2},{4,5},{5,4},{6,7},{7,6},{8,9},{9,8},{10,11... | collective-permute-start | bytes 503816 | tf_op jit(solution)/shard_map/ppermute | solution.py:407
  50.9 11.5 %collective-permute-start = (f32[328,128]{1,0:T(8,128)S(1)}, f32[328,128]{1,0:T(8,128)S(1)}, u32[]{:S(2)}, u32[]{:S(2)}) collective-permute-start(f32[328,128]{1,0:T(8,128)S(1)} %reduce_sum.27), channel_id=1, source_target_pairs={{0,2},{2,4},{4,6},{6,8},{8,10},{10,12},{12,14},{14,16},{16,18},{18... | collective-permute-start | bytes 503816 | tf_op jit(solution)/shard_map/ppermute | solution.py:416
  62.4 2.6 collective-permute-start.2
  65.1 4.6 %collective-permute-start.3 = (f32[328,128]{1,0:T(8,128)S(1)}, f32[328,128]{1,0:T(8,128)S(1)}, u32[]{:S(2)}, u32[]{:S(2)}) collective-permute-start(f32[328,128]{1,0:T(8,128)S(1)} %collective-permute-done), channel_id=1, source_target_pairs={{0,2},{2,4},{4,6},{6,8},{8,10},{10,12},{12,14},{14,16},{16,18},{18... | collective-permute-start | bytes 503816 | tf_op jit(solution)/shard_map/ppermute | solution.py:416
  69.7 2.6 collective-permute-start.4
  72.4 4.6 %collective-permute-start.5 = (f32[328,128]{1,0:T(8,128)S(1)}, f32[328,128]{1,0:T(8,128)S(1)}, u32[]{:S(2)}, u32[]{:S(2)}) collective-permute-start(f32[328,128]{1,0:T(8,128)S(1)} %collective-permute-done.3), channel_id=1, source_target_pairs={{0,2},{2,4},{4,6},{6,8},{8,10},{10,12},{12,14},{14,16},{16,18},{18... | collective-permute-start | bytes 503816 | tf_op jit(solution)/shard_map/ppermute | solution.py:416
  77.0 2.6 collective-permute-start.6
  79.7 4.6 %collective-permute-start.7 = (f32[328,128]{1,0:T(8,128)S(1)}, f32[328,128]{1,0:T(8,128)S(1)}, u32[]{:S(2)}, u32[]{:S(2)}) collective-permute-start(f32[328,128]{1,0:T(8,128)S(1)} %collective-permute-done.5), channel_id=1, source_target_pairs={{0,2},{2,4},{4,6},{6,8},{8,10},{10,12},{12,14},{14,16},{16,18},{18... | collective-permute-start | bytes 503816 | tf_op jit(solution)/shard_map/ppermute | solution.py:416
  84.3 2.6 collective-permute-start.8
  87.0 4.6 %collective-permute-start.9 = (f32[328,128]{1,0:T(8,128)S(1)}, f32[328,128]{1,0:T(8,128)S(1)}, u32[]{:S(2)}, u32[]{:S(2)}) collective-permute-start(f32[328,128]{1,0:T(8,128)S(1)} %collective-permute-done.7), channel_id=1, source_target_pairs={{0,2},{2,4},{4,6},{6,8},{8,10},{10,12},{12,14},{14,16},{16,18},{18... | collective-permute-start | bytes 503816 | tf_op jit(solution)/shard_map/ppermute | solution.py:416
  91.7 2.6 collective-permute-start.10
  94.3 4.6 %collective-permute-start.11 = (f32[328,128]{1,0:T(8,128)S(1)}, f32[328,128]{1,0:T(8,128)S(1)}, u32[]{:S(2)}, u32[]{:S(2)}) collective-permute-start(f32[328,128]{1,0:T(8,128)S(1)} %collective-permute-done.9), channel_id=1, source_target_pairs={{0,2},{2,4},{4,6},{6,8},{8,10},{10,12},{12,14},{14,16},{16,18},{18... | collective-permute-start | bytes 503816 | tf_op jit(solution)/shard_map/ppermute | solution.py:416
  101.6 4.6 %collective-permute-start.13 = (f32[328,128]{1,0:T(8,128)S(1)}, f32[328,128]{1,0:T(8,128)S(1)}, u32[]{:S(2)}, u32[]{:S(2)}) collective-permute-start(f32[328,128]{1,0:T(8,128)S(1)} %collective-permute-done.11), channel_id=1, source_target_pairs={{0,2},{2,4},{4,6},{6,8},{8,10},{10,12},{12,14},{14,16},{16,18},{18... | collective-permute-start | bytes 503816 | tf_op jit(solution)/shard_map/ppermute | solution.py:416
  106.3 2.6 collective-permute-start.14
  108.9 4.6 %collective-permute-start.15 = (f32[328,128]{1,0:T(8,128)S(1)}, f32[328,128]{1,0:T(8,128)S(1)}, u32[]{:S(2)}, u32[]{:S(2)}) collective-permute-start(f32[328,128]{1,0:T(8,128)S(1)} %collective-permute-done.13), channel_id=1, source_target_pairs={{1,31},{3,1},{5,3},{7,5},{9,7},{11,9},{13,11},{15,13},{17,15},{19,... | collective-permute-start | bytes 503816 | tf_op jit(solution)/shard_map/ppermute | solution.py:416
  116.3 3.3 %collective-permute-done.16 = f32[328,128]{1,0:T(8,128)S(1)} collective-permute-done((f32[328,128]{1,0:T(8,128)S(1)}, f32[328,128]{1,0:T(8,128)S(1)}, u32[]{:S(2)}, u32[]{:S(2)}) %collective-permute-start.16) | collective-permute-done | bytes 167968 | tf_op jit(solution)/shard_map/ppermute | solution.py:416
  122.4 13.3 %all_to_all.36 = f32[16,64,128]{2,1,0:T(8,128)S(1)} all-to-all(f32[16,64,128]{2,1,0:T(8,128)S(1)} %broadcast_in_dim.15), channel_id=1, replica_groups=mesh['rep'=16,'z'=16,'core'=2] {'rep'}, dimensions={0} | all-to-all | bytes 1048576 | tf_op jit(solution)/shard_map/all_to_all | solution.py:399
  136.2 4.0 %collective-permute-start.17 = (f32[16,64,128]{2,1,0:T(8,128)S(1)}, f32[16,64,128]{2,1,0:T(8,128)}, u32[]{:S(2)}, u32[]{:S(2)}) collective-permute-start(f32[16,64,128]{2,1,0:T(8,128)S(1)} %bitcast.80), channel_id=1, source_target_pairs={{0,1},{1,0},{2,3},{3,2},{4,5},{5,4},{6,7},{7,6},{8,9},{9,8},{10,11... | collective-permute-start | bytes 1572872 | tf_op jit(solution)/shard_map/ppermute | solution.py:407
  143.6 12.2 %first.1 = (f32[16,64,128]{2,1,0:T(8,128)S(1)}, bf16[320,4096]{1,0:T(8,128)(2,1)S(1)}, bf16[320,4096]{1,0:T(8,128)(2,1)S(1)}) custom-call(s32[2]{0:T(128)S(1)} %pad_add_fusion.info, f32[16,64,128]{2,1,0:T(8,128)S(1)} %bitcast.81, f32[16,64,128]{2,1,0:T(8,128)} %collective-permute-done.17.other, f32[8,2,320,128]{3,2,1,0:T(8,128)S(1)} %copy-done.4, ...), custom_call_target="tpu_custom_call" | custom-call | tf_op jit(solution)/shard_map/first/pallas_call | solution.py:297
  157.3 13.3 %all_to_all.37 = f32[16,64,128]{2,1,0:T(8,128)S(1)} all-to-all(f32[16,64,128]{2,1,0:T(8,128)S(1)} %get-tuple-element.9), channel_id=1, replica_groups=mesh['rep'=16,'z'=16,'core'=2] {'rep'}, dimensions={0} | all-to-all | bytes 1048576 | tf_op jit(solution)/shard_map/all_to_all | solution.py:399
  170.7 12.7 %all_to_all.38.own = f32[16,64,128]{2,1,0:T(8,128)S(1)} all-to-all(f32[16,64,128]{2,1,0:T(8,128)S(1)} %broadcast_in_dim.32), channel_id=1, replica_groups=mesh['rep'=16,'z'=16,'core'=2] {'rep'}, dimensions={0} | all-to-all | bytes 1048576 | tf_op jit(solution)/shard_map/all_to_all | solution.py:399
  183.5 5.2 %collective-permute-start.19 = (f32[16,64,128]{2,1,0:T(8,128)S(1)}, f32[16,64,128]{2,1,0:T(8,128)S(1)}, u32[]{:S(2)}, u32[]{:S(2)}) collective-permute-start(f32[16,64,128]{2,1,0:T(8,128)S(1)} %all_to_all.38.own), channel_id=1, source_target_pairs={{0,1},{1,0},{2,3},{3,2},{4,5},{5,4},{6,7},{7,6},{8,9},{9,8},{10,11... | collective-permute-start | bytes 1572872 | tf_op jit(solution)/shard_map/ppermute | solution.py:407
  191.9 12.3 %step.1 = f32[16,64,128]{2,1,0:T(8,128)S(1)} custom-call(s32[2]{0:T(128)S(1)} %pad_add_fusion.info, f32[16,64,128]{2,1,0:T(8,128)S(1)} %all_to_all.38.own, f32[16,64,128]{2,1,0:T(8,128)S(1)} %collective-permute-done.19.other, bf16[320,4096]{1,0:T(8,128)(2,1)S(1)} %get-tuple-element.10.high_in, bf16[320,4096]{1,0:T(8,128)(2,1)S(1)} %copy-done.1), custom_call_target="tpu_custom_call" | custom-call | tf_op jit(solution)/shard_map/step/pallas_call | solution.py:311
  204.2 13.3 %all_to_all.39 = f32[16,64,128]{2,1,0:T(8,128)S(1)} all-to-all(f32[16,64,128]{2,1,0:T(8,128)S(1)} %step.1), channel_id=1, replica_groups=mesh['rep'=16,'z'=16,'core'=2] {'rep'}, dimensions={0} | all-to-all | bytes 1048576 | tf_op jit(solution)/shard_map/all_to_all | solution.py:399
  217.6 12.7 %all_to_all.40.own = f32[16,64,128]{2,1,0:T(8,128)S(1)} all-to-all(f32[16,64,128]{2,1,0:T(8,128)S(1)} %broadcast_in_dim.33), channel_id=1, replica_groups=mesh['rep'=16,'z'=16,'core'=2] {'rep'}, dimensions={0} | all-to-all | bytes 1048576 | tf_op jit(solution)/shard_map/all_to_all | solution.py:399
  230.4 5.4 %collective-permute-start.20 = (f32[16,64,128]{2,1,0:T(8,128)S(1)}, f32[16,64,128]{2,1,0:T(8,128)}, u32[]{:S(2)}, u32[]{:S(2)}) collective-permute-start(f32[16,64,128]{2,1,0:T(8,128)S(1)} %all_to_all.40.own), channel_id=1, source_target_pairs={{0,1},{1,0},{2,3},{3,2},{4,5},{5,4},{6,7},{7,6},{8,9},{9,8},{10,11... | collective-permute-start | bytes 1572872 | tf_op jit(solution)/shard_map/ppermute | solution.py:407
  238.9 12.4 %last.1 = (f32[2,80,128]{2,1,0:T(8,128)S(1)}, f32[64,128]{1,0:T(8,128)S(1)}) custom-call(s32[2]{0:T(128)S(1)} %pad_add_fusion.info, f32[16,64,128]{2,1,0:T(8,128)S(1)} %all_to_all.40.own, f32[16,64,128]{2,1,0:T(8,128)} %collective-permute-done.20.other, bf16[320,4096]{1,0:T(8,128)(2,1)S(1)} %get-tuple-element.10.high_in, bf16[320,4096]{1,0:T(8,128)(2,1)S(1)} %copy-done.2), custom_call_target="tpu_custom_call" | custom-call | tf_op jit(solution)/shard_map/last/pallas_call | solution.py:325
  251.4 14.9 %all_to_all.41.own = f32[16,80,128]{2,1,0:T(8,128)S(1)} all-to-all(f32[16,80,128]{2,1,0:T(8,128)S(1)} %broadcast_in_dim.35), channel_id=1, replica_groups=mesh['rep'=16,'z'=16,'core'=2] {'rep'}, dimensions={0} | all-to-all | bytes 1310720 | tf_op jit(solution)/shard_map/all_to_all | solution.py:399
  266.3 3.6 %collective-permute-start.21 = (f32[16,80,128]{2,1,0:T(8,128)S(1)}, f32[16,80,128]{2,1,0:T(8,128)S(1)}, u32[]{:S(2)}, u32[]{:S(2)}) collective-permute-start(f32[16,80,128]{2,1,0:T(8,128)S(1)} %all_to_all.41.own), channel_id=1, source_target_pairs={{0,1},{1,0},{2,3},{3,2},{4,5},{5,4},{6,7},{7,6},{8,9},{9,8},{10,11... | collective-permute-start | bytes 1966088 | tf_op jit(solution)/shard_map/ppermute | solution.py:407
  271.6 3.0 %finish.1 = (bf16[128,5120]{1,0:T(8,128)(2,1)}, f32[64,5120]{1,0:T(8,128)}) custom-call(s32[1]{0:T(128)} %bitcast.flag, bf16[128,5120]{1,0:T(8,128)(2,1)S(1)} %bitcast.77, bf16[128,5120]{1,0:T(8,128)(2,1)S(1)} %bitcast.79, f32[16,80,128]{2,1,0:T(8,128)S(1)} %all_to_all.41.own, f32[16,80,128]{2,1,0:T(8,128)S(1)} %collective-permute-done.21.other, ...), custom_call_target="tpu_custom_call" | custom-call | tf_op jit(solution)/shard_map/finish/pallas_call | solution.py:387
  (62 shorter events, 21.9 us)
Async XLA Ops:
  44.9 17.5 %collective-permute-start.1 = (f32[328,128]{1,0:T(8,128)S(1)}, f32[328,128]{1,0:T(8,128)S(1)}, u32[]{:S(2)}, u32[]{:S(2)}) collective-permute-start(f32[328,128]{1,0:T(8,128)S(1)} %reduce_sum.27), channel_id=1, source_target_pairs={{0,1},{1,0},{2,3},{3,2},{4,5},{5,4},{6,7},{7,6},{8,9},{9,8},{10,11... | collective-permute-start | bytes 503816 | tf_op jit(solution)/shard_map/ppermute | solution.py:407
  50.9 14.1 %collective-permute-start = (f32[328,128]{1,0:T(8,128)S(1)}, f32[328,128]{1,0:T(8,128)S(1)}, u32[]{:S(2)}, u32[]{:S(2)}) collective-permute-start(f32[328,128]{1,0:T(8,128)S(1)} %reduce_sum.27), channel_id=1, source_target_pairs={{0,2},{2,4},{4,6},{6,8},{8,10},{10,12},{12,14},{14,16},{16,18},{18... | collective-permute-start | bytes 503816 | tf_op jit(solution)/shard_map/ppermute | solution.py:416
  62.4 7.3 %collective-permute-start.2 = (f32[328,128]{1,0:T(8,128)S(1)}, f32[328,128]{1,0:T(8,128)S(1)}, u32[]{:S(2)}, u32[]{:S(2)}) collective-permute-start(f32[328,128]{1,0:T(8,128)S(1)} %collective-permute-done.1), channel_id=1, source_target_pairs={{0,2},{2,4},{4,6},{6,8},{8,10},{10,12},{12,14},{14,16},{16,18},{18... | collective-permute-start | bytes 503816 | tf_op jit(solution)/shard_map/ppermute | solution.py:416
  65.1 7.3 %collective-permute-start.3 = (f32[328,128]{1,0:T(8,128)S(1)}, f32[328,128]{1,0:T(8,128)S(1)}, u32[]{:S(2)}, u32[]{:S(2)}) collective-permute-start(f32[328,128]{1,0:T(8,128)S(1)} %collective-permute-done), channel_id=1, source_target_pairs={{0,2},{2,4},{4,6},{6,8},{8,10},{10,12},{12,14},{14,16},{16,18},{18... | collective-permute-start | bytes 503816 | tf_op jit(solution)/shard_map/ppermute | solution.py:416
  69.7 7.3 %collective-permute-start.4 = (f32[328,128]{1,0:T(8,128)S(1)}, f32[328,128]{1,0:T(8,128)S(1)}, u32[]{:S(2)}, u32[]{:S(2)}) collective-permute-start(f32[328,128]{1,0:T(8,128)S(1)} %collective-permute-done.2), channel_id=1, source_target_pairs={{0,2},{2,4},{4,6},{6,8},{8,10},{10,12},{12,14},{14,16},{16,18},{18... | collective-permute-start | bytes 503816 | tf_op jit(solution)/shard_map/ppermute | solution.py:416
  72.4 7.3 %collective-permute-start.5 = (f32[328,128]{1,0:T(8,128)S(1)}, f32[328,128]{1,0:T(8,128)S(1)}, u32[]{:S(2)}, u32[]{:S(2)}) collective-permute-start(f32[328,128]{1,0:T(8,128)S(1)} %collective-permute-done.3), channel_id=1, source_target_pairs={{0,2},{2,4},{4,6},{6,8},{8,10},{10,12},{12,14},{14,16},{16,18},{18... | collective-permute-start | bytes 503816 | tf_op jit(solution)/shard_map/ppermute | solution.py:416
  77.0 7.3 %collective-permute-start.6 = (f32[328,128]{1,0:T(8,128)S(1)}, f32[328,128]{1,0:T(8,128)S(1)}, u32[]{:S(2)}, u32[]{:S(2)}) collective-permute-start(f32[328,128]{1,0:T(8,128)S(1)} %collective-permute-done.4), channel_id=1, source_target_pairs={{0,2},{2,4},{4,6},{6,8},{8,10},{10,12},{12,14},{14,16},{16,18},{18... | collective-permute-start | bytes 503816 | tf_op jit(solution)/shard_map/ppermute | solution.py:416
  79.7 7.3 %collective-permute-start.7 = (f32[328,128]{1,0:T(8,128)S(1)}, f32[328,128]{1,0:T(8,128)S(1)}, u32[]{:S(2)}, u32[]{:S(2)}) collective-permute-start(f32[328,128]{1,0:T(8,128)S(1)} %collective-permute-done.5), channel_id=1, source_target_pairs={{0,2},{2,4},{4,6},{6,8},{8,10},{10,12},{12,14},{14,16},{16,18},{18... | collective-permute-start | bytes 503816 | tf_op jit(solution)/shard_map/ppermute | solution.py:416
  84.3 7.3 %collective-permute-start.8 = (f32[328,128]{1,0:T(8,128)S(1)}, f32[328,128]{1,0:T(8,128)S(1)}, u32[]{:S(2)}, u32[]{:S(2)}) collective-permute-start(f32[328,128]{1,0:T(8,128)S(1)} %collective-permute-done.6), channel_id=1, source_target_pairs={{0,2},{2,4},{4,6},{6,8},{8,10},{10,12},{12,14},{14,16},{16,18},{18... | collective-permute-start | bytes 503816 | tf_op jit(solution)/shard_map/ppermute | solution.py:416
  87.0 7.3 %collective-permute-start.9 = (f32[328,128]{1,0:T(8,128)S(1)}, f32[328,128]{1,0:T(8,128)S(1)}, u32[]{:S(2)}, u32[]{:S(2)}) collective-permute-start(f32[328,128]{1,0:T(8,128)S(1)} %collective-permute-done.7), channel_id=1, source_target_pairs={{0,2},{2,4},{4,6},{6,8},{8,10},{10,12},{12,14},{14,16},{16,18},{18... | collective-permute-start | bytes 503816 | tf_op jit(solution)/shard_map/ppermute | solution.py:416
  91.7 7.3 %collective-permute-start.10 = (f32[328,128]{1,0:T(8,128)S(1)}, f32[328,128]{1,0:T(8,128)S(1)}, u32[]{:S(2)}, u32[]{:S(2)}) collective-permute-start(f32[328,128]{1,0:T(8,128)S(1)} %collective-permute-done.8), channel_id=1, source_target_pairs={{0,2},{2,4},{4,6},{6,8},{8,10},{10,12},{12,14},{14,16},{16,18},{18... | collective-permute-start | bytes 503816 | tf_op jit(solution)/shard_map/ppermute | solution.py:416
  94.3 7.3 %collective-permute-start.11 = (f32[328,128]{1,0:T(8,128)S(1)}, f32[328,128]{1,0:T(8,128)S(1)}, u32[]{:S(2)}, u32[]{:S(2)}) collective-permute-start(f32[328,128]{1,0:T(8,128)S(1)} %collective-permute-done.9), channel_id=1, source_target_pairs={{0,2},{2,4},{4,6},{6,8},{8,10},{10,12},{12,14},{14,16},{16,18},{18... | collective-permute-start | bytes 503816 | tf_op jit(solution)/shard_map/ppermute | solution.py:416
  99.0 7.3 %collective-permute-start.12 = (f32[328,128]{1,0:T(8,128)S(1)}, f32[328,128]{1,0:T(8,128)S(1)}, u32[]{:S(2)}, u32[]{:S(2)}) collective-permute-start(f32[328,128]{1,0:T(8,128)S(1)} %collective-permute-done.10), channel_id=1, source_target_pairs={{0,2},{2,4},{4,6},{6,8},{8,10},{10,12},{12,14},{14,16},{16,18},{18... | collective-permute-start | bytes 503816 | tf_op jit(solution)/shard_map/ppermute | solution.py:416
  101.6 7.3 %collective-permute-start.13 = (f32[328,128]{1,0:T(8,128)S(1)}, f32[328,128]{1,0:T(8,128)S(1)}, u32[]{:S(2)}, u32[]{:S(2)}) collective-permute-start(f32[328,128]{1,0:T(8,128)S(1)} %collective-permute-done.11), channel_id=1, source_target_pairs={{0,2},{2,4},{4,6},{6,8},{8,10},{10,12},{12,14},{14,16},{16,18},{18... | collective-permute-start | bytes 503816 | tf_op jit(solution)/shard_map/ppermute | solution.py:416
  106.3 7.3 %collective-permute-start.14 = (f32[328,128]{1,0:T(8,128)S(1)}, f32[328,128]{1,0:T(8,128)S(1)}, u32[]{:S(2)}, u32[]{:S(2)}) collective-permute-start(f32[328,128]{1,0:T(8,128)S(1)} %collective-permute-done.12), channel_id=1, source_target_pairs={{0,2},{2,4},{4,6},{6,8},{8,10},{10,12},{12,14},{14,16},{16,18},{18... | collective-permute-start | bytes 503816 | tf_op jit(solution)/shard_map/ppermute | solution.py:416
  108.9 7.3 %collective-permute-start.15 = (f32[328,128]{1,0:T(8,128)S(1)}, f32[328,128]{1,0:T(8,128)S(1)}, u32[]{:S(2)}, u32[]{:S(2)}) collective-permute-start(f32[328,128]{1,0:T(8,128)S(1)} %collective-permute-done.13), channel_id=1, source_target_pairs={{1,31},{3,1},{5,3},{7,5},{9,7},{11,9},{13,11},{15,13},{17,15},{19,... | collective-permute-start | bytes 503816 | tf_op jit(solution)/shard_map/ppermute | solution.py:416
  113.6 6.1 %collective-permute-start.16 = (f32[328,128]{1,0:T(8,128)S(1)}, f32[328,128]{1,0:T(8,128)S(1)}, u32[]{:S(2)}, u32[]{:S(2)}) collective-permute-start(f32[328,128]{1,0:T(8,128)S(1)} %collective-permute-done.14), channel_id=1, source_target_pairs={{1,31},{3,1},{5,3},{7,5},{9,7},{11,9},{13,11},{15,13},{17,15},{19,... | collective-permute-start | bytes 503816 | tf_op jit(solution)/shard_map/ppermute | solution.py:416
  120.3 21.5 %copy-start.3 = (f32[8,2,320,128]{3,2,1,0:T(8,128)}, f32[8,2,320,128]{3,2,1,0:T(8,128)S(1)}, u32[]{:S(2)}) copy-start(f32[8,2,320,128]{3,2,1,0:T(8,128)S(1)} %slice.9.total) | copy-start | bytes 7864324
  120.3 21.5 %collective-permute-start.18 = (f32[8,2,320,128]{3,2,1,0:T(8,128)S(1)}, f32[8,2,320,128]{3,2,1,0:T(8,128)}, u32[]{:S(2)}, u32[]{:S(2)}) collective-permute-start(f32[8,2,320,128]{3,2,1,0:T(8,128)S(1)} %slice.9.total), channel_id=1, source_target_pairs={{0,1},{1,0},{2,3},{3,2},{4,5},{5,4},{6,7},{7,6},{8,9},{9,8},{10,11... | collective-permute-start | bytes 7864328 | tf_op jit(solution)/shard_map/ppermute | solution.py:407
  136.2 5.7 %collective-permute-start.17 = (f32[16,64,128]{2,1,0:T(8,128)S(1)}, f32[16,64,128]{2,1,0:T(8,128)}, u32[]{:S(2)}, u32[]{:S(2)}) collective-permute-start(f32[16,64,128]{2,1,0:T(8,128)S(1)} %bitcast.80), channel_id=1, source_target_pairs={{0,1},{1,0},{2,3},{3,2},{4,5},{5,4},{6,7},{7,6},{8,9},{9,8},{10,11... | collective-permute-start | bytes 1572872 | tf_op jit(solution)/shard_map/ppermute | solution.py:407
  141.9 1.7 copy-start.4
  155.8 1.5 copy-start
  183.5 6.7 %collective-permute-start.19 = (f32[16,64,128]{2,1,0:T(8,128)S(1)}, f32[16,64,128]{2,1,0:T(8,128)S(1)}, u32[]{:S(2)}, u32[]{:S(2)}) collective-permute-start(f32[16,64,128]{2,1,0:T(8,128)S(1)} %all_to_all.38.own), channel_id=1, source_target_pairs={{0,1},{1,0},{2,3},{3,2},{4,5},{5,4},{6,7},{7,6},{8,9},{9,8},{10,11... | collective-permute-start | bytes 1572872 | tf_op jit(solution)/shard_map/ppermute | solution.py:407
  190.1 1.7 copy-start.1
  230.4 6.8 %collective-permute-start.20 = (f32[16,64,128]{2,1,0:T(8,128)S(1)}, f32[16,64,128]{2,1,0:T(8,128)}, u32[]{:S(2)}, u32[]{:S(2)}) collective-permute-start(f32[16,64,128]{2,1,0:T(8,128)S(1)} %all_to_all.40.own), channel_id=1, source_target_pairs={{0,1},{1,0},{2,3},{3,2},{4,5},{5,4},{6,7},{7,6},{8,9},{9,8},{10,11... | collective-permute-start | bytes 1572872 | tf_op jit(solution)/shard_map/ppermute | solution.py:407
  237.2 1.7 copy-start.2
  238.9 32.7 %copy-start.5 = (bf16[1,128,5120]{2,1,0:T(8,128)(2,1)S(1)}, bf16[1,128,5120]{2,1,0:T(8,128)(2,1)}, u32[]{:S(2)}) copy-start(bf16[1,128,5120]{2,1,0:T(8,128)(2,1)} %param.3) | copy-start | bytes 3932164
  238.9 32.7 %copy-start.6 = (bf16[1,128,5120]{2,1,0:T(8,128)(2,1)S(1)}, bf16[1,128,5120]{2,1,0:T(8,128)(2,1)}, u32[]{:S(2)}) copy-start(bf16[1,128,5120]{2,1,0:T(8,128)(2,1)} %param.4) | copy-start | bytes 3932164
  266.3 5.3 %collective-permute-start.21 = (f32[16,80,128]{2,1,0:T(8,128)S(1)}, f32[16,80,128]{2,1,0:T(8,128)S(1)}, u32[]{:S(2)}, u32[]{:S(2)}) collective-permute-start(f32[16,80,128]{2,1,0:T(8,128)S(1)} %all_to_all.41.own), channel_id=1, source_target_pairs={{0,1},{1,0},{2,3},{3,2},{4,5},{5,4},{6,7},{7,6},{8,9},{9,8},{10,11... | collective-permute-start | bytes 1966088 | tf_op jit(solution)/shard_map/ppermute | solution.py:407

commit v3 on v2

--- a/solution.py
+++ b/solution.py
@@ -39,8 +39,9 @@
     return pltpu.CompilerParams(vmem_limit_bytes=limit)
 
 
-def start_kernel(grads, errors, q_start, out, g_held, e_held, q_held, sems):
-    reps, tall, rows = out.shape
+def start_kernel(grads, errors, q_start, near, far, g_held, e_held, q_held, sems):
+    reps, tall, rows = near.shape
+    split = tall - 8
     rank, width = q_start.shape
     cut = width // reps
     extra = rank // reps
@@ -59,25 +60,26 @@
             load.wait()
         g, e = g_held[:, span], e_held[:, span]
         turned = (g.astype(F32) + e.astype(F32)).T
-        out[2 * i, :cut, :] = turned[:cut]
-        out[2 * i + 1, :cut, :] = turned[cut:]
+        for side in range(2):
+            near[2 * i + side, :split, :] = turned[side * cut : side * cut + split]
+            far[2 * i + side] = turned[side * cut + split : (side + 1) * cut]
         high, low = split2(q_held[:, span])
         both = jnp.concatenate([high, low], axis=0)
         left = left + (dot(both, g, NT) + dot(both, e, NT))
     left = left[:rank] + left[rank:]
     for i in range(reps):
-        out[i, cut : cut + extra, :] = left[extra * i : extra * (i + 1)]
-        out[i, cut + extra :, :] = jnp.zeros((tall - cut - extra, rows), F32)
-
-
-def start(grads, errors, q_start, reps):
+        near[i, split : split + extra, :] = left[extra * i : extra * (i + 1)]
+        near[i, split + extra :, :] = jnp.zeros((tall - split - extra, rows), F32)
+
+
+def start(grads, errors, q_start, reps, split):
     rows, width = grads.shape
-    tall = width // reps + 8
+    rest = width // reps - split
     return pl.pallas_call(
         start_kernel,
         in_specs=[HBM_SPEC] * 3,
-        out_specs=VMEM_SPEC,
-        out_shape=jax.ShapeDtypeStruct((reps, tall, rows), F32),
+        out_specs=[VMEM_SPEC, VMEM_SPEC],
+        out_shape=[jax.ShapeDtypeStruct((reps, tall, rows), F32) for tall in (split + 8, rest)],
         scratch_shapes=[
             pltpu.VMEM(grads.shape, BF16),
             pltpu.VMEM(errors.shape, BF16),
@@ -223,24 +225,30 @@
         out[2 * j + 1] = x[:, rows:]
 
 
-def first_kernel(scale, info, own, other, total, total_other, out, high_out, low_out, held, high, low, sems):
-    length = own.shape[0]
-    for mine, blocks in ((True, total), (False, total_other)):
+def orth_kernel(info, own, other, rows_out, weights_out, held):
+    weights_out[...] = orthonormal(info, own, other, held)
+    rows_out[...] = held[...]
+
+
+def first_kernel(scale, info, held, second, near, near_other, far, far_other, out, high_out, low_out, high, low, sems):
+    length = out.shape[0]
+    split = near.shape[2]
+    for mine, pieces in ((True, (near, far)), (False, (near_other, far_other))):
         at = planes(info, length, mine)
         core = info[1] if mine else 1 - info[1]
         for j in range(length // 2):
             for stream in range(2):
                 side = core if stream == 0 else 1 - core
                 span = pl.ds(pl.multiple_of(at(j) + side * LANES, LANES), LANES)
-                high[:, span], low[:, span] = split2(blocks[j, stream])
+                for blocks, rows in zip(pieces, (slice(0, split), slice(split, high.shape[0]))):
+                    high[rows, span], low[rows, span] = split2(blocks[j, stream])
     stores = [
         pltpu.make_async_copy(high, high_out, sems.at[0]),
         pltpu.make_async_copy(low, low_out, sems.at[1]),
     ]
     for store in stores:
         store.start()
-    second = orthonormal(info, own, other, held)
-    next_left(info, right_factor(scale, second, held, high, low), high, low, out)
+    next_left(info, right_factor(scale, second[...], held, high, low), high, low, out)
     for store in stores:
         store.wait()
 
@@ -289,20 +297,33 @@
     return [pltpu.VMEM((4 * rank, n), BF16)], [pltpu.VMEM((cut, n), BF16)] * 2
 
 
-def first(scale, info, own, other, total, total_other):
+def orth(info, own, other):
     length, rank, rows = own.shape
-    cut = total.shape[2]
-    held, both = scratch(length, rank, cut)
+    shape = (4 * rank, 2 * length * rows)
+    return pl.pallas_call(
+        orth_kernel,
+        in_specs=[SMEM_SPEC, VMEM_SPEC, VMEM_SPEC],
+        out_shape=[jax.ShapeDtypeStruct(shape, BF16), jax.ShapeDtypeStruct((rank, 2 * rank), F32)],
+        scratch_shapes=[pltpu.VMEM(shape, BF16)],
+        compiler_params=params(),
+        name="orth",
+    )(info, own, other)
+
+
+def first(scale, info, held, second, near, far, shape):
+    length, rank, rows = shape
+    cut = near[0].shape[2] + far[0].shape[2]
+    _, both = scratch(length, rank, cut)
     whole = jax.ShapeDtypeStruct((cut, 2 * length * rows), BF16)
     return pl.pallas_call(
         functools.partial(first_kernel, scale),
-        in_specs=[SMEM_SPEC] + [VMEM_SPEC] * 4,
+        in_specs=[SMEM_SPEC] + [VMEM_SPEC] * 6,
         out_specs=[VMEM_SPEC, HBM_SPEC, HBM_SPEC],
-        out_shape=[jax.ShapeDtypeStruct(own.shape, F32), whole, whole],
-        scratch_shapes=held + both + [pltpu.SemaphoreType.DMA((2,))],
+        out_shape=[jax.ShapeDtypeStruct(shape, F32), whole, whole],
+        scratch_shapes=both + [pltpu.SemaphoreType.DMA((2,))],
         compiler_params=params(),
         name="first",
-    )(info, own, other, total, total_other)
+    )(info, held, second, *near, *far)
 
 
 def step(scale, info, own, other, high, low):
@@ -407,14 +428,17 @@
     return lax.ppermute(block, "core", [(0, 1), (1, 0)])
 
 
-def ring(block, length):
-    half = length // 2
+def ring_step(block, length, both):
     up = [(2 * i, 2 * ((i + 1) % length)) for i in range(length)]
     down = [(2 * i + 1, 2 * ((i - 1) % length) + 1) for i in range(length)]
-    blocks = [block]
-    for s in range(half):
-        blocks.append(lax.ppermute(blocks[-1], ("z", "core"), up + down if s < half - 1 else down))
-    return blocks
+    return lax.ppermute(block, ("z", "core"), up + down if both else down)
+
+
+def after(x, earlier):
+    return lax.optimization_barrier((x, earlier))[0]
+
+
+LAG = 1
 
 
 def body(grads, errors, q_start):
@@ -424,21 +448,41 @@
     reps, length = lax.axis_size("rep"), lax.axis_size("z")
     core, place = lax.axis_index("core"), lax.axis_index("z")
     cut, extra = width // reps, rank // reps
+    split = cut // 2
+    half = length // 2
     scale = 1.0 / reps
     flag = core.reshape(1).astype(jnp.int32)
     info = jnp.stack([place, core]).astype(jnp.int32)
 
-    block = jnp.sum(exchange(start(grads, errors, q_start, reps), "rep"), axis=0)
-    streams = ring(block, length), ring(swap_cores(block), length)
-    held = jnp.stack(
-        [jnp.stack([jnp.where(core == 0, x[j], x[j + 1]) for x in streams]) for j in range(length // 2)]
-    )
-    total = held[:, :, :cut]
-    piece = held[:, :, cut : cut + extra]
+    def pair(block):
+        return jnp.stack([block, swap_cores(block)])
+
+    near, far = start(grads, errors, q_start, reps, split)
+    near = jnp.sum(exchange(near, "rep"), axis=0)
+    far = jnp.sum(exchange(after(far, near), "rep"), axis=0)
+    rings = [[pair(near)], []]
+    for turn in range(half + LAG):
+        if turn == LAG:
+            rings[1].append(pair(after(far, rings[0][-1])))
+        for blocks in rings:
+            s = len(blocks)
+            if 0 < s <= half:
+                blocks.append(ring_step(blocks[-1], length, s < half))
+    def stacked(blocks):
+        return jnp.stack([jnp.where(core == 0, blocks[j], blocks[j + 1]) for j in range(half)])
+
+    near = stacked(rings[0])
+    piece = near[:, :, split : split + extra]
+    near = near[:, :, :split]
     piece = jnp.where(core == 0, piece, piece[:, ::-1]).reshape(length * extra, rows)
     own = gather(piece, "rep", reps).reshape(reps, length, extra, rows)
     own = own.transpose(1, 0, 2, 3).reshape(length, rank, rows)
-    partial, high, low = first(scale, info, own, swap_cores(own), total, swap_cores(total))
+    rings[1][-1] = after(rings[1][-1], own)
+    far = stacked(rings[1])
+    held, weight = orth(info, own, swap_cores(own))
+    partial, high, low = first(
+        scale, info, held, weight, (near, swap_cores(near)), (far, swap_cores(far)), own.shape
+    )
     for turn in range(ITERS - 1):
         own = gather(jnp.sum(exchange(partial, "rep"), axis=0), "rep", reps)
         if turn < ITERS - 2:

time: 276 us -> 314 us (1.14)
  starting transfers between devices: 91.1 us -> 123 us
  blocking collectives: 120 us -> 95 us
  waiting for transfers between devices: 9.6 us -> 34.3 us
    all_to_all x7 -> x6, blocking collectives: 120 us -> 95 us  [exchange(): return lax.all_to_all(chunks, axis, 0, 0)]
    ppermute x16, waiting for transfers between devices: 3.38 us -> 27.3 us  [ring_step(): return lax.ppermute(block, ('z', 'core'), up + down if both else down)]
    ppermute x16, starting transfers between devices: 65 us -> 81.9 us  [ring_step(): return lax.ppermute(block, ('z', 'core'), up + down if both else down)]
    pallas_call x1 -> x2, Pallas kernels: 5 us -> 13.3 us  [the longest x1 8.36 us: orth(): pl.pallas_call(orth_kernel, in_specs=[SMEM_SPEC, VMEM_SPEC, VMEM_SPEC], o...]
    all_to_all x0 -> x2, starting transfers between devices: none -> 7.92 us  [exchange(): return lax.all_to_all(chunks, axis, 0, 0)]
    ppermute x6 -> x8, starting transfers between devices: 26.1 us -> 33.6 us  [swap_cores(): return lax.ppermute(block, 'core', [(0, 1), (1, 0)])]
    pallas_call x1, Pallas kernels: 12.2 us -> 6.99 us  [first(): pl.pallas_call(functools.partial(first_kernel, scale), in_specs=[SMEM_SPE...]
    unnamed x14 -> x18, local copies, waits for them, and re-layouts: 6.73 us -> 8.7 us
  transfers between devices with their start and end apart: 22 -> 26, of which waited for: 5 -> 18; matrix products, arithmetic and copies ran while one was open for 0% -> 1% of each run, Pallas kernels for 0% -> 3%
where the time goes in v3:
time: 314 us; the launch traced here: 313 us
  starting transfers between devices  123 us (39%)
  blocking collectives  95 us (30%)
  Pallas kernels  48 us (15%)
  waiting for transfers between devices  34.3 us (11%)
  local copies, waits for them, and re-layouts  10.4 us (3%)
    all_to_all x6, blocking collectives, exchange(): return lax.all_to_all(chunks, axis, 0, 0)  95 us
    ppermute x16, starting transfers between devices, ring_step(): return lax.ppermute(block, ('z', 'core'), up + down if both else down)  81.9 us
    ppermute x8, starting transfers between devices, swap_cores(): return lax.ppermute(block, 'core', [(0, 1), (1, 0)])  33.6 us
    ppermute x16, waiting for transfers between devices, ring_step(): return lax.ppermute(block, ('z', 'core'), up + down if both else down)  27.3 us
    pallas_call x1, Pallas kernels, step(): pl.pallas_call(functools.partial(step_kernel, scale), in_specs=[SMEM_SPEC...  12.3 us
    pallas_call x1, Pallas kernels, last(): pl.pallas_call(functools.partial(last_kernel, scale), in_specs=[SMEM_SPEC...  12.3 us
    unnamed x18, local copies, waits for them, and re-layouts  8.7 us
    pallas_call x1, Pallas kernels, orth(): pl.pallas_call(orth_kernel, in_specs=[SMEM_SPEC, VMEM_SPEC, VMEM_SPEC], o...  8.36 us
  transfers between devices with their start and end apart: 26, of which 18 were waited for; matrix products, arithmetic and copies ran while one was open for 1% of the time, Pallas kernels for 3%

profile of v3, /device:TPU:1, one launch (start us, length us, event | category | flops | bytes accessed | tf_op | source)
XLA Modules:
  0.0 313.0 jit_solution(992355026414530030)
XLA Ops:
  0.6 4.9 %start.1 = (f32[16,168,128]{2,1,0:T(8,128)}, f32[16,160,128]{2,1,0:T(8,128)}) custom-call(bf16[128,5120]{1,0:T(8,128)(2,1)} %bitcast.48, bf16[128,5120]{1,0:T(8,128)(2,1)} %bitcast.50, f32[64,5120]{1,0:T(8,128)} %q_start.1), custom_call_target="tpu_custom_call" | custom-call | tf_op jit(solution)/shard_map/start/pallas_call | solution.py:78
  5.6 24.4 %all_to_all.40 = f32[16,168,128]{2,1,0:T(8,128)S(1)} all-to-all(f32[16,168,128]{2,1,0:T(8,128)} %get-tuple-element.16), channel_id=1, replica_groups=mesh['rep'=16,'z'=16,'core'=2] {'rep'}, dimensions={0} | all-to-all | bytes 2752512 | tf_op jit(solution)/shard_map/all_to_all | solution.py:420
  30.1 6.4 %collective-permute-start = (f32[168,128]{1,0:T(8,128)S(1)}, f32[168,128]{1,0:T(8,128)S(1)}, u32[]{:S(2)}, u32[]{:S(2)}) collective-permute-start(f32[168,128]{1,0:T(8,128)S(1)} %reduce_sum.36), channel_id=1, source_target_pairs={{0,1},{1,0},{2,3},{3,2},{4,5},{5,4},{6,7},{7,6},{8,9},{9,8},{10,11... | collective-permute-start | bytes 258056 | tf_op jit(solution)/shard_map/ppermute | solution.py:428
  37.4 11.1 %collective-permute-start.1 = (f32[2,168,128]{2,1,0:T(8,128)S(1)}, f32[2,168,128]{2,1,0:T(8,128)S(1)}, u32[]{:S(2)}, u32[]{:S(2)}) collective-permute-start(f32[2,168,128]{2,1,0:T(8,128)S(1)} %pad_maximum_fusion), channel_id=1, source_target_pairs={{0,2},{2,4},{4,6},{6,8},{8,10},{10,12},{12,14},{14,16},{16,18},{18... | collective-permute-start | bytes 516104 | tf_op jit(solution)/shard_map/ppermute | solution.py:434
  48.6 3.7 %all-to-all-start.2 = ((f32[16,160,128]{2,1,0:T(8,128)}), f32[16,160,128]{2,1,0:T(8,128)S(1)}, u32[]{:S(2)}, u32[]{:S(2)}) async-start(f32[16,160,128]{2,1,0:T(8,128)} %get-tuple-element.20), calls=%async_computation.2 | async-start | bytes 2621440 | tf_op jit(solution)/shard_map/all_to_all | solution.py:420
  58.8 4.8 %collective-permute-start.3 = (f32[2,168,128]{2,1,0:T(8,128)S(1)}, f32[2,168,128]{2,1,0:T(8,128)S(1)}, u32[]{:S(2)}, u32[]{:S(2)}) collective-permute-start(f32[2,168,128]{2,1,0:T(8,128)S(1)} %collective-permute-done.2), channel_id=1, source_target_pairs={{0,2},{2,4},{4,6},{6,8},{8,10},{10,12},{12,14},{14,16},{16,18},{18... | collective-permute-start | bytes 516104 | tf_op jit(solution)/shard_map/ppermute | solution.py:434
  65.9 5.3 %collective-permute-start.4 = (f32[2,168,128]{2,1,0:T(8,128)S(1)}, f32[2,168,128]{2,1,0:T(8,128)S(1)}, u32[]{:S(2)}, u32[]{:S(2)}) collective-permute-start(f32[2,168,128]{2,1,0:T(8,128)S(1)} %collective-permute-done.3), channel_id=1, source_target_pairs={{0,2},{2,4},{4,6},{6,8},{8,10},{10,12},{12,14},{14,16},{16,18},{18... | collective-permute-start | bytes 516104 | tf_op jit(solution)/shard_map/ppermute | solution.py:434
  73.5 5.0 %collective-permute-start.5 = (f32[2,168,128]{2,1,0:T(8,128)S(1)}, f32[2,168,128]{2,1,0:T(8,128)S(1)}, u32[]{:S(2)}, u32[]{:S(2)}) collective-permute-start(f32[2,168,128]{2,1,0:T(8,128)S(1)} %collective-permute-done.4), channel_id=1, source_target_pairs={{0,2},{2,4},{4,6},{6,8},{8,10},{10,12},{12,14},{14,16},{16,18},{18... | collective-permute-start | bytes 516104 | tf_op jit(solution)/shard_map/ppermute | solution.py:434
  80.9 5.0 %collective-permute-start.6 = (f32[2,168,128]{2,1,0:T(8,128)S(1)}, f32[2,168,128]{2,1,0:T(8,128)S(1)}, u32[]{:S(2)}, u32[]{:S(2)}) collective-permute-start(f32[2,168,128]{2,1,0:T(8,128)S(1)} %collective-permute-done.5), channel_id=1, source_target_pairs={{0,2},{2,4},{4,6},{6,8},{8,10},{10,12},{12,14},{14,16},{16,18},{18... | collective-permute-start | bytes 516104 | tf_op jit(solution)/shard_map/ppermute | solution.py:434
  88.2 5.0 %collective-permute-start.7 = (f32[2,168,128]{2,1,0:T(8,128)S(1)}, f32[2,168,128]{2,1,0:T(8,128)S(1)}, u32[]{:S(2)}, u32[]{:S(2)}) collective-permute-start(f32[2,168,128]{2,1,0:T(8,128)S(1)} %collective-permute-done.6), channel_id=1, source_target_pairs={{0,2},{2,4},{4,6},{6,8},{8,10},{10,12},{12,14},{14,16},{16,18},{18... | collective-permute-start | bytes 516104 | tf_op jit(solution)/shard_map/ppermute | solution.py:434
  93.4 5.6 %collective-permute-start.11 = (f32[160,128]{1,0:T(8,128)S(1)}, f32[160,128]{1,0:T(8,128)S(1)}, u32[]{:S(2)}, u32[]{:S(2)}) collective-permute-start(f32[160,128]{1,0:T(8,128)S(1)} %reduce_sum.37), channel_id=1, source_target_pairs={{0,1},{1,0},{2,3},{3,2},{4,5},{5,4},{6,7},{7,6},{8,9},{9,8},{10,11... | collective-permute-start | bytes 245768 | tf_op jit(solution)/shard_map/ppermute | solution.py:428
  99.0 4.9 %collective-permute-start.8 = (f32[2,168,128]{2,1,0:T(8,128)S(1)}, f32[2,168,128]{2,1,0:T(8,128)S(1)}, u32[]{:S(2)}, u32[]{:S(2)}) collective-permute-start(f32[2,168,128]{2,1,0:T(8,128)S(1)} %collective-permute-done.7), channel_id=1, source_target_pairs={{1,31},{3,1},{5,3},{7,5},{9,7},{11,9},{13,11},{15,13},{17,15},{19,... | collective-permute-start | bytes 516104 | tf_op jit(solution)/shard_map/ppermute | solution.py:434
  107.4 4.2 %all-to-all-start.1 = ((f32[16,64,128]{2,1,0:T(8,128)}), f32[16,64,128]{2,1,0:T(8,128)S(1)}, u32[]{:S(2)}, u32[]{:S(2)}) async-start(f32[16,64,128]{2,1,0:T(8,128)} %broadcast_in_dim.15), calls=%async_computation.1 | async-start | bytes 1048576 | tf_op jit(solution)/shard_map/all_to_all | solution.py:420
  113.8 4.9 %collective-permute-start.13 = (f32[2,160,128]{2,1,0:T(8,128)S(1)}, f32[2,160,128]{2,1,0:T(8,128)S(1)}, u32[]{:S(2)}, u32[]{:S(2)}) collective-permute-start(f32[2,160,128]{2,1,0:T(8,128)S(1)} %collective-permute-done.12), channel_id=1, source_target_pairs={{0,2},{2,4},{4,6},{6,8},{8,10},{10,12},{12,14},{14,16},{16,18},{18... | collective-permute-start | bytes 491528 | tf_op jit(solution)/shard_map/ppermute | solution.py:434
  120.9 5.3 %collective-permute-start.14 = (f32[2,160,128]{2,1,0:T(8,128)S(1)}, f32[2,160,128]{2,1,0:T(8,128)S(1)}, u32[]{:S(2)}, u32[]{:S(2)}) collective-permute-start(f32[2,160,128]{2,1,0:T(8,128)S(1)} %collective-permute-done.13), channel_id=1, source_target_pairs={{0,2},{2,4},{4,6},{6,8},{8,10},{10,12},{12,14},{14,16},{16,18},{18... | collective-permute-start | bytes 491528 | tf_op jit(solution)/shard_map/ppermute | solution.py:434
  128.5 5.0 %collective-permute-start.15 = (f32[2,160,128]{2,1,0:T(8,128)S(1)}, f32[2,160,128]{2,1,0:T(8,128)S(1)}, u32[]{:S(2)}, u32[]{:S(2)}) collective-permute-start(f32[2,160,128]{2,1,0:T(8,128)S(1)} %collective-permute-done.14), channel_id=1, source_target_pairs={{0,2},{2,4},{4,6},{6,8},{8,10},{10,12},{12,14},{14,16},{16,18},{18... | collective-permute-start | bytes 491528 | tf_op jit(solution)/shard_map/ppermute | solution.py:434
  135.7 5.0 %collective-permute-start.16 = (f32[2,160,128]{2,1,0:T(8,128)S(1)}, f32[2,160,128]{2,1,0:T(8,128)S(1)}, u32[]{:S(2)}, u32[]{:S(2)}) collective-permute-start(f32[2,160,128]{2,1,0:T(8,128)S(1)} %collective-permute-done.15), channel_id=1, source_target_pairs={{0,2},{2,4},{4,6},{6,8},{8,10},{10,12},{12,14},{14,16},{16,18},{18... | collective-permute-start | bytes 491528 | tf_op jit(solution)/shard_map/ppermute | solution.py:434
  143.0 5.0 %collective-permute-start.17 = (f32[2,160,128]{2,1,0:T(8,128)S(1)}, f32[2,160,128]{2,1,0:T(8,128)S(1)}, u32[]{:S(2)}, u32[]{:S(2)}) collective-permute-start(f32[2,160,128]{2,1,0:T(8,128)S(1)} %collective-permute-done.16), channel_id=1, source_target_pairs={{0,2},{2,4},{4,6},{6,8},{8,10},{10,12},{12,14},{14,16},{16,18},{18... | collective-permute-start | bytes 491528 | tf_op jit(solution)/shard_map/ppermute | solution.py:434
  150.2 5.0 %collective-permute-start.18 = (f32[2,160,128]{2,1,0:T(8,128)S(1)}, f32[2,160,128]{2,1,0:T(8,128)S(1)}, u32[]{:S(2)}, u32[]{:S(2)}) collective-permute-start(f32[2,160,128]{2,1,0:T(8,128)S(1)} %collective-permute-done.17), channel_id=1, source_target_pairs={{0,2},{2,4},{4,6},{6,8},{8,10},{10,12},{12,14},{14,16},{16,18},{18... | collective-permute-start | bytes 491528 | tf_op jit(solution)/shard_map/ppermute | solution.py:434
  157.5 5.0 %collective-permute-start.19 = (f32[2,160,128]{2,1,0:T(8,128)S(1)}, f32[2,160,128]{2,1,0:T(8,128)S(1)}, u32[]{:S(2)}, u32[]{:S(2)}) collective-permute-start(f32[2,160,128]{2,1,0:T(8,128)S(1)} %collective-permute-done.18), channel_id=1, source_target_pairs={{1,31},{3,1},{5,3},{7,5},{9,7},{11,9},{13,11},{15,13},{17,15},{19,... | collective-permute-start | bytes 491528 | tf_op jit(solution)/shard_map/ppermute | solution.py:434
  172.3 8.4 %orth.1 = (bf16[256,4096]{1,0:T(8,128)(2,1)S(1)}, f32[64,128]{1,0:T(8,128)S(1)}) custom-call(s32[2]{0:T(128)S(1)} %pad_add_fusion.info, f32[16,64,128]{2,1,0:T(8,128)S(1)} %bitcast.53, f32[16,64,128]{2,1,0:T(8,128)} %collective-permute-done.9.other), custom_call_target="tpu_custom_call" | custom-call | tf_op jit(solution)/shard_map/orth/pallas_call | solution.py:303
  183.3 7.0 %first.1 = (f32[16,64,128]{2,1,0:T(8,128)S(1)}, bf16[320,4096]{1,0:T(8,128)(2,1)S(1)}, bf16[320,4096]{1,0:T(8,128)(2,1)S(1)}) custom-call(s32[2]{0:T(128)S(1)} %pad_add_fusion.info, bf16[256,4096]{1,0:T(8,128)(2,1)S(1)} %get-tuple-element.17.held, f32[64,128]{1,0:T(8,128)S(1)} %get-tuple-element.18.second, f32[8,2,160,128]{3,2,1,0:T(8,128)S(1)} %copy-done.6, ...), custom_call_target="tpu_custom_call" | custom-call | tf_op jit(solution)/shard_map/first/pallas_call | solution.py:318
  191.8 16.6 %all_to_all.41 = f32[16,64,128]{2,1,0:T(8,128)S(1)} all-to-all(f32[16,64,128]{2,1,0:T(8,128)S(1)} %get-tuple-element.23), channel_id=1, replica_groups=mesh['rep'=16,'z'=16,'core'=2] {'rep'}, dimensions={0} | all-to-all | bytes 1048576 | tf_op jit(solution)/shard_map/all_to_all | solution.py:420
  208.5 12.9 %all_to_all.42.own = f32[16,64,128]{2,1,0:T(8,128)S(1)} all-to-all(f32[16,64,128]{2,1,0:T(8,128)S(1)} %broadcast_in_dim.32), channel_id=1, replica_groups=mesh['rep'=16,'z'=16,'core'=2] {'rep'}, dimensions={0} | all-to-all | bytes 1048576 | tf_op jit(solution)/shard_map/all_to_all | solution.py:420
  221.4 5.7 %collective-permute-start.21 = (f32[16,64,128]{2,1,0:T(8,128)S(1)}, f32[16,64,128]{2,1,0:T(8,128)S(1)}, u32[]{:S(2)}, u32[]{:S(2)}) collective-permute-start(f32[16,64,128]{2,1,0:T(8,128)S(1)} %all_to_all.42.own), channel_id=1, source_target_pairs={{0,1},{1,0},{2,3},{3,2},{4,5},{5,4},{6,7},{7,6},{8,9},{9,8},{10,11... | collective-permute-start | bytes 1572872 | tf_op jit(solution)/shard_map/ppermute | solution.py:428
  230.1 12.3 %step.1 = f32[16,64,128]{2,1,0:T(8,128)S(1)} custom-call(s32[2]{0:T(128)S(1)} %pad_add_fusion.info, f32[16,64,128]{2,1,0:T(8,128)S(1)} %all_to_all.42.own, f32[16,64,128]{2,1,0:T(8,128)S(1)} %collective-permute-done.21.other, bf16[320,4096]{1,0:T(8,128)(2,1)S(1)} %get-tuple-element.24.high_in, bf16[320,4096]{1,0:T(8,128)(2,1)S(1)} %copy-done.1), custom_call_target="tpu_custom_call" | custom-call | tf_op jit(solution)/shard_map/step/pallas_call | solution.py:332
  242.5 13.3 %all_to_all.43 = f32[16,64,128]{2,1,0:T(8,128)S(1)} all-to-all(f32[16,64,128]{2,1,0:T(8,128)S(1)} %step.1), channel_id=1, replica_groups=mesh['rep'=16,'z'=16,'core'=2] {'rep'}, dimensions={0} | all-to-all | bytes 1048576 | tf_op jit(solution)/shard_map/all_to_all | solution.py:420
  255.9 12.7 %all_to_all.44.own = f32[16,64,128]{2,1,0:T(8,128)S(1)} all-to-all(f32[16,64,128]{2,1,0:T(8,128)S(1)} %broadcast_in_dim.33), channel_id=1, replica_groups=mesh['rep'=16,'z'=16,'core'=2] {'rep'}, dimensions={0} | all-to-all | bytes 1048576 | tf_op jit(solution)/shard_map/all_to_all | solution.py:420
  268.6 5.4 %collective-permute-start.22 = (f32[16,64,128]{2,1,0:T(8,128)S(1)}, f32[16,64,128]{2,1,0:T(8,128)}, u32[]{:S(2)}, u32[]{:S(2)}) collective-permute-start(f32[16,64,128]{2,1,0:T(8,128)S(1)} %all_to_all.44.own), channel_id=1, source_target_pairs={{0,1},{1,0},{2,3},{3,2},{4,5},{5,4},{6,7},{7,6},{8,9},{9,8},{10,11... | collective-permute-start | bytes 1572872 | tf_op jit(solution)/shard_map/ppermute | solution.py:428
  277.2 12.3 %last.1 = (f32[2,80,128]{2,1,0:T(8,128)S(1)}, f32[64,128]{1,0:T(8,128)S(1)}) custom-call(s32[2]{0:T(128)S(1)} %pad_add_fusion.info, f32[16,64,128]{2,1,0:T(8,128)S(1)} %all_to_all.44.own, f32[16,64,128]{2,1,0:T(8,128)} %collective-permute-done.22.other, bf16[320,4096]{1,0:T(8,128)(2,1)S(1)} %get-tuple-element.24.high_in, bf16[320,4096]{1,0:T(8,128)(2,1)S(1)} %copy-done.2), custom_call_target="tpu_custom_call" | custom-call | tf_op jit(solution)/shard_map/last/pallas_call | solution.py:346
  289.6 15.1 %all_to_all.45.own = f32[16,80,128]{2,1,0:T(8,128)S(1)} all-to-all(f32[16,80,128]{2,1,0:T(8,128)S(1)} %broadcast_in_dim.35), channel_id=1, replica_groups=mesh['rep'=16,'z'=16,'core'=2] {'rep'}, dimensions={0} | all-to-all | bytes 1310720 | tf_op jit(solution)/shard_map/all_to_all | solution.py:420
  304.6 3.6 %collective-permute-start.23 = (f32[16,80,128]{2,1,0:T(8,128)S(1)}, f32[16,80,128]{2,1,0:T(8,128)S(1)}, u32[]{:S(2)}, u32[]{:S(2)}) collective-permute-start(f32[16,80,128]{2,1,0:T(8,128)S(1)} %all_to_all.45.own), channel_id=1, source_target_pairs={{0,1},{1,0},{2,3},{3,2},{4,5},{5,4},{6,7},{7,6},{8,9},{9,8},{10,11... | collective-permute-start | bytes 1966088 | tf_op jit(solution)/shard_map/ppermute | solution.py:428
  (83 shorter events, 60.8 us)
Async XLA Ops:
  30.1 7.3 %collective-permute-start = (f32[168,128]{1,0:T(8,128)S(1)}, f32[168,128]{1,0:T(8,128)S(1)}, u32[]{:S(2)}, u32[]{:S(2)}) collective-permute-start(f32[168,128]{1,0:T(8,128)S(1)} %reduce_sum.36), channel_id=1, source_target_pairs={{0,1},{1,0},{2,3},{3,2},{4,5},{5,4},{6,7},{7,6},{8,9},{9,8},{10,11... | collective-permute-start | bytes 258056 | tf_op jit(solution)/shard_map/ppermute | solution.py:428
  37.4 14.9 %collective-permute-start.1 = (f32[2,168,128]{2,1,0:T(8,128)S(1)}, f32[2,168,128]{2,1,0:T(8,128)S(1)}, u32[]{:S(2)}, u32[]{:S(2)}) collective-permute-start(f32[2,168,128]{2,1,0:T(8,128)S(1)} %pad_maximum_fusion), channel_id=1, source_target_pairs={{0,2},{2,4},{4,6},{6,8},{8,10},{10,12},{12,14},{14,16},{16,18},{18... | collective-permute-start | bytes 516104 | tf_op jit(solution)/shard_map/ppermute | solution.py:434
  48.6 44.7 %all-to-all-start.2 = ((f32[16,160,128]{2,1,0:T(8,128)}), f32[16,160,128]{2,1,0:T(8,128)S(1)}, u32[]{:S(2)}, u32[]{:S(2)}) async-start(f32[16,160,128]{2,1,0:T(8,128)} %get-tuple-element.20), calls=%async_computation.2 | async-start | bytes 2621440 | tf_op jit(solution)/shard_map/all_to_all | solution.py:420
  52.3 6.4 %collective-permute-start.2 = (f32[2,168,128]{2,1,0:T(8,128)S(1)}, f32[2,168,128]{2,1,0:T(8,128)S(1)}, u32[]{:S(2)}, u32[]{:S(2)}) collective-permute-start(f32[2,168,128]{2,1,0:T(8,128)S(1)} %collective-permute-done.1), channel_id=1, source_target_pairs={{0,2},{2,4},{4,6},{6,8},{8,10},{10,12},{12,14},{14,16},{16,18},{18... | collective-permute-start | bytes 516104 | tf_op jit(solution)/shard_map/ppermute | solution.py:434
  58.8 7.1 %collective-permute-start.3 = (f32[2,168,128]{2,1,0:T(8,128)S(1)}, f32[2,168,128]{2,1,0:T(8,128)S(1)}, u32[]{:S(2)}, u32[]{:S(2)}) collective-permute-start(f32[2,168,128]{2,1,0:T(8,128)S(1)} %collective-permute-done.2), channel_id=1, source_target_pairs={{0,2},{2,4},{4,6},{6,8},{8,10},{10,12},{12,14},{14,16},{16,18},{18... | collective-permute-start | bytes 516104 | tf_op jit(solution)/shard_map/ppermute | solution.py:434
  65.9 7.6 %collective-permute-start.4 = (f32[2,168,128]{2,1,0:T(8,128)S(1)}, f32[2,168,128]{2,1,0:T(8,128)S(1)}, u32[]{:S(2)}, u32[]{:S(2)}) collective-permute-start(f32[2,168,128]{2,1,0:T(8,128)S(1)} %collective-permute-done.3), channel_id=1, source_target_pairs={{0,2},{2,4},{4,6},{6,8},{8,10},{10,12},{12,14},{14,16},{16,18},{18... | collective-permute-start | bytes 516104 | tf_op jit(solution)/shard_map/ppermute | solution.py:434
  73.5 7.3 %collective-permute-start.5 = (f32[2,168,128]{2,1,0:T(8,128)S(1)}, f32[2,168,128]{2,1,0:T(8,128)S(1)}, u32[]{:S(2)}, u32[]{:S(2)}) collective-permute-start(f32[2,168,128]{2,1,0:T(8,128)S(1)} %collective-permute-done.4), channel_id=1, source_target_pairs={{0,2},{2,4},{4,6},{6,8},{8,10},{10,12},{12,14},{14,16},{16,18},{18... | collective-permute-start | bytes 516104 | tf_op jit(solution)/shard_map/ppermute | solution.py:434
  80.9 7.3 %collective-permute-start.6 = (f32[2,168,128]{2,1,0:T(8,128)S(1)}, f32[2,168,128]{2,1,0:T(8,128)S(1)}, u32[]{:S(2)}, u32[]{:S(2)}) collective-permute-start(f32[2,168,128]{2,1,0:T(8,128)S(1)} %collective-permute-done.5), channel_id=1, source_target_pairs={{0,2},{2,4},{4,6},{6,8},{8,10},{10,12},{12,14},{14,16},{16,18},{18... | collective-permute-start | bytes 516104 | tf_op jit(solution)/shard_map/ppermute | solution.py:434
  88.2 10.8 %collective-permute-start.7 = (f32[2,168,128]{2,1,0:T(8,128)S(1)}, f32[2,168,128]{2,1,0:T(8,128)S(1)}, u32[]{:S(2)}, u32[]{:S(2)}) collective-permute-start(f32[2,168,128]{2,1,0:T(8,128)S(1)} %collective-permute-done.6), channel_id=1, source_target_pairs={{0,2},{2,4},{4,6},{6,8},{8,10},{10,12},{12,14},{14,16},{16,18},{18... | collective-permute-start | bytes 516104 | tf_op jit(solution)/shard_map/ppermute | solution.py:434
  93.4 10.5 %collective-permute-start.11 = (f32[160,128]{1,0:T(8,128)S(1)}, f32[160,128]{1,0:T(8,128)S(1)}, u32[]{:S(2)}, u32[]{:S(2)}) collective-permute-start(f32[160,128]{1,0:T(8,128)S(1)} %reduce_sum.37), channel_id=1, source_target_pairs={{0,1},{1,0},{2,3},{3,2},{4,5},{5,4},{6,7},{7,6},{8,9},{9,8},{10,11... | collective-permute-start | bytes 245768 | tf_op jit(solution)/shard_map/ppermute | solution.py:428
  99.0 7.2 %collective-permute-start.8 = (f32[2,168,128]{2,1,0:T(8,128)S(1)}, f32[2,168,128]{2,1,0:T(8,128)S(1)}, u32[]{:S(2)}, u32[]{:S(2)}) collective-permute-start(f32[2,168,128]{2,1,0:T(8,128)S(1)} %collective-permute-done.7), channel_id=1, source_target_pairs={{1,31},{3,1},{5,3},{7,5},{9,7},{11,9},{13,11},{15,13},{17,15},{19,... | collective-permute-start | bytes 516104 | tf_op jit(solution)/shard_map/ppermute | solution.py:434
  104.0 9.8 %collective-permute-start.12 = (f32[2,160,128]{2,1,0:T(8,128)S(1)}, f32[2,160,128]{2,1,0:T(8,128)S(1)}, u32[]{:S(2)}, u32[]{:S(2)}) collective-permute-start(f32[2,160,128]{2,1,0:T(8,128)S(1)} %pad_maximum_fusion.1), channel_id=1, source_target_pairs={{0,2},{2,4},{4,6},{6,8},{8,10},{10,12},{12,14},{14,16},{16,18},{18... | collective-permute-start | bytes 491528 | tf_op jit(solution)/shard_map/ppermute | solution.py:434
  106.4 19.8 %copy-start.5 = (f32[8,2,160,128]{3,2,1,0:T(8,128)}, f32[8,2,160,128]{3,2,1,0:T(8,128)S(1)}, u32[]{:S(2)}) copy-start(f32[8,2,160,128]{3,2,1,0:T(8,128)S(1)} %slice.9.near) | copy-start | bytes 3932164
  107.4 26.1 %all-to-all-start.1 = ((f32[16,64,128]{2,1,0:T(8,128)}), f32[16,64,128]{2,1,0:T(8,128)S(1)}, u32[]{:S(2)}, u32[]{:S(2)}) async-start(f32[16,64,128]{2,1,0:T(8,128)} %broadcast_in_dim.15), calls=%async_computation.1 | async-start | bytes 1048576 | tf_op jit(solution)/shard_map/all_to_all | solution.py:420
  111.6 69.1 %collective-permute-start.10 = (f32[8,2,160,128]{3,2,1,0:T(8,128)S(1)}, f32[8,2,160,128]{3,2,1,0:T(8,128)}, u32[]{:S(2)}, u32[]{:S(2)}) collective-permute-start(f32[8,2,160,128]{3,2,1,0:T(8,128)S(1)} %slice.9.near), channel_id=1, source_target_pairs={{0,1},{1,0},{2,3},{3,2},{4,5},{5,4},{6,7},{7,6},{8,9},{9,8},{10,11... | collective-permute-start | bytes 3932168 | tf_op jit(solution)/shard_map/ppermute | solution.py:428
  113.8 7.1 %collective-permute-start.13 = (f32[2,160,128]{2,1,0:T(8,128)S(1)}, f32[2,160,128]{2,1,0:T(8,128)S(1)}, u32[]{:S(2)}, u32[]{:S(2)}) collective-permute-start(f32[2,160,128]{2,1,0:T(8,128)S(1)} %collective-permute-done.12), channel_id=1, source_target_pairs={{0,2},{2,4},{4,6},{6,8},{8,10},{10,12},{12,14},{14,16},{16,18},{18... | collective-permute-start | bytes 491528 | tf_op jit(solution)/shard_map/ppermute | solution.py:434
  120.9 7.6 %collective-permute-start.14 = (f32[2,160,128]{2,1,0:T(8,128)S(1)}, f32[2,160,128]{2,1,0:T(8,128)S(1)}, u32[]{:S(2)}, u32[]{:S(2)}) collective-permute-start(f32[2,160,128]{2,1,0:T(8,128)S(1)} %collective-permute-done.13), channel_id=1, source_target_pairs={{0,2},{2,4},{4,6},{6,8},{8,10},{10,12},{12,14},{14,16},{16,18},{18... | collective-permute-start | bytes 491528 | tf_op jit(solution)/shard_map/ppermute | solution.py:434
  128.5 7.3 %collective-permute-start.15 = (f32[2,160,128]{2,1,0:T(8,128)S(1)}, f32[2,160,128]{2,1,0:T(8,128)S(1)}, u32[]{:S(2)}, u32[]{:S(2)}) collective-permute-start(f32[2,160,128]{2,1,0:T(8,128)S(1)} %collective-permute-done.14), channel_id=1, source_target_pairs={{0,2},{2,4},{4,6},{6,8},{8,10},{10,12},{12,14},{14,16},{16,18},{18... | collective-permute-start | bytes 491528 | tf_op jit(solution)/shard_map/ppermute | solution.py:434
  135.7 7.3 %collective-permute-start.16 = (f32[2,160,128]{2,1,0:T(8,128)S(1)}, f32[2,160,128]{2,1,0:T(8,128)S(1)}, u32[]{:S(2)}, u32[]{:S(2)}) collective-permute-start(f32[2,160,128]{2,1,0:T(8,128)S(1)} %collective-permute-done.15), channel_id=1, source_target_pairs={{0,2},{2,4},{4,6},{6,8},{8,10},{10,12},{12,14},{14,16},{16,18},{18... | collective-permute-start | bytes 491528 | tf_op jit(solution)/shard_map/ppermute | solution.py:434
  143.0 7.3 %collective-permute-start.17 = (f32[2,160,128]{2,1,0:T(8,128)S(1)}, f32[2,160,128]{2,1,0:T(8,128)S(1)}, u32[]{:S(2)}, u32[]{:S(2)}) collective-permute-start(f32[2,160,128]{2,1,0:T(8,128)S(1)} %collective-permute-done.16), channel_id=1, source_target_pairs={{0,2},{2,4},{4,6},{6,8},{8,10},{10,12},{12,14},{14,16},{16,18},{18... | collective-permute-start | bytes 491528 | tf_op jit(solution)/shard_map/ppermute | solution.py:434
  150.2 7.3 %collective-permute-start.18 = (f32[2,160,128]{2,1,0:T(8,128)S(1)}, f32[2,160,128]{2,1,0:T(8,128)S(1)}, u32[]{:S(2)}, u32[]{:S(2)}) collective-permute-start(f32[2,160,128]{2,1,0:T(8,128)S(1)} %collective-permute-done.17), channel_id=1, source_target_pairs={{0,2},{2,4},{4,6},{6,8},{8,10},{10,12},{12,14},{14,16},{16,18},{18... | collective-permute-start | bytes 491528 | tf_op jit(solution)/shard_map/ppermute | solution.py:434
  157.5 7.3 %collective-permute-start.19 = (f32[2,160,128]{2,1,0:T(8,128)S(1)}, f32[2,160,128]{2,1,0:T(8,128)S(1)}, u32[]{:S(2)}, u32[]{:S(2)}) collective-permute-start(f32[2,160,128]{2,1,0:T(8,128)S(1)} %collective-permute-done.18), channel_id=1, source_target_pairs={{1,31},{3,1},{5,3},{7,5},{9,7},{11,9},{13,11},{15,13},{17,15},{19,... | collective-permute-start | bytes 491528 | tf_op jit(solution)/shard_map/ppermute | solution.py:434
  164.8 15.9 %collective-permute-start.20 = (f32[8,2,160,128]{3,2,1,0:T(8,128)S(1)}, f32[8,2,160,128]{3,2,1,0:T(8,128)}, u32[]{:S(2)}, u32[]{:S(2)}) collective-permute-start(f32[8,2,160,128]{3,2,1,0:T(8,128)S(1)} %bitcast_dynamic-update-slice_fusion.8.far), channel_id=1, source_target_pairs={{0,1},{1,0},{2,3},{3,2},{4,5},{5,4},{6,7},{7,6},{8,9},{9,8},{10,11... | collective-permute-start | bytes 3932168 | tf_op jit(solution)/shard_map/ppermute | solution.py:428
  168.4 3.9 %collective-permute-start.9 = (f32[16,64,128]{2,1,0:T(8,128)S(1)}, f32[16,64,128]{2,1,0:T(8,128)}, u32[]{:S(2)}, u32[]{:S(2)}) collective-permute-start(f32[16,64,128]{2,1,0:T(8,128)S(1)} %bitcast.52), channel_id=1, source_target_pairs={{0,1},{1,0},{2,3},{3,2},{4,5},{5,4},{6,7},{7,6},{8,9},{9,8},{10,11... | collective-permute-start | bytes 1572872 | tf_op jit(solution)/shard_map/ppermute | solution.py:428
  190.3 1.5 copy-start
  221.4 7.0 %collective-permute-start.21 = (f32[16,64,128]{2,1,0:T(8,128)S(1)}, f32[16,64,128]{2,1,0:T(8,128)S(1)}, u32[]{:S(2)}, u32[]{:S(2)}) collective-permute-start(f32[16,64,128]{2,1,0:T(8,128)S(1)} %all_to_all.42.own), channel_id=1, source_target_pairs={{0,1},{1,0},{2,3},{3,2},{4,5},{5,4},{6,7},{7,6},{8,9},{9,8},{10,11... | collective-permute-start | bytes 1572872 | tf_op jit(solution)/shard_map/ppermute | solution.py:428
  228.4 1.7 copy-start.1
  268.6 6.8 %collective-permute-start.22 = (f32[16,64,128]{2,1,0:T(8,128)S(1)}, f32[16,64,128]{2,1,0:T(8,128)}, u32[]{:S(2)}, u32[]{:S(2)}) collective-permute-start(f32[16,64,128]{2,1,0:T(8,128)S(1)} %all_to_all.44.own), channel_id=1, source_target_pairs={{0,1},{1,0},{2,3},{3,2},{4,5},{5,4},{6,7},{7,6},{8,9},{9,8},{10,11... | collective-permute-start | bytes 1572872 | tf_op jit(solution)/shard_map/ppermute | solution.py:428
  275.4 1.7 copy-start.2
  277.2 32.8 %copy-start.4 = (bf16[1,128,5120]{2,1,0:T(8,128)(2,1)S(1)}, bf16[1,128,5120]{2,1,0:T(8,128)(2,1)}, u32[]{:S(2)}) copy-start(bf16[1,128,5120]{2,1,0:T(8,128)(2,1)} %param.4) | copy-start | bytes 3932164
  289.5 20.5 %copy-start.3 = (bf16[1,128,5120]{2,1,0:T(8,128)(2,1)S(1)}, bf16[1,128,5120]{2,1,0:T(8,128)(2,1)}, u32[]{:S(2)}) copy-start(bf16[1,128,5120]{2,1,0:T(8,128)(2,1)} %param.3) | copy-start | bytes 3932164
  304.6 5.3 %collective-permute-start.23 = (f32[16,80,128]{2,1,0:T(8,128)S(1)}, f32[16,80,128]{2,1,0:T(8,128)S(1)}, u32[]{:S(2)}, u32[]{:S(2)}) collective-permute-start(f32[16,80,128]{2,1,0:T(8,128)S(1)} %all_to_all.45.own), channel_id=1, source_target_pairs={{0,1},{1,0},{2,3},{3,2},{4,5},{5,4},{6,7},{7,6},{8,9},{9,8},{10,11... | collective-permute-start | bytes 1966088 | tf_op jit(solution)/shard_map/ppermute | solution.py:428
  (3 other events, 3.7 us)

commit v4 on v2

--- a/solution.py
+++ b/solution.py
@@ -12,6 +12,7 @@
 BF16 = jnp.bfloat16
 LANES = 128
 VMEM = 20 * 1024 * 1024
+WIDE = 58 * 1024 * 1024
 SMEM_SPEC = pl.BlockSpec(memory_space=pltpu.SMEM)
 VMEM_SPEC = pl.BlockSpec(memory_space=pltpu.VMEM)
 HBM_SPEC = pl.BlockSpec(memory_space=pltpu.HBM)
@@ -313,7 +314,7 @@
         in_specs=[SMEM_SPEC, VMEM_SPEC, VMEM_SPEC, HBM_SPEC, HBM_SPEC],
         out_shape=jax.ShapeDtypeStruct(own.shape, F32),
         scratch_shapes=held + both + [pltpu.SemaphoreType.DMA((2,))],
-        compiler_params=params(),
+        compiler_params=params(WIDE),
         name="step",
     )(info, own, other, high, low)
 
@@ -327,7 +328,7 @@
         in_specs=[SMEM_SPEC, VMEM_SPEC, VMEM_SPEC, HBM_SPEC, HBM_SPEC],
         out_shape=[jax.ShapeDtypeStruct(x, F32) for x in shapes],
         scratch_shapes=held + both + [pltpu.SemaphoreType.DMA((2,))],
-        compiler_params=params(),
+        compiler_params=params(WIDE),
         name="last",
     )(info, own, other, high, low)
 
@@ -409,11 +410,13 @@
 
 def ring(block, length):
     half = length // 2
-    up = [(2 * i, 2 * ((i + 1) % length)) for i in range(length)]
-    down = [(2 * i + 1, 2 * ((i - 1) % length) + 1) for i in range(length)]
     blocks = [block]
-    for s in range(half):
-        blocks.append(lax.ppermute(blocks[-1], ("z", "core"), up + down if s < half - 1 else down))
+    for s in range(1, half, 2):
+        for far in (2, 1):
+            up = [(2 * i, 2 * ((i + far) % length)) for i in range(length)]
+            down = [(2 * i + 1, 2 * ((i - far) % length) + 1) for i in range(length)]
+            pairs = up + down if s + far - 1 < half else down
+            blocks.insert(s, lax.ppermute(blocks[s - 1], ("z", "core"), pairs))
     return blocks
 
 

time: 276 us -> 280 us (1.014)
  Pallas kernels: 44.9 us -> 50.5 us
  starting transfers between devices: 91.1 us -> 87.4 us
    ppermute x16, starting transfers between devices: 65 us -> 60.5 us  [ring(): blocks.insert(s, lax.ppermute(blocks[s - 1], ('z', 'core'), pairs))]
    pallas_call x1, Pallas kernels: 12.3 us -> 15.6 us  [step(): pl.pallas_call(functools.partial(step_kernel, scale), in_specs=[SMEM_SPEC...]
    ppermute x16, waiting for transfers between devices: 3.38 us -> 6.23 us  [ring(): blocks.insert(s, lax.ppermute(blocks[s - 1], ('z', 'core'), pairs))]
    unnamed x14 -> x20, local copies, waits for them, and re-layouts: 6.73 us -> 5.41 us
  transfers between devices with their start and end apart: 22 -> 22, of which waited for: 5 -> 7; matrix products, arithmetic and copies ran while one was open for 0% -> 0% of each run, Pallas kernels for 0% -> 0%
where the time goes in v4:
time: 280 us; the launch traced here: 279 us
  blocking collectives  120 us (43%)
  starting transfers between devices  87.4 us (31%)
  Pallas kernels  50.5 us (18%)
  waiting for transfers between devices  12.3 us (4%)
  local copies, waits for them, and re-layouts  7.14 us (3%)
    all_to_all x7, blocking collectives, exchange(): return lax.all_to_all(chunks, axis, 0, 0)  120 us
    ppermute x16, starting transfers between devices, ring(): blocks.insert(s, lax.ppermute(blocks[s - 1], ('z', 'core'), pairs))  60.5 us
    ppermute x6, starting transfers between devices, swap_cores(): return lax.ppermute(block, 'core', [(0, 1), (1, 0)])  26.9 us
    pallas_call x1, Pallas kernels, step(): pl.pallas_call(functools.partial(step_kernel, scale), in_specs=[SMEM_SPEC...  15.6 us
    pallas_call x1, Pallas kernels, last(): pl.pallas_call(functools.partial(last_kernel, scale), in_specs=[SMEM_SPEC...  14.8 us
    pallas_call x1, Pallas kernels, first(): pl.pallas_call(functools.partial(first_kernel, scale), in_specs=[SMEM_SPE...  12.2 us
    ppermute x16, waiting for transfers between devices, ring(): blocks.insert(s, lax.ppermute(blocks[s - 1], ('z', 'core'), pairs))  6.23 us
    ppermute x6, waiting for transfers between devices, swap_cores(): return lax.ppermute(block, 'core', [(0, 1), (1, 0)])  6.05 us
  transfers between devices with their start and end apart: 22, of which 7 were waited for; matrix products, arithmetic and copies ran while one was open for 0% of the time, Pallas kernels for 0%

profile of v4, /device:TPU:1, one launch (start us, length us, event | category | flops | bytes accessed | tf_op | source)
XLA Modules:
  0.0 279.2 jit_solution(4736037311658083716)
XLA Ops:
  0.6 5.0 %start.1 = f32[16,328,128]{2,1,0:T(8,128)} custom-call(bf16[128,5120]{1,0:T(8,128)(2,1)} %bitcast.76, bf16[128,5120]{1,0:T(8,128)(2,1)} %bitcast.78, f32[64,5120]{1,0:T(8,128)} %q_start.1), custom_call_target="tpu_custom_call" | custom-call | tf_op jit(solution)/shard_map/start/pallas_call | solution.py:77
  5.6 39.2 %all_to_all.35 = f32[16,328,128]{2,1,0:T(8,128)S(1)} all-to-all(f32[16,328,128]{2,1,0:T(8,128)} %start.1), channel_id=1, replica_groups=mesh['rep'=16,'z'=16,'core'=2] {'rep'}, dimensions={0} | all-to-all | bytes 5373952 | tf_op jit(solution)/shard_map/all_to_all | solution.py:400
  44.9 6.0 %collective-permute-start.1 = (f32[328,128]{1,0:T(8,128)S(1)}, f32[328,128]{1,0:T(8,128)S(1)}, u32[]{:S(2)}, u32[]{:S(2)}) collective-permute-start(f32[328,128]{1,0:T(8,128)S(1)} %reduce_sum.27), channel_id=1, source_target_pairs={{0,1},{1,0},{2,3},{3,2},{4,5},{5,4},{6,7},{7,6},{8,9},{9,8},{10,11... | collective-permute-start | bytes 503816 | tf_op jit(solution)/shard_map/ppermute | solution.py:408
  50.9 11.9 %collective-permute-start.3 = (f32[328,128]{1,0:T(8,128)S(1)}, f32[328,128]{1,0:T(8,128)S(1)}, u32[]{:S(2)}, u32[]{:S(2)}) collective-permute-start(f32[328,128]{1,0:T(8,128)S(1)} %reduce_sum.27), channel_id=1, source_target_pairs={{0,4},{2,6},{4,8},{6,10},{8,12},{10,14},{12,16},{14,18},{16,20},{1... | collective-permute-start | bytes 503816 | tf_op jit(solution)/shard_map/ppermute | solution.py:419
  62.9 3.1 %collective-permute-start.4 = (f32[328,128]{1,0:T(8,128)S(1)}, f32[328,128]{1,0:T(8,128)S(1)}, u32[]{:S(2)}, u32[]{:S(2)}) collective-permute-start(f32[328,128]{1,0:T(8,128)S(1)} %collective-permute-done.1), channel_id=1, source_target_pairs={{0,4},{2,6},{4,8},{6,10},{8,12},{10,14},{12,16},{14,18},{16,20},{1... | collective-permute-start | bytes 503816 | tf_op jit(solution)/shard_map/ppermute | solution.py:419
  66.9 6.0 %collective-permute-start.7 = (f32[328,128]{1,0:T(8,128)S(1)}, f32[328,128]{1,0:T(8,128)S(1)}, u32[]{:S(2)}, u32[]{:S(2)}) collective-permute-start(f32[328,128]{1,0:T(8,128)S(1)} %collective-permute-done.3), channel_id=1, source_target_pairs={{0,4},{2,6},{4,8},{6,10},{8,12},{10,14},{12,16},{14,18},{16,20},{1... | collective-permute-start | bytes 503816 | tf_op jit(solution)/shard_map/ppermute | solution.py:419
  73.0 3.6 %collective-permute-start.8 = (f32[328,128]{1,0:T(8,128)S(1)}, f32[328,128]{1,0:T(8,128)S(1)}, u32[]{:S(2)}, u32[]{:S(2)}) collective-permute-start(f32[328,128]{1,0:T(8,128)S(1)} %collective-permute-done.4), channel_id=1, source_target_pairs={{0,4},{2,6},{4,8},{6,10},{8,12},{10,14},{12,16},{14,18},{16,20},{1... | collective-permute-start | bytes 503816 | tf_op jit(solution)/shard_map/ppermute | solution.py:419
  78.1 5.9 %collective-permute-start.11 = (f32[328,128]{1,0:T(8,128)S(1)}, f32[328,128]{1,0:T(8,128)S(1)}, u32[]{:S(2)}, u32[]{:S(2)}) collective-permute-start(f32[328,128]{1,0:T(8,128)S(1)} %collective-permute-done.7), channel_id=1, source_target_pairs={{0,4},{2,6},{4,8},{6,10},{8,12},{10,14},{12,16},{14,18},{16,20},{1... | collective-permute-start | bytes 503816 | tf_op jit(solution)/shard_map/ppermute | solution.py:419
  85.9 2.2 collective-permute-start.5
  88.1 3.2 %collective-permute-start.9 = (f32[328,128]{1,0:T(8,128)S(1)}, f32[328,128]{1,0:T(8,128)S(1)}, u32[]{:S(2)}, u32[]{:S(2)}) collective-permute-start(f32[328,128]{1,0:T(8,128)S(1)} %collective-permute-done.7), channel_id=1, source_target_pairs={{0,2},{2,4},{4,6},{6,8},{8,10},{10,12},{12,14},{14,16},{16,18},{18... | collective-permute-start | bytes 503816 | tf_op jit(solution)/shard_map/ppermute | solution.py:419
  91.4 3.0 %collective-permute-start.12 = (f32[328,128]{1,0:T(8,128)S(1)}, f32[328,128]{1,0:T(8,128)S(1)}, u32[]{:S(2)}, u32[]{:S(2)}) collective-permute-start(f32[328,128]{1,0:T(8,128)S(1)} %collective-permute-done.8), channel_id=1, source_target_pairs={{0,4},{2,6},{4,8},{6,10},{8,12},{10,14},{12,16},{14,18},{16,20},{1... | collective-permute-start | bytes 503816 | tf_op jit(solution)/shard_map/ppermute | solution.py:419
  94.4 2.3 collective-permute-start.13
  96.7 3.5 %collective-permute-start.15 = (f32[328,128]{1,0:T(8,128)S(1)}, f32[328,128]{1,0:T(8,128)S(1)}, u32[]{:S(2)}, u32[]{:S(2)}) collective-permute-start(f32[328,128]{1,0:T(8,128)S(1)} %collective-permute-done.11), channel_id=1, source_target_pairs={{1,29},{3,31},{5,1},{7,3},{9,5},{11,7},{13,9},{15,11},{17,13},{19,... | collective-permute-start | bytes 503816 | tf_op jit(solution)/shard_map/ppermute | solution.py:419
  102.2 2.5 collective-permute-start.6
  106.6 2.4 collective-permute-start.14
  109.1 5.1 %collective-permute-start.16 = (f32[328,128]{1,0:T(8,128)S(1)}, f32[328,128]{1,0:T(8,128)S(1)}, u32[]{:S(2)}, u32[]{:S(2)}) collective-permute-start(f32[328,128]{1,0:T(8,128)S(1)} %collective-permute-done.12), channel_id=1, source_target_pairs={{1,29},{3,31},{5,1},{7,3},{9,5},{11,7},{13,9},{15,11},{17,13},{19,... | collective-permute-start | bytes 503816 | tf_op jit(solution)/shard_map/ppermute | solution.py:419
  114.3 3.7 %collective-permute-done.16 = f32[328,128]{1,0:T(8,128)S(1)} collective-permute-done((f32[328,128]{1,0:T(8,128)S(1)}, f32[328,128]{1,0:T(8,128)S(1)}, u32[]{:S(2)}, u32[]{:S(2)}) %collective-permute-start.16) | collective-permute-done | bytes 167968 | tf_op jit(solution)/shard_map/ppermute | solution.py:419
  118.6 2.3 collective-permute-start.18
  121.0 13.1 %all_to_all.36 = f32[16,64,128]{2,1,0:T(8,128)S(1)} all-to-all(f32[16,64,128]{2,1,0:T(8,128)S(1)} %broadcast_in_dim.15), channel_id=1, replica_groups=mesh['rep'=16,'z'=16,'core'=2] {'rep'}, dimensions={0} | all-to-all | bytes 1048576 | tf_op jit(solution)/shard_map/all_to_all | solution.py:400
  134.7 4.2 %collective-permute-start.17 = (f32[16,64,128]{2,1,0:T(8,128)S(1)}, f32[16,64,128]{2,1,0:T(8,128)}, u32[]{:S(2)}, u32[]{:S(2)}) collective-permute-start(f32[16,64,128]{2,1,0:T(8,128)S(1)} %bitcast.80), channel_id=1, source_target_pairs={{0,1},{1,0},{2,3},{3,2},{4,5},{5,4},{6,7},{7,6},{8,9},{9,8},{10,11... | collective-permute-start | bytes 1572872 | tf_op jit(solution)/shard_map/ppermute | solution.py:408
  140.6 12.2 %first.1 = (f32[16,64,128]{2,1,0:T(8,128)S(1)}, bf16[320,4096]{1,0:T(8,128)(2,1)S(1)}, bf16[320,4096]{1,0:T(8,128)(2,1)S(1)}) custom-call(s32[2]{0:T(128)S(1)} %pad_add_fusion.info, f32[16,64,128]{2,1,0:T(8,128)S(1)} %bitcast.81, f32[16,64,128]{2,1,0:T(8,128)} %collective-permute-done.17.other, f32[8,2,320,128]{3,2,1,0:T(8,128)S(1)} %slice.9.total, ...), custom_call_target="tpu_custom_call" | custom-call | tf_op jit(solution)/shard_map/first/pallas_call | solution.py:298
  155.8 13.3 %all_to_all.37 = f32[16,64,128]{2,1,0:T(8,128)S(1)} all-to-all(f32[16,64,128]{2,1,0:T(8,128)S(1)} %get-tuple-element.9), channel_id=1, replica_groups=mesh['rep'=16,'z'=16,'core'=2] {'rep'}, dimensions={0} | all-to-all | bytes 1048576 | tf_op jit(solution)/shard_map/all_to_all | solution.py:400
  169.2 12.7 %all_to_all.38.own = f32[16,64,128]{2,1,0:T(8,128)S(1)} all-to-all(f32[16,64,128]{2,1,0:T(8,128)S(1)} %broadcast_in_dim.32), channel_id=1, replica_groups=mesh['rep'=16,'z'=16,'core'=2] {'rep'}, dimensions={0} | all-to-all | bytes 1048576 | tf_op jit(solution)/shard_map/all_to_all | solution.py:400
  181.9 5.2 %collective-permute-start.19 = (f32[16,64,128]{2,1,0:T(8,128)S(1)}, f32[16,64,128]{2,1,0:T(8,128)S(1)}, u32[]{:S(2)}, u32[]{:S(2)}) collective-permute-start(f32[16,64,128]{2,1,0:T(8,128)S(1)} %all_to_all.38.own), channel_id=1, source_target_pairs={{0,1},{1,0},{2,3},{3,2},{4,5},{5,4},{6,7},{7,6},{8,9},{9,8},{10,11... | collective-permute-start | bytes 1572872 | tf_op jit(solution)/shard_map/ppermute | solution.py:408
  189.4 15.6 %step.1 = f32[16,64,128]{2,1,0:T(8,128)} custom-call(s32[2]{0:T(128)} %copy-done.5, f32[16,64,128]{2,1,0:T(8,128)} %copy-done.7, f32[16,64,128]{2,1,0:T(8,128)} %copy-done.9, bf16[320,4096]{1,0:T(8,128)(2,1)} %copy-done, bf16[320,4096]{1,0:T(8,128)(2,1)} %copy-done.1), custom_call_target="tpu_custom_call" | custom-call | tf_op jit(solution)/shard_map/step/pallas_call | solution.py:312
  205.0 13.8 %all_to_all.39 = f32[16,64,128]{2,1,0:T(8,128)S(1)} all-to-all(f32[16,64,128]{2,1,0:T(8,128)} %step.1), channel_id=1, replica_groups=mesh['rep'=16,'z'=16,'core'=2] {'rep'}, dimensions={0} | all-to-all | bytes 1048576 | tf_op jit(solution)/shard_map/all_to_all | solution.py:400
  218.9 12.9 %all_to_all.40.own = f32[16,64,128]{2,1,0:T(8,128)S(1)} all-to-all(f32[16,64,128]{2,1,0:T(8,128)S(1)} %broadcast_in_dim.33), channel_id=1, replica_groups=mesh['rep'=16,'z'=16,'core'=2] {'rep'}, dimensions={0} | all-to-all | bytes 1048576 | tf_op jit(solution)/shard_map/all_to_all | solution.py:400
  231.8 5.6 %collective-permute-start.20 = (f32[16,64,128]{2,1,0:T(8,128)S(1)}, f32[16,64,128]{2,1,0:T(8,128)S(1)}, u32[]{:S(2)}, u32[]{:S(2)}) collective-permute-start(f32[16,64,128]{2,1,0:T(8,128)S(1)} %all_to_all.40.own), channel_id=1, source_target_pairs={{0,1},{1,0},{2,3},{3,2},{4,5},{5,4},{6,7},{7,6},{8,9},{9,8},{10,11... | collective-permute-start | bytes 1572872 | tf_op jit(solution)/shard_map/ppermute | solution.py:408
  239.5 14.8 %last.1 = (f32[2,80,128]{2,1,0:T(8,128)}, f32[64,128]{1,0:T(8,128)}) custom-call(s32[2]{0:T(128)} %copy-done.5, f32[16,64,128]{2,1,0:T(8,128)} %copy-done.6, f32[16,64,128]{2,1,0:T(8,128)} %copy-done.8, bf16[320,4096]{1,0:T(8,128)(2,1)} %copy-done, bf16[320,4096]{1,0:T(8,128)(2,1)} %copy-done.1), custom_call_target="tpu_custom_call" | custom-call | tf_op jit(solution)/shard_map/last/pallas_call | solution.py:326
  255.1 15.0 %all_to_all.41.own = f32[16,80,128]{2,1,0:T(8,128)S(1)} all-to-all(f32[16,80,128]{2,1,0:T(8,128)S(1)} %broadcast_in_dim.35), channel_id=1, replica_groups=mesh['rep'=16,'z'=16,'core'=2] {'rep'}, dimensions={0} | all-to-all | bytes 1310720 | tf_op jit(solution)/shard_map/all_to_all | solution.py:400
  270.1 3.6 %collective-permute-start.21 = (f32[16,80,128]{2,1,0:T(8,128)S(1)}, f32[16,80,128]{2,1,0:T(8,128)S(1)}, u32[]{:S(2)}, u32[]{:S(2)}) collective-permute-start(f32[16,80,128]{2,1,0:T(8,128)S(1)} %all_to_all.41.own), channel_id=1, source_target_pairs={{0,1},{1,0},{2,3},{3,2},{4,5},{5,4},{6,7},{7,6},{8,9},{9,8},{10,11... | collective-permute-start | bytes 1966088 | tf_op jit(solution)/shard_map/ppermute | solution.py:408
  276.2 3.0 %finish.1 = (bf16[128,5120]{1,0:T(8,128)(2,1)}, f32[64,5120]{1,0:T(8,128)}) custom-call(s32[1]{0:T(128)} %bitcast.flag, bf16[128,5120]{1,0:T(8,128)(2,1)S(1)} %bitcast.77, bf16[128,5120]{1,0:T(8,128)(2,1)S(1)} %bitcast.79, f32[16,80,128]{2,1,0:T(8,128)S(1)} %all_to_all.41.own, f32[16,80,128]{2,1,0:T(8,128)S(1)} %collective-permute-done.21.other, ...), custom_call_target="tpu_custom_call" | custom-call | tf_op jit(solution)/shard_map/finish/pallas_call | solution.py:388
  (68 shorter events, 22.2 us)
Async XLA Ops:
  44.9 17.9 %collective-permute-start.1 = (f32[328,128]{1,0:T(8,128)S(1)}, f32[328,128]{1,0:T(8,128)S(1)}, u32[]{:S(2)}, u32[]{:S(2)}) collective-permute-start(f32[328,128]{1,0:T(8,128)S(1)} %reduce_sum.27), channel_id=1, source_target_pairs={{0,1},{1,0},{2,3},{3,2},{4,5},{5,4},{6,7},{7,6},{8,9},{9,8},{10,11... | collective-permute-start | bytes 503816 | tf_op jit(solution)/shard_map/ppermute | solution.py:408
  50.9 16.0 %collective-permute-start.3 = (f32[328,128]{1,0:T(8,128)S(1)}, f32[328,128]{1,0:T(8,128)S(1)}, u32[]{:S(2)}, u32[]{:S(2)}) collective-permute-start(f32[328,128]{1,0:T(8,128)S(1)} %reduce_sum.27), channel_id=1, source_target_pairs={{0,4},{2,6},{4,8},{6,10},{8,12},{10,14},{12,16},{14,18},{16,20},{1... | collective-permute-start | bytes 503816 | tf_op jit(solution)/shard_map/ppermute | solution.py:419
  62.9 10.1 %collective-permute-start.4 = (f32[328,128]{1,0:T(8,128)S(1)}, f32[328,128]{1,0:T(8,128)S(1)}, u32[]{:S(2)}, u32[]{:S(2)}) collective-permute-start(f32[328,128]{1,0:T(8,128)S(1)} %collective-permute-done.1), channel_id=1, source_target_pairs={{0,4},{2,6},{4,8},{6,10},{8,12},{10,14},{12,16},{14,18},{16,20},{1... | collective-permute-start | bytes 503816 | tf_op jit(solution)/shard_map/ppermute | solution.py:419
  66.9 11.2 %collective-permute-start.7 = (f32[328,128]{1,0:T(8,128)S(1)}, f32[328,128]{1,0:T(8,128)S(1)}, u32[]{:S(2)}, u32[]{:S(2)}) collective-permute-start(f32[328,128]{1,0:T(8,128)S(1)} %collective-permute-done.3), channel_id=1, source_target_pairs={{0,4},{2,6},{4,8},{6,10},{8,12},{10,14},{12,16},{14,18},{16,20},{1... | collective-permute-start | bytes 503816 | tf_op jit(solution)/shard_map/ppermute | solution.py:419
  73.0 18.4 %collective-permute-start.8 = (f32[328,128]{1,0:T(8,128)S(1)}, f32[328,128]{1,0:T(8,128)S(1)}, u32[]{:S(2)}, u32[]{:S(2)}) collective-permute-start(f32[328,128]{1,0:T(8,128)S(1)} %collective-permute-done.4), channel_id=1, source_target_pairs={{0,4},{2,6},{4,8},{6,10},{8,12},{10,14},{12,16},{14,18},{16,20},{1... | collective-permute-start | bytes 503816 | tf_op jit(solution)/shard_map/ppermute | solution.py:419
  78.1 16.3 %collective-permute-start.11 = (f32[328,128]{1,0:T(8,128)S(1)}, f32[328,128]{1,0:T(8,128)S(1)}, u32[]{:S(2)}, u32[]{:S(2)}) collective-permute-start(f32[328,128]{1,0:T(8,128)S(1)} %collective-permute-done.7), channel_id=1, source_target_pairs={{0,4},{2,6},{4,8},{6,10},{8,12},{10,14},{12,16},{14,18},{16,20},{1... | collective-permute-start | bytes 503816 | tf_op jit(solution)/shard_map/ppermute | solution.py:419
  84.0 12.7 %collective-permute-start = (f32[328,128]{1,0:T(8,128)S(1)}, f32[328,128]{1,0:T(8,128)S(1)}, u32[]{:S(2)}, u32[]{:S(2)}) collective-permute-start(f32[328,128]{1,0:T(8,128)S(1)} %reduce_sum.27), channel_id=1, source_target_pairs={{0,2},{2,4},{4,6},{6,8},{8,10},{10,12},{12,14},{14,16},{16,18},{18... | collective-permute-start | bytes 503816 | tf_op jit(solution)/shard_map/ppermute | solution.py:419
  85.9 14.3 %collective-permute-start.5 = (f32[328,128]{1,0:T(8,128)S(1)}, f32[328,128]{1,0:T(8,128)S(1)}, u32[]{:S(2)}, u32[]{:S(2)}) collective-permute-start(f32[328,128]{1,0:T(8,128)S(1)} %collective-permute-done.3), channel_id=1, source_target_pairs={{0,2},{2,4},{4,6},{6,8},{8,10},{10,12},{12,14},{14,16},{16,18},{18... | collective-permute-start | bytes 503816 | tf_op jit(solution)/shard_map/ppermute | solution.py:419
  88.1 14.0 %collective-permute-start.9 = (f32[328,128]{1,0:T(8,128)S(1)}, f32[328,128]{1,0:T(8,128)S(1)}, u32[]{:S(2)}, u32[]{:S(2)}) collective-permute-start(f32[328,128]{1,0:T(8,128)S(1)} %collective-permute-done.7), channel_id=1, source_target_pairs={{0,2},{2,4},{4,6},{6,8},{8,10},{10,12},{12,14},{14,16},{16,18},{18... | collective-permute-start | bytes 503816 | tf_op jit(solution)/shard_map/ppermute | solution.py:419
  91.4 13.3 %collective-permute-start.12 = (f32[328,128]{1,0:T(8,128)S(1)}, f32[328,128]{1,0:T(8,128)S(1)}, u32[]{:S(2)}, u32[]{:S(2)}) collective-permute-start(f32[328,128]{1,0:T(8,128)S(1)} %collective-permute-done.8), channel_id=1, source_target_pairs={{0,4},{2,6},{4,8},{6,10},{8,12},{10,14},{12,16},{14,18},{16,20},{1... | collective-permute-start | bytes 503816 | tf_op jit(solution)/shard_map/ppermute | solution.py:419
  94.4 12.3 %collective-permute-start.13 = (f32[328,128]{1,0:T(8,128)S(1)}, f32[328,128]{1,0:T(8,128)S(1)}, u32[]{:S(2)}, u32[]{:S(2)}) collective-permute-start(f32[328,128]{1,0:T(8,128)S(1)} %collective-permute-done.11), channel_id=1, source_target_pairs={{0,2},{2,4},{4,6},{6,8},{8,10},{10,12},{12,14},{14,16},{16,18},{18... | collective-permute-start | bytes 503816 | tf_op jit(solution)/shard_map/ppermute | solution.py:419
  96.7 12.4 %collective-permute-start.15 = (f32[328,128]{1,0:T(8,128)S(1)}, f32[328,128]{1,0:T(8,128)S(1)}, u32[]{:S(2)}, u32[]{:S(2)}) collective-permute-start(f32[328,128]{1,0:T(8,128)S(1)} %collective-permute-done.11), channel_id=1, source_target_pairs={{1,29},{3,31},{5,1},{7,3},{9,5},{11,7},{13,9},{15,11},{17,13},{19,... | collective-permute-start | bytes 503816 | tf_op jit(solution)/shard_map/ppermute | solution.py:419
  100.2 14.1 %collective-permute-start.2 = (f32[328,128]{1,0:T(8,128)S(1)}, f32[328,128]{1,0:T(8,128)S(1)}, u32[]{:S(2)}, u32[]{:S(2)}) collective-permute-start(f32[328,128]{1,0:T(8,128)S(1)} %collective-permute-done.1), channel_id=1, source_target_pairs={{0,2},{2,4},{4,6},{6,8},{8,10},{10,12},{12,14},{14,16},{16,18},{18... | collective-permute-start | bytes 503816 | tf_op jit(solution)/shard_map/ppermute | solution.py:419
  102.2 12.2 %collective-permute-start.6 = (f32[328,128]{1,0:T(8,128)S(1)}, f32[328,128]{1,0:T(8,128)S(1)}, u32[]{:S(2)}, u32[]{:S(2)}) collective-permute-start(f32[328,128]{1,0:T(8,128)S(1)} %collective-permute-done.4), channel_id=1, source_target_pairs={{0,2},{2,4},{4,6},{6,8},{8,10},{10,12},{12,14},{14,16},{16,18},{18... | collective-permute-start | bytes 503816 | tf_op jit(solution)/shard_map/ppermute | solution.py:419
  104.7 9.6 %collective-permute-start.10 = (f32[328,128]{1,0:T(8,128)S(1)}, f32[328,128]{1,0:T(8,128)S(1)}, u32[]{:S(2)}, u32[]{:S(2)}) collective-permute-start(f32[328,128]{1,0:T(8,128)S(1)} %collective-permute-done.8), channel_id=1, source_target_pairs={{0,2},{2,4},{4,6},{6,8},{8,10},{10,12},{12,14},{14,16},{16,18},{18... | collective-permute-start | bytes 503816 | tf_op jit(solution)/shard_map/ppermute | solution.py:419
  106.6 7.7 %collective-permute-start.14 = (f32[328,128]{1,0:T(8,128)S(1)}, f32[328,128]{1,0:T(8,128)S(1)}, u32[]{:S(2)}, u32[]{:S(2)}) collective-permute-start(f32[328,128]{1,0:T(8,128)S(1)} %collective-permute-done.12), channel_id=1, source_target_pairs={{0,2},{2,4},{4,6},{6,8},{8,10},{10,12},{12,14},{14,16},{16,18},{18... | collective-permute-start | bytes 503816 | tf_op jit(solution)/shard_map/ppermute | solution.py:419
  109.1 8.9 %collective-permute-start.16 = (f32[328,128]{1,0:T(8,128)S(1)}, f32[328,128]{1,0:T(8,128)S(1)}, u32[]{:S(2)}, u32[]{:S(2)}) collective-permute-start(f32[328,128]{1,0:T(8,128)S(1)} %collective-permute-done.12), channel_id=1, source_target_pairs={{1,29},{3,31},{5,1},{7,3},{9,5},{11,7},{13,9},{15,11},{17,13},{19,... | collective-permute-start | bytes 503816 | tf_op jit(solution)/shard_map/ppermute | solution.py:419
  118.6 21.9 %collective-permute-start.18 = (f32[8,2,320,128]{3,2,1,0:T(8,128)S(1)}, f32[8,2,320,128]{3,2,1,0:T(8,128)}, u32[]{:S(2)}, u32[]{:S(2)}) collective-permute-start(f32[8,2,320,128]{3,2,1,0:T(8,128)S(1)} %slice.9.total), channel_id=1, source_target_pairs={{0,1},{1,0},{2,3},{3,2},{4,5},{5,4},{6,7},{7,6},{8,9},{9,8},{10,11... | collective-permute-start | bytes 7864328 | tf_op jit(solution)/shard_map/ppermute | solution.py:408
  134.7 5.9 %collective-permute-start.17 = (f32[16,64,128]{2,1,0:T(8,128)S(1)}, f32[16,64,128]{2,1,0:T(8,128)}, u32[]{:S(2)}, u32[]{:S(2)}) collective-permute-start(f32[16,64,128]{2,1,0:T(8,128)S(1)} %bitcast.80), channel_id=1, source_target_pairs={{0,1},{1,0},{2,3},{3,2},{4,5},{5,4},{6,7},{7,6},{8,9},{9,8},{10,11... | collective-permute-start | bytes 1572872 | tf_op jit(solution)/shard_map/ppermute | solution.py:408
  139.0 13.7 %copy-start.5 = (s32[2]{0:T(128)}, s32[2]{0:T(128)S(1)}, u32[]{:S(2)}) copy-start(s32[2]{0:T(128)S(1)} %pad_add_fusion.info) | copy-start | bytes 28
  152.8 1.5 copy-start
  154.3 1.5 copy-start.1
  181.9 6.7 %copy-start.7 = (f32[16,64,128]{2,1,0:T(8,128)}, f32[16,64,128]{2,1,0:T(8,128)S(1)}, u32[]{:S(2)}) copy-start(f32[16,64,128]{2,1,0:T(8,128)S(1)} %all_to_all.38.own) | copy-start | bytes 1572868
  181.9 6.7 %collective-permute-start.19 = (f32[16,64,128]{2,1,0:T(8,128)S(1)}, f32[16,64,128]{2,1,0:T(8,128)S(1)}, u32[]{:S(2)}, u32[]{:S(2)}) collective-permute-start(f32[16,64,128]{2,1,0:T(8,128)S(1)} %all_to_all.38.own), channel_id=1, source_target_pairs={{0,1},{1,0},{2,3},{3,2},{4,5},{5,4},{6,7},{7,6},{8,9},{9,8},{10,11... | collective-permute-start | bytes 1572872 | tf_op jit(solution)/shard_map/ppermute | solution.py:408
  188.6 0.8 copy-start.9
  231.8 6.9 %copy-start.6 = (f32[16,64,128]{2,1,0:T(8,128)}, f32[16,64,128]{2,1,0:T(8,128)S(1)}, u32[]{:S(2)}) copy-start(f32[16,64,128]{2,1,0:T(8,128)S(1)} %all_to_all.40.own) | copy-start | bytes 1572868
  231.8 6.9 %collective-permute-start.20 = (f32[16,64,128]{2,1,0:T(8,128)S(1)}, f32[16,64,128]{2,1,0:T(8,128)S(1)}, u32[]{:S(2)}, u32[]{:S(2)}) collective-permute-start(f32[16,64,128]{2,1,0:T(8,128)S(1)} %all_to_all.40.own), channel_id=1, source_target_pairs={{0,1},{1,0},{2,3},{3,2},{4,5},{5,4},{6,7},{7,6},{8,9},{9,8},{10,11... | collective-permute-start | bytes 1572872 | tf_op jit(solution)/shard_map/ppermute | solution.py:408
  237.4 38.0 %copy-start.2 = (bf16[1,128,5120]{2,1,0:T(8,128)(2,1)S(1)}, bf16[1,128,5120]{2,1,0:T(8,128)(2,1)}, u32[]{:S(2)}) copy-start(bf16[1,128,5120]{2,1,0:T(8,128)(2,1)} %param.3) | copy-start | bytes 3932164
  237.4 38.0 %copy-start.3 = (bf16[1,128,5120]{2,1,0:T(8,128)(2,1)S(1)}, bf16[1,128,5120]{2,1,0:T(8,128)(2,1)}, u32[]{:S(2)}) copy-start(bf16[1,128,5120]{2,1,0:T(8,128)(2,1)} %param.4) | copy-start | bytes 3932164
  238.7 0.8 copy-start.8
  270.1 5.3 %collective-permute-start.21 = (f32[16,80,128]{2,1,0:T(8,128)S(1)}, f32[16,80,128]{2,1,0:T(8,128)S(1)}, u32[]{:S(2)}, u32[]{:S(2)}) collective-permute-start(f32[16,80,128]{2,1,0:T(8,128)S(1)} %all_to_all.41.own), channel_id=1, source_target_pairs={{0,1},{1,0},{2,3},{3,2},{4,5},{5,4},{6,7},{7,6},{8,9},{9,8},{10,11... | collective-permute-start | bytes 1966088 | tf_op jit(solution)/shard_map/ppermute | solution.py:408
  275.4 0.8 copy-start.4

commit v5 on v2

--- a/solution.py
+++ b/solution.py
@@ -191,17 +191,22 @@
     return at
 
 
+def whiten(held):
+    rank = held.shape[0] // 4
+    left = weights(inverse_factor(gram_of(held, CHUNK)))
+    for at in range(0, held.shape[1], CHUNK):
+        y = dot(left, held[:, at : at + CHUNK], NN)
+        put(held, at, y[:rank] + (y[rank : 2 * rank] + y[2 * rank :]))
+    return inverse_factor(gram_of(held, CHUNK))
+
+
 def orthonormal(info, own, other, held):
     length = own.shape[0]
     for mine, blocks in ((True, own), (False, other)):
         at = planes(info, length, mine)
         for j in range(length // 2):
             put(held, at(j), jnp.concatenate([blocks[2 * j], blocks[2 * j + 1]], axis=1))
-    left = weights(inverse_factor(gram_of(held, CHUNK)))
-    for at in range(0, held.shape[1], CHUNK):
-        y = dot(left, held[:, at : at + CHUNK], NN)
-        put(held, at, y[: y.shape[0] // 3] + (y[y.shape[0] // 3 : 2 * y.shape[0] // 3] + y[2 * y.shape[0] // 3 :]))
-    return inverse_factor(gram_of(held, CHUNK))
+    return whiten(held)
 
 
 def right_factor(scale, second, held, high, low):
@@ -223,8 +228,13 @@
         out[2 * j + 1] = x[:, rows:]
 
 
-def first_kernel(scale, info, own, other, total, total_other, out, high_out, low_out, held, high, low, sems):
-    length = own.shape[0]
+def orth_kernel(info, own, other, rows_out, weights_out, held):
+    weights_out[...] = orthonormal(info, own, other, held)
+    rows_out[...] = held[...]
+
+
+def first_kernel(scale, info, held, second, total, total_other, out, high_out, low_out, high, low, sems):
+    length = out.shape[0]
     for mine, blocks in ((True, total), (False, total_other)):
         at = planes(info, length, mine)
         core = info[1] if mine else 1 - info[1]
@@ -239,8 +249,7 @@
     ]
     for store in stores:
         store.start()
-    second = orthonormal(info, own, other, held)
-    next_left(info, right_factor(scale, second, held, high, low), high, low, out)
+    next_left(info, right_factor(scale, second[...], held, high, low), high, low, out)
     for store in stores:
         store.wait()
 
@@ -289,20 +298,33 @@
     return [pltpu.VMEM((4 * rank, n), BF16)], [pltpu.VMEM((cut, n), BF16)] * 2
 
 
-def first(scale, info, own, other, total, total_other):
+def orth(info, own, other):
     length, rank, rows = own.shape
+    shape = (4 * rank, 2 * length * rows)
+    return pl.pallas_call(
+        orth_kernel,
+        in_specs=[SMEM_SPEC, VMEM_SPEC, VMEM_SPEC],
+        out_shape=[jax.ShapeDtypeStruct(shape, BF16), jax.ShapeDtypeStruct((rank, 2 * rank), F32)],
+        scratch_shapes=[pltpu.VMEM(shape, BF16)],
+        compiler_params=params(),
+        name="orth",
+    )(info, own, other)
+
+
+def first(scale, info, held, second, total, total_other, shape):
+    length, rank, rows = shape
     cut = total.shape[2]
-    held, both = scratch(length, rank, cut)
+    _, both = scratch(length, rank, cut)
     whole = jax.ShapeDtypeStruct((cut, 2 * length * rows), BF16)
     return pl.pallas_call(
         functools.partial(first_kernel, scale),
         in_specs=[SMEM_SPEC] + [VMEM_SPEC] * 4,
         out_specs=[VMEM_SPEC, HBM_SPEC, HBM_SPEC],
-        out_shape=[jax.ShapeDtypeStruct(own.shape, F32), whole, whole],
-        scratch_shapes=held + both + [pltpu.SemaphoreType.DMA((2,))],
+        out_shape=[jax.ShapeDtypeStruct(shape, F32), whole, whole],
+        scratch_shapes=both + [pltpu.SemaphoreType.DMA((2,))],
         compiler_params=params(),
         name="first",
-    )(info, own, other, total, total_other)
+    )(info, held, second, total, total_other)
 
 
 def step(scale, info, own, other, high, low):
@@ -407,14 +429,14 @@
     return lax.ppermute(block, "core", [(0, 1), (1, 0)])
 
 
-def ring(block, length):
-    half = length // 2
-    up = [(2 * i, 2 * ((i + 1) % length)) for i in range(length)]
-    down = [(2 * i + 1, 2 * ((i - 1) % length) + 1) for i in range(length)]
-    blocks = [block]
-    for s in range(half):
-        blocks.append(lax.ppermute(blocks[-1], ("z", "core"), up + down if s < half - 1 else down))
-    return blocks
+def along_ring(block, length, far, both=True):
+    up = [(2 * i, 2 * ((i + far) % length)) for i in range(length)]
+    down = [(2 * i + 1, 2 * ((i - far) % length) + 1) for i in range(length)]
+    return lax.ppermute(block, ("z", "core"), up + down if both else down)
+
+
+def after(x, earlier):
+    return lax.optimization_barrier((x, earlier))[0]
 
 
 def body(grads, errors, q_start):
@@ -424,21 +446,38 @@
     reps, length = lax.axis_size("rep"), lax.axis_size("z")
     core, place = lax.axis_index("core"), lax.axis_index("z")
     cut, extra = width // reps, rank // reps
+    half = length // 2
     scale = 1.0 / reps
     flag = core.reshape(1).astype(jnp.int32)
     info = jnp.stack([place, core]).astype(jnp.int32)
 
     block = jnp.sum(exchange(start(grads, errors, q_start, reps), "rep"), axis=0)
-    streams = ring(block, length), ring(swap_cores(block), length)
-    held = jnp.stack(
-        [jnp.stack([jnp.where(core == 0, x[j], x[j + 1]) for x in streams]) for j in range(length // 2)]
-    )
-    total = held[:, :, :cut]
-    piece = held[:, :, cut : cut + extra]
-    piece = jnp.where(core == 0, piece, piece[:, ::-1]).reshape(length * extra, rows)
-    own = gather(piece, "rep", reps).reshape(reps, length, extra, rows)
-    own = own.transpose(1, 0, 2, 3).reshape(length, rank, rows)
-    partial, high, low = first(scale, info, own, swap_cores(own), total, swap_cores(total))
+    other = swap_cores(block)
+    now = [block[:cut], other[:cut]]
+    pieces = jnp.stack([block[cut : cut + extra], other[cut : cut + extra]])[None]
+    pieces = jnp.where(core == 0, pieces, pieces[:, ::-1])
+    held = []
+    reach = 1
+    for s in range(half):
+        later = [along_ring(x, length, 1, s < half - 1) for x in now]
+        held.append([now, later])
+        if reach < half:
+            pieces = jnp.concatenate([pieces, along_ring(pieces, length, reach)], axis=0)
+            reach *= 2
+            later[0] = after(later[0], pieces)
+        elif reach == half:
+            shifted = along_ring(pieces, length, 1, False)
+            pieces = jnp.where(core == 0, pieces, shifted).reshape(length * extra, rows)
+            reach *= 2
+            later[0] = after(later[0], pieces)
+            own = gather(pieces, "rep", reps).reshape(reps, length, extra, rows)
+            own = own.transpose(1, 0, 2, 3).reshape(length, rank, rows)
+        elif s == half - 2:
+            later[0] = after(later[0], own)
+        now = later
+    total = jnp.stack([jnp.stack([jnp.where(core == 0, x, y) for x, y in zip(*pair)]) for pair in held])
+    rows_of, weight = orth(info, own, swap_cores(own))
+    partial, high, low = first(scale, info, rows_of, weight, total, swap_cores(total), own.shape)
     for turn in range(ITERS - 1):
         own = gather(jnp.sum(exchange(partial, "rep"), axis=0), "rep", reps)
         if turn < ITERS - 2:

time: 276 us -> 296 us (1.072)
  blocking collectives: 120 us -> 70.8 us
  waiting for transfers between devices: 9.6 us -> 47.5 us
  starting transfers between devices: 91.1 us -> 115 us
  Pallas kernels: 44.9 us -> 48.1 us
    all_to_all x7 -> x5, blocking collectives: 120 us -> 70.8 us  [exchange(): return lax.all_to_all(chunks, axis, 0, 0)]
    all_to_all x0 -> x2, waiting for transfers between devices: none -> 31 us  [exchange(): return lax.all_to_all(chunks, axis, 0, 0)]
    all_to_all x0 -> x2, starting transfers between devices: none -> 11.9 us  [exchange(): return lax.all_to_all(chunks, axis, 0, 0)]
    pallas_call x0 -> x1, Pallas kernels: none -> 8.36 us  [orth(): pl.pallas_call(orth_kernel, in_specs=[SMEM_SPEC, VMEM_SPEC, VMEM_SPEC], o...]
    ppermute x16 -> x20, waiting for transfers between devices: 3.38 us -> 10.3 us  [along_ring(): return lax.ppermute(block, ('z', 'core'), up + down if both else down)]
    ppermute x16 -> x20, starting transfers between devices: 65 us -> 71.2 us  [along_ring(): return lax.ppermute(block, ('z', 'core'), up + down if both else down)]
    ppermute x6, starting transfers between devices: 26.1 us -> 31.8 us  [swap_cores(): return lax.ppermute(block, 'core', [(0, 1), (1, 0)])]
    pallas_call x1, Pallas kernels: 12.2 us -> 6.99 us  [first(): pl.pallas_call(functools.partial(first_kernel, scale), in_specs=[SMEM_SPE...]
  transfers between devices with their start and end apart: 22 -> 28, of which waited for: 5 -> 11; matrix products, arithmetic and copies ran while one was open for 0% -> 1% of each run, Pallas kernels for 0% -> 3%
where the time goes in v5:
time: 296 us; the launch traced here: 295 us
  starting transfers between devices  115 us (39%)
  blocking collectives  70.8 us (24%)
  Pallas kernels  48.1 us (16%)
  waiting for transfers between devices  47.5 us (16%)
  local copies, waits for them, and re-layouts  9.8 us (3%)
    ppermute x20, starting transfers between devices, along_ring(): return lax.ppermute(block, ('z', 'core'), up + down if both else down)  71.2 us
    all_to_all x5, blocking collectives, exchange(): return lax.all_to_all(chunks, axis, 0, 0)  70.8 us
    ppermute x6, starting transfers between devices, swap_cores(): return lax.ppermute(block, 'core', [(0, 1), (1, 0)])  31.8 us
    all_to_all x2, waiting for transfers between devices, exchange(): return lax.all_to_all(chunks, axis, 0, 0)  31 us
    pallas_call x1, Pallas kernels, last(): pl.pallas_call(functools.partial(last_kernel, scale), in_specs=[SMEM_SPEC...  12.4 us
    pallas_call x1, Pallas kernels, step(): pl.pallas_call(functools.partial(step_kernel, scale), in_specs=[SMEM_SPEC...  12.3 us
    all_to_all x2, starting transfers between devices, exchange(): return lax.all_to_all(chunks, axis, 0, 0)  11.9 us
    ppermute x20, waiting for transfers between devices, along_ring(): return lax.ppermute(block, ('z', 'core'), up + down if both else down)  10.3 us
  transfers between devices with their start and end apart: 28, of which 11 were waited for; matrix products, arithmetic and copies ran while one was open for 1% of the time, Pallas kernels for 3%

profile of v5, /device:TPU:1, one launch (start us, length us, event | category | flops | bytes accessed | tf_op | source)
XLA Modules:
  0.0 295.1 jit_solution(8001798509248281947)
XLA Ops:
  0.6 5.0 %start.1 = f32[16,328,128]{2,1,0:T(8,128)} custom-call(bf16[128,5120]{1,0:T(8,128)(2,1)} %bitcast.82, bf16[128,5120]{1,0:T(8,128)(2,1)} %bitcast.84, f32[64,5120]{1,0:T(8,128)} %q_start.1), custom_call_target="tpu_custom_call" | custom-call | tf_op jit(solution)/shard_map/start/pallas_call | solution.py:76
  5.6 7.6 %all-to-all-start = ((f32[16,328,128]{2,1,0:T(8,128)}), f32[16,328,128]{2,1,0:T(8,128)S(1)}, u32[]{:S(2)}, u32[]{:S(2)}) async-start(f32[16,328,128]{2,1,0:T(8,128)} %start.1), calls=%async_computation | async-start | bytes 5373952 | tf_op jit(solution)/shard_map/all_to_all | solution.py:421
  13.2 31.0 %all-to-all-done = f32[16,328,128]{2,1,0:T(8,128)S(1)} async-done(((f32[16,328,128]{2,1,0:T(8,128)}), f32[16,328,128]{2,1,0:T(8,128)S(1)}, u32[]{:S(2)}, u32[]{:S(2)}) %all-to-all-start) | async-done | bytes 2687008 | tf_op jit(solution)/shard_map/all_to_all | solution.py:421
  44.4 8.3 %collective-permute-start = (f32[328,128]{1,0:T(8,128)S(1)}, f32[328,128]{1,0:T(8,128)S(1)}, u32[]{:S(2)}, u32[]{:S(2)}) collective-permute-start(f32[328,128]{1,0:T(8,128)S(1)} %reduce_sum.27), channel_id=1, source_target_pairs={{0,1},{1,0},{2,3},{3,2},{4,5},{5,4},{6,7},{7,6},{8,9},{9,8},{10,11... | collective-permute-start | bytes 503816 | tf_op jit(solution)/shard_map/ppermute | solution.py:429
  52.6 12.6 %collective-permute-start.6 = (f32[320,128]{1,0:T(8,128)S(1)}, f32[320,128]{1,0:T(8,128)S(1)}, u32[]{:S(2)}, u32[]{:S(2)}) collective-permute-start(f32[320,128]{1,0:T(8,128)S(1)} %slice.18), channel_id=1, source_target_pairs={{0,2},{2,4},{4,6},{6,8},{8,10},{10,12},{12,14},{14,16},{16,18},{18... | collective-permute-start | bytes 491528 | tf_op jit(solution)/shard_map/ppermute | solution.py:435
  67.9 2.6 collective-permute-start.7
  70.6 2.9 collective-permute-start.8
  73.5 4.1 %collective-permute-start.2 = (f32[2,2,4,128]{3,2,1,0:T(4,128)S(1)}, f32[2,2,4,128]{3,2,1,0:T(4,128)S(1)}, u32[]{:S(2)}, u32[]{:S(2)}) collective-permute-start(f32[2,2,4,128]{3,2,1,0:T(4,128)S(1)} %pad_maximum_fusion.2), channel_id=1, source_target_pairs={{0,4},{2,6},{4,8},{6,10},{8,12},{10,14},{12,16},{14,18},{16,20},{1... | collective-permute-start | bytes 24584 | tf_op jit(solution)/shard_map/ppermute | solution.py:435
  78.8 4.8 %collective-permute-start.9 = (f32[320,128]{1,0:T(8,128)S(1)}, f32[320,128]{1,0:T(8,128)S(1)}, u32[]{:S(2)}, u32[]{:S(2)}) collective-permute-start(f32[320,128]{1,0:T(8,128)S(1)} %collective-permute-done.7), channel_id=1, source_target_pairs={{0,2},{2,4},{4,6},{6,8},{8,10},{10,12},{12,14},{14,16},{16,18},{18... | collective-permute-start | bytes 491528 | tf_op jit(solution)/shard_map/ppermute | solution.py:435
  86.3 3.0 %collective-permute-start.3 = (f32[4,2,4,128]{3,2,1,0:T(4,128)S(1)}, f32[4,2,4,128]{3,2,1,0:T(4,128)S(1)}, u32[]{:S(2)}, u32[]{:S(2)}) collective-permute-start(f32[4,2,4,128]{3,2,1,0:T(4,128)S(1)} %pad_maximum_fusion.1), channel_id=1, source_target_pairs={{0,8},{2,10},{4,12},{6,14},{8,16},{10,18},{12,20},{14,22},{16,24},... | collective-permute-start | bytes 49160 | tf_op jit(solution)/shard_map/ppermute | solution.py:435
  89.3 5.3 %collective-permute-done.3 = f32[4,2,4,128]{3,2,1,0:T(4,128)S(1)} collective-permute-done((f32[4,2,4,128]{3,2,1,0:T(4,128)S(1)}, f32[4,2,4,128]{3,2,1,0:T(4,128)S(1)}, u32[]{:S(2)}, u32[]{:S(2)}) %collective-permute-start.3) | collective-permute-done | bytes 16416 | tf_op jit(solution)/shard_map/ppermute | solution.py:435
  96.6 2.7 collective-permute-start.11
  99.3 2.8 collective-permute-start.12
  103.0 4.3 %all-to-all-start.1 = ((f32[16,64,128]{2,1,0:T(8,128)}), f32[16,64,128]{2,1,0:T(8,128)S(1)}, u32[]{:S(2)}, u32[]{:S(2)}) async-start(f32[16,64,128]{2,1,0:T(8,128)} %broadcast_in_dim.15), calls=%async_computation.1 | async-start | bytes 1048576 | tf_op jit(solution)/shard_map/all_to_all | solution.py:421
  113.4 3.7 %collective-permute-start.15 = (f32[320,128]{1,0:T(8,128)S(1)}, f32[320,128]{1,0:T(8,128)S(1)}, u32[]{:S(2)}, u32[]{:S(2)}) collective-permute-start(f32[320,128]{1,0:T(8,128)S(1)} %collective-permute-done.13), channel_id=1, source_target_pairs={{0,2},{2,4},{4,6},{6,8},{8,10},{10,12},{12,14},{14,16},{16,18},{18... | collective-permute-start | bytes 491528 | tf_op jit(solution)/shard_map/ppermute | solution.py:435
  119.8 4.6 %collective-permute-start.17 = (f32[320,128]{1,0:T(8,128)S(1)}, f32[320,128]{1,0:T(8,128)}, u32[]{:S(2)}, u32[]{:S(2)}) collective-permute-start(f32[320,128]{1,0:T(8,128)S(1)} %collective-permute-done.15), channel_id=1, source_target_pairs={{0,2},{2,4},{4,6},{6,8},{8,10},{10,12},{12,14},{14,16},{16,18},{18... | collective-permute-start | bytes 491528 | tf_op jit(solution)/shard_map/ppermute | solution.py:435
  127.2 4.6 %collective-permute-start.19 = (f32[320,128]{1,0:T(8,128)}, f32[320,128]{1,0:T(8,128)S(1)}, u32[]{:S(2)}, u32[]{:S(2)}) collective-permute-start(f32[320,128]{1,0:T(8,128)} %collective-permute-done.17), channel_id=1, source_target_pairs={{0,2},{2,4},{4,6},{6,8},{8,10},{10,12},{12,14},{14,16},{16,18},{18... | collective-permute-start | bytes 491528 | tf_op jit(solution)/shard_map/ppermute | solution.py:435
  134.3 4.9 %collective-permute-start.21 = (f32[320,128]{1,0:T(8,128)S(1)}, f32[320,128]{1,0:T(8,128)S(1)}, u32[]{:S(2)}, u32[]{:S(2)}) collective-permute-start(f32[320,128]{1,0:T(8,128)S(1)} %collective-permute-done.19), channel_id=1, source_target_pairs={{1,31},{3,1},{5,3},{7,5},{9,7},{11,9},{13,11},{15,13},{17,15},{19,... | collective-permute-start | bytes 491528 | tf_op jit(solution)/shard_map/ppermute | solution.py:435
  142.8 7.0 %collective-permute-start.22 = (f32[8,2,320,128]{3,2,1,0:T(8,128)S(1)}, f32[8,2,320,128]{3,2,1,0:T(8,128)}, u32[]{:S(2)}, u32[]{:S(2)}) collective-permute-start(f32[8,2,320,128]{3,2,1,0:T(8,128)S(1)} %fusion.7.total), channel_id=1, source_target_pairs={{0,1},{1,0},{2,3},{3,2},{4,5},{5,4},{6,7},{7,6},{8,9},{9,8},{10,11... | collective-permute-start | bytes 7864328 | tf_op jit(solution)/shard_map/ppermute | solution.py:429
  155.3 8.4 %orth.1 = (bf16[256,4096]{1,0:T(8,128)(2,1)S(1)}, f32[64,128]{1,0:T(8,128)S(1)}) custom-call(s32[2]{0:T(128)S(1)} %pad_add_fusion.info, f32[16,64,128]{2,1,0:T(8,128)S(1)} %bitcast.87, f32[16,64,128]{2,1,0:T(8,128)} %collective-permute-done.5.other), custom_call_target="tpu_custom_call" | custom-call | tf_op jit(solution)/shard_map/orth/pallas_call | solution.py:304
  165.4 7.0 %first.1 = (f32[16,64,128]{2,1,0:T(8,128)S(1)}, bf16[320,4096]{1,0:T(8,128)(2,1)S(1)}, bf16[320,4096]{1,0:T(8,128)(2,1)S(1)}) custom-call(s32[2]{0:T(128)S(1)} %pad_add_fusion.info, bf16[256,4096]{1,0:T(8,128)(2,1)S(1)} %get-tuple-element.15.held, f32[64,128]{1,0:T(8,128)S(1)} %get-tuple-element.16.second, f32[8,2,320,128]{3,2,1,0:T(8,128)S(1)} %copy-done.6, ...), custom_call_target="tpu_custom_call" | custom-call | tf_op jit(solution)/shard_map/first/pallas_call | solution.py:319
  173.9 17.1 %all_to_all.35 = f32[16,64,128]{2,1,0:T(8,128)S(1)} all-to-all(f32[16,64,128]{2,1,0:T(8,128)S(1)} %get-tuple-element.21), channel_id=1, replica_groups=mesh['rep'=16,'z'=16,'core'=2] {'rep'}, dimensions={0} | all-to-all | bytes 1048576 | tf_op jit(solution)/shard_map/all_to_all | solution.py:421
  191.1 12.7 %all_to_all.36.own = f32[16,64,128]{2,1,0:T(8,128)S(1)} all-to-all(f32[16,64,128]{2,1,0:T(8,128)S(1)} %broadcast_in_dim.16), channel_id=1, replica_groups=mesh['rep'=16,'z'=16,'core'=2] {'rep'}, dimensions={0} | all-to-all | bytes 1048576 | tf_op jit(solution)/shard_map/all_to_all | solution.py:421
  203.8 5.4 %collective-permute-start.23 = (f32[16,64,128]{2,1,0:T(8,128)S(1)}, f32[16,64,128]{2,1,0:T(8,128)S(1)}, u32[]{:S(2)}, u32[]{:S(2)}) collective-permute-start(f32[16,64,128]{2,1,0:T(8,128)S(1)} %all_to_all.36.own), channel_id=1, source_target_pairs={{0,1},{1,0},{2,3},{3,2},{4,5},{5,4},{6,7},{7,6},{8,9},{9,8},{10,11... | collective-permute-start | bytes 1572872 | tf_op jit(solution)/shard_map/ppermute | solution.py:429
  212.3 12.3 %step.1 = f32[16,64,128]{2,1,0:T(8,128)S(1)} custom-call(s32[2]{0:T(128)S(1)} %pad_add_fusion.info, f32[16,64,128]{2,1,0:T(8,128)S(1)} %all_to_all.36.own, f32[16,64,128]{2,1,0:T(8,128)S(1)} %collective-permute-done.23.other, bf16[320,4096]{1,0:T(8,128)(2,1)S(1)} %get-tuple-element.22.high_in, bf16[320,4096]{1,0:T(8,128)(2,1)S(1)} %copy-done.1), custom_call_target="tpu_custom_call" | custom-call | tf_op jit(solution)/shard_map/step/pallas_call | solution.py:333
  224.6 13.3 %all_to_all.37 = f32[16,64,128]{2,1,0:T(8,128)S(1)} all-to-all(f32[16,64,128]{2,1,0:T(8,128)S(1)} %step.1), channel_id=1, replica_groups=mesh['rep'=16,'z'=16,'core'=2] {'rep'}, dimensions={0} | all-to-all | bytes 1048576 | tf_op jit(solution)/shard_map/all_to_all | solution.py:421
  238.0 12.7 %all_to_all.38.own = f32[16,64,128]{2,1,0:T(8,128)S(1)} all-to-all(f32[16,64,128]{2,1,0:T(8,128)S(1)} %broadcast_in_dim.34), channel_id=1, replica_groups=mesh['rep'=16,'z'=16,'core'=2] {'rep'}, dimensions={0} | all-to-all | bytes 1048576 | tf_op jit(solution)/shard_map/all_to_all | solution.py:421
  250.7 5.4 %collective-permute-start.24 = (f32[16,64,128]{2,1,0:T(8,128)S(1)}, f32[16,64,128]{2,1,0:T(8,128)}, u32[]{:S(2)}, u32[]{:S(2)}) collective-permute-start(f32[16,64,128]{2,1,0:T(8,128)S(1)} %all_to_all.38.own), channel_id=1, source_target_pairs={{0,1},{1,0},{2,3},{3,2},{4,5},{5,4},{6,7},{7,6},{8,9},{9,8},{10,11... | collective-permute-start | bytes 1572872 | tf_op jit(solution)/shard_map/ppermute | solution.py:429
  259.3 12.4 %last.1 = (f32[2,80,128]{2,1,0:T(8,128)S(1)}, f32[64,128]{1,0:T(8,128)S(1)}) custom-call(s32[2]{0:T(128)S(1)} %pad_add_fusion.info, f32[16,64,128]{2,1,0:T(8,128)S(1)} %all_to_all.38.own, f32[16,64,128]{2,1,0:T(8,128)} %collective-permute-done.24.other, bf16[320,4096]{1,0:T(8,128)(2,1)S(1)} %get-tuple-element.22.high_in, bf16[320,4096]{1,0:T(8,128)(2,1)S(1)} %copy-done.2), custom_call_target="tpu_custom_call" | custom-call | tf_op jit(solution)/shard_map/last/pallas_call | solution.py:347
  271.8 14.9 %all_to_all.39.own = f32[16,80,128]{2,1,0:T(8,128)S(1)} all-to-all(f32[16,80,128]{2,1,0:T(8,128)S(1)} %broadcast_in_dim.36), channel_id=1, replica_groups=mesh['rep'=16,'z'=16,'core'=2] {'rep'}, dimensions={0} | all-to-all | bytes 1310720 | tf_op jit(solution)/shard_map/all_to_all | solution.py:421
  286.7 3.6 %collective-permute-start.25 = (f32[16,80,128]{2,1,0:T(8,128)S(1)}, f32[16,80,128]{2,1,0:T(8,128)S(1)}, u32[]{:S(2)}, u32[]{:S(2)}) collective-permute-start(f32[16,80,128]{2,1,0:T(8,128)S(1)} %all_to_all.39.own), channel_id=1, source_target_pairs={{0,1},{1,0},{2,3},{3,2},{4,5},{5,4},{6,7},{7,6},{8,9},{9,8},{10,11... | collective-permute-start | bytes 1966088 | tf_op jit(solution)/shard_map/ppermute | solution.py:429
  292.0 3.0 %finish.1 = (bf16[128,5120]{1,0:T(8,128)(2,1)}, f32[64,5120]{1,0:T(8,128)}) custom-call(s32[1]{0:T(128)} %bitcast.flag, bf16[128,5120]{1,0:T(8,128)(2,1)S(1)} %bitcast.83, bf16[128,5120]{1,0:T(8,128)(2,1)S(1)} %bitcast.85, f32[16,80,128]{2,1,0:T(8,128)S(1)} %all_to_all.39.own, f32[16,80,128]{2,1,0:T(8,128)S(1)} %collective-permute-done.25.other, ...), custom_call_target="tpu_custom_call" | custom-call | tf_op jit(solution)/shard_map/finish/pallas_call | solution.py:409
  (80 shorter events, 43.7 us)
Async XLA Ops:
  5.6 38.6 %all-to-all-start = ((f32[16,328,128]{2,1,0:T(8,128)}), f32[16,328,128]{2,1,0:T(8,128)S(1)}, u32[]{:S(2)}, u32[]{:S(2)}) async-start(f32[16,328,128]{2,1,0:T(8,128)} %start.1), calls=%async_computation | async-start | bytes 5373952 | tf_op jit(solution)/shard_map/all_to_all | solution.py:421
  44.4 20.9 %collective-permute-start = (f32[328,128]{1,0:T(8,128)S(1)}, f32[328,128]{1,0:T(8,128)S(1)}, u32[]{:S(2)}, u32[]{:S(2)}) collective-permute-start(f32[328,128]{1,0:T(8,128)S(1)} %reduce_sum.27), channel_id=1, source_target_pairs={{0,1},{1,0},{2,3},{3,2},{4,5},{5,4},{6,7},{7,6},{8,9},{9,8},{10,11... | collective-permute-start | bytes 503816 | tf_op jit(solution)/shard_map/ppermute | solution.py:429
  52.6 18.0 %collective-permute-start.6 = (f32[320,128]{1,0:T(8,128)S(1)}, f32[320,128]{1,0:T(8,128)S(1)}, u32[]{:S(2)}, u32[]{:S(2)}) collective-permute-start(f32[320,128]{1,0:T(8,128)S(1)} %slice.18), channel_id=1, source_target_pairs={{0,2},{2,4},{4,6},{6,8},{8,10},{10,12},{12,14},{14,16},{16,18},{18... | collective-permute-start | bytes 491528 | tf_op jit(solution)/shard_map/ppermute | solution.py:435
  65.3 5.3 %collective-permute-start.1 = (f32[1,2,4,128]{3,2,1,0:T(4,128)S(1)}, f32[1,2,4,128]{3,2,1,0:T(4,128)S(1)}, u32[]{:S(2)}, u32[]{:S(2)}) collective-permute-start(f32[1,2,4,128]{3,2,1,0:T(4,128)S(1)} %fusion.8), channel_id=1, source_target_pairs={{0,2},{2,4},{4,6},{6,8},{8,10},{10,12},{12,14},{14,16},{16,18},{18... | collective-permute-start | bytes 12296 | tf_op jit(solution)/shard_map/ppermute | solution.py:435
  67.9 10.9 %collective-permute-start.7 = (f32[320,128]{1,0:T(8,128)S(1)}, f32[320,128]{1,0:T(8,128)S(1)}, u32[]{:S(2)}, u32[]{:S(2)}) collective-permute-start(f32[320,128]{1,0:T(8,128)S(1)} %slice.19), channel_id=1, source_target_pairs={{0,2},{2,4},{4,6},{6,8},{8,10},{10,12},{12,14},{14,16},{16,18},{18... | collective-permute-start | bytes 491528 | tf_op jit(solution)/shard_map/ppermute | solution.py:435
  70.6 13.0 %collective-permute-start.8 = (f32[320,128]{1,0:T(8,128)S(1)}, f32[320,128]{1,0:T(8,128)S(1)}, u32[]{:S(2)}, u32[]{:S(2)}) collective-permute-start(f32[320,128]{1,0:T(8,128)S(1)} %collective-permute-done.6), channel_id=1, source_target_pairs={{0,2},{2,4},{4,6},{6,8},{8,10},{10,12},{12,14},{14,16},{16,18},{18... | collective-permute-start | bytes 491528 | tf_op jit(solution)/shard_map/ppermute | solution.py:435
  73.5 5.3 %collective-permute-start.2 = (f32[2,2,4,128]{3,2,1,0:T(4,128)S(1)}, f32[2,2,4,128]{3,2,1,0:T(4,128)S(1)}, u32[]{:S(2)}, u32[]{:S(2)}) collective-permute-start(f32[2,2,4,128]{3,2,1,0:T(4,128)S(1)} %pad_maximum_fusion.2), channel_id=1, source_target_pairs={{0,4},{2,6},{4,8},{6,10},{8,12},{10,14},{12,16},{14,18},{16,20},{1... | collective-permute-start | bytes 24584 | tf_op jit(solution)/shard_map/ppermute | solution.py:435
  78.8 17.8 %collective-permute-start.9 = (f32[320,128]{1,0:T(8,128)S(1)}, f32[320,128]{1,0:T(8,128)S(1)}, u32[]{:S(2)}, u32[]{:S(2)}) collective-permute-start(f32[320,128]{1,0:T(8,128)S(1)} %collective-permute-done.7), channel_id=1, source_target_pairs={{0,2},{2,4},{4,6},{6,8},{8,10},{10,12},{12,14},{14,16},{16,18},{18... | collective-permute-start | bytes 491528 | tf_op jit(solution)/shard_map/ppermute | solution.py:435
  83.7 15.7 %collective-permute-start.10 = (f32[320,128]{1,0:T(8,128)S(1)}, f32[320,128]{1,0:T(8,128)S(1)}, u32[]{:S(2)}, u32[]{:S(2)}) collective-permute-start(f32[320,128]{1,0:T(8,128)S(1)} %collective-permute-done.8), channel_id=1, source_target_pairs={{0,2},{2,4},{4,6},{6,8},{8,10},{10,12},{12,14},{14,16},{16,18},{18... | collective-permute-start | bytes 491528 | tf_op jit(solution)/shard_map/ppermute | solution.py:435
  86.3 8.4 %collective-permute-start.3 = (f32[4,2,4,128]{3,2,1,0:T(4,128)S(1)}, f32[4,2,4,128]{3,2,1,0:T(4,128)S(1)}, u32[]{:S(2)}, u32[]{:S(2)}) collective-permute-start(f32[4,2,4,128]{3,2,1,0:T(4,128)S(1)} %pad_maximum_fusion.1), channel_id=1, source_target_pairs={{0,8},{2,10},{4,12},{6,14},{8,16},{10,18},{12,20},{14,22},{16,24},... | collective-permute-start | bytes 49160 | tf_op jit(solution)/shard_map/ppermute | solution.py:435
  94.7 7.5 %collective-permute-start.4 = (f32[8,2,4,128]{3,2,1,0:T(4,128)S(1)}, f32[8,2,4,128]{3,2,1,0:T(4,128)S(1)}, u32[]{:S(2)}, u32[]{:S(2)}) collective-permute-start(f32[8,2,4,128]{3,2,1,0:T(4,128)S(1)} %pad_maximum_fusion), channel_id=1, source_target_pairs={{1,31},{3,1},{5,3},{7,5},{9,7},{11,9},{13,11},{15,13},{17,15},{19,... | collective-permute-start | bytes 98312 | tf_op jit(solution)/shard_map/ppermute | solution.py:435
  96.6 10.7 %collective-permute-start.11 = (f32[320,128]{1,0:T(8,128)S(1)}, f32[320,128]{1,0:T(8,128)S(1)}, u32[]{:S(2)}, u32[]{:S(2)}) collective-permute-start(f32[320,128]{1,0:T(8,128)S(1)} %collective-permute-done.9), channel_id=1, source_target_pairs={{0,2},{2,4},{4,6},{6,8},{8,10},{10,12},{12,14},{14,16},{16,18},{18... | collective-permute-start | bytes 491528 | tf_op jit(solution)/shard_map/ppermute | solution.py:435
  99.3 10.2 %collective-permute-start.12 = (f32[320,128]{1,0:T(8,128)S(1)}, f32[320,128]{1,0:T(8,128)S(1)}, u32[]{:S(2)}, u32[]{:S(2)}) collective-permute-start(f32[320,128]{1,0:T(8,128)S(1)} %collective-permute-done.10), channel_id=1, source_target_pairs={{0,2},{2,4},{4,6},{6,8},{8,10},{10,12},{12,14},{14,16},{16,18},{18... | collective-permute-start | bytes 491528 | tf_op jit(solution)/shard_map/ppermute | solution.py:435
  103.0 23.6 %all-to-all-start.1 = ((f32[16,64,128]{2,1,0:T(8,128)}), f32[16,64,128]{2,1,0:T(8,128)S(1)}, u32[]{:S(2)}, u32[]{:S(2)}) async-start(f32[16,64,128]{2,1,0:T(8,128)} %broadcast_in_dim.15), calls=%async_computation.1 | async-start | bytes 1048576 | tf_op jit(solution)/shard_map/all_to_all | solution.py:421
  107.4 6.1 %collective-permute-start.13 = (f32[320,128]{1,0:T(8,128)S(1)}, f32[320,128]{1,0:T(8,128)S(1)}, u32[]{:S(2)}, u32[]{:S(2)}) collective-permute-start(f32[320,128]{1,0:T(8,128)S(1)} %collective-permute-done.11), channel_id=1, source_target_pairs={{0,2},{2,4},{4,6},{6,8},{8,10},{10,12},{12,14},{14,16},{16,18},{18... | collective-permute-start | bytes 491528 | tf_op jit(solution)/shard_map/ppermute | solution.py:435
  109.6 7.5 %collective-permute-start.14 = (f32[320,128]{1,0:T(8,128)S(1)}, f32[320,128]{1,0:T(8,128)}, u32[]{:S(2)}, u32[]{:S(2)}) collective-permute-start(f32[320,128]{1,0:T(8,128)S(1)} %collective-permute-done.12), channel_id=1, source_target_pairs={{0,2},{2,4},{4,6},{6,8},{8,10},{10,12},{12,14},{14,16},{16,18},{18... | collective-permute-start | bytes 491528 | tf_op jit(solution)/shard_map/ppermute | solution.py:435
  113.4 6.3 %collective-permute-start.15 = (f32[320,128]{1,0:T(8,128)S(1)}, f32[320,128]{1,0:T(8,128)S(1)}, u32[]{:S(2)}, u32[]{:S(2)}) collective-permute-start(f32[320,128]{1,0:T(8,128)S(1)} %collective-permute-done.13), channel_id=1, source_target_pairs={{0,2},{2,4},{4,6},{6,8},{8,10},{10,12},{12,14},{14,16},{16,18},{18... | collective-permute-start | bytes 491528 | tf_op jit(solution)/shard_map/ppermute | solution.py:435
  117.1 7.3 %collective-permute-start.16 = (f32[320,128]{1,0:T(8,128)}, f32[320,128]{1,0:T(8,128)}, u32[]{:S(2)}, u32[]{:S(2)}) collective-permute-start(f32[320,128]{1,0:T(8,128)} %collective-permute-done.14), channel_id=1, source_target_pairs={{0,2},{2,4},{4,6},{6,8},{8,10},{10,12},{12,14},{14,16},{16,18},{18... | collective-permute-start | bytes 491528 | tf_op jit(solution)/shard_map/ppermute | solution.py:435
  119.8 7.4 %collective-permute-start.17 = (f32[320,128]{1,0:T(8,128)S(1)}, f32[320,128]{1,0:T(8,128)}, u32[]{:S(2)}, u32[]{:S(2)}) collective-permute-start(f32[320,128]{1,0:T(8,128)S(1)} %collective-permute-done.15), channel_id=1, source_target_pairs={{0,2},{2,4},{4,6},{6,8},{8,10},{10,12},{12,14},{14,16},{16,18},{18... | collective-permute-start | bytes 491528 | tf_op jit(solution)/shard_map/ppermute | solution.py:435
  124.4 7.4 %collective-permute-start.18 = (f32[320,128]{1,0:T(8,128)}, f32[320,128]{1,0:T(8,128)}, u32[]{:S(2)}, u32[]{:S(2)}) collective-permute-start(f32[320,128]{1,0:T(8,128)} %collective-permute-done.16), channel_id=1, source_target_pairs={{0,2},{2,4},{4,6},{6,8},{8,10},{10,12},{12,14},{14,16},{16,18},{18... | collective-permute-start | bytes 491528 | tf_op jit(solution)/shard_map/ppermute | solution.py:435
  127.2 7.1 %collective-permute-start.19 = (f32[320,128]{1,0:T(8,128)}, f32[320,128]{1,0:T(8,128)S(1)}, u32[]{:S(2)}, u32[]{:S(2)}) collective-permute-start(f32[320,128]{1,0:T(8,128)} %collective-permute-done.17), channel_id=1, source_target_pairs={{0,2},{2,4},{4,6},{6,8},{8,10},{10,12},{12,14},{14,16},{16,18},{18... | collective-permute-start | bytes 491528 | tf_op jit(solution)/shard_map/ppermute | solution.py:435
  131.8 7.5 %collective-permute-start.20 = (f32[320,128]{1,0:T(8,128)}, f32[320,128]{1,0:T(8,128)S(1)}, u32[]{:S(2)}, u32[]{:S(2)}) collective-permute-start(f32[320,128]{1,0:T(8,128)} %collective-permute-done.18), channel_id=1, source_target_pairs={{1,31},{3,1},{5,3},{7,5},{9,7},{11,9},{13,11},{15,13},{17,15},{19,... | collective-permute-start | bytes 491528 | tf_op jit(solution)/shard_map/ppermute | solution.py:435
  134.3 7.2 %collective-permute-start.21 = (f32[320,128]{1,0:T(8,128)S(1)}, f32[320,128]{1,0:T(8,128)S(1)}, u32[]{:S(2)}, u32[]{:S(2)}) collective-permute-start(f32[320,128]{1,0:T(8,128)S(1)} %collective-permute-done.19), channel_id=1, source_target_pairs={{1,31},{3,1},{5,3},{7,5},{9,7},{11,9},{13,11},{15,13},{17,15},{19,... | collective-permute-start | bytes 491528 | tf_op jit(solution)/shard_map/ppermute | solution.py:435
  142.8 20.9 %collective-permute-start.22 = (f32[8,2,320,128]{3,2,1,0:T(8,128)S(1)}, f32[8,2,320,128]{3,2,1,0:T(8,128)}, u32[]{:S(2)}, u32[]{:S(2)}) collective-permute-start(f32[8,2,320,128]{3,2,1,0:T(8,128)S(1)} %fusion.7.total), channel_id=1, source_target_pairs={{0,1},{1,0},{2,3},{3,2},{4,5},{5,4},{6,7},{7,6},{8,9},{9,8},{10,11... | collective-permute-start | bytes 7864328 | tf_op jit(solution)/shard_map/ppermute | solution.py:429
  151.3 3.9 %collective-permute-start.5 = (f32[16,64,128]{2,1,0:T(8,128)S(1)}, f32[16,64,128]{2,1,0:T(8,128)}, u32[]{:S(2)}, u32[]{:S(2)}) collective-permute-start(f32[16,64,128]{2,1,0:T(8,128)S(1)} %bitcast.86), channel_id=1, source_target_pairs={{0,1},{1,0},{2,3},{3,2},{4,5},{5,4},{6,7},{7,6},{8,9},{9,8},{10,11... | collective-permute-start | bytes 1572872 | tf_op jit(solution)/shard_map/ppermute | solution.py:429
  163.6 1.8 copy-start.6
  203.8 6.7 %collective-permute-start.23 = (f32[16,64,128]{2,1,0:T(8,128)S(1)}, f32[16,64,128]{2,1,0:T(8,128)S(1)}, u32[]{:S(2)}, u32[]{:S(2)}) collective-permute-start(f32[16,64,128]{2,1,0:T(8,128)S(1)} %all_to_all.36.own), channel_id=1, source_target_pairs={{0,1},{1,0},{2,3},{3,2},{4,5},{5,4},{6,7},{7,6},{8,9},{9,8},{10,11... | collective-permute-start | bytes 1572872 | tf_op jit(solution)/shard_map/ppermute | solution.py:429
  210.5 1.7 copy-start.1
  250.7 6.8 %collective-permute-start.24 = (f32[16,64,128]{2,1,0:T(8,128)S(1)}, f32[16,64,128]{2,1,0:T(8,128)}, u32[]{:S(2)}, u32[]{:S(2)}) collective-permute-start(f32[16,64,128]{2,1,0:T(8,128)S(1)} %all_to_all.38.own), channel_id=1, source_target_pairs={{0,1},{1,0},{2,3},{3,2},{4,5},{5,4},{6,7},{7,6},{8,9},{9,8},{10,11... | collective-permute-start | bytes 1572872 | tf_op jit(solution)/shard_map/ppermute | solution.py:429
  259.3 32.7 %copy-start.3 = (bf16[1,128,5120]{2,1,0:T(8,128)(2,1)S(1)}, bf16[1,128,5120]{2,1,0:T(8,128)(2,1)}, u32[]{:S(2)}) copy-start(bf16[1,128,5120]{2,1,0:T(8,128)(2,1)} %param.3) | copy-start | bytes 3932164
  259.3 32.7 %copy-start.4 = (bf16[1,128,5120]{2,1,0:T(8,128)(2,1)S(1)}, bf16[1,128,5120]{2,1,0:T(8,128)(2,1)}, u32[]{:S(2)}) copy-start(bf16[1,128,5120]{2,1,0:T(8,128)(2,1)} %param.4) | copy-start | bytes 3932164
  286.7 5.3 %collective-permute-start.25 = (f32[16,80,128]{2,1,0:T(8,128)S(1)}, f32[16,80,128]{2,1,0:T(8,128)S(1)}, u32[]{:S(2)}, u32[]{:S(2)}) collective-permute-start(f32[16,80,128]{2,1,0:T(8,128)S(1)} %all_to_all.39.own), channel_id=1, source_target_pairs={{0,1},{1,0},{2,3},{3,2},{4,5},{5,4},{6,7},{7,6},{8,9},{9,8},{10,11... | collective-permute-start | bytes 1966088 | tf_op jit(solution)/shard_map/ppermute | solution.py:429
  (3 other events, 4.8 us)

commit v6 on v2

--- a/solution.py
+++ b/solution.py
@@ -95,43 +95,57 @@
     count = rank // step
     row = lax.broadcasted_iota(jnp.int32, (step, wide), 0)
     col = lax.broadcasted_iota(jnp.int32, (step, wide), 1)
+
+    def spread(x, k):
+        return jnp.broadcast_to(x[:, k : k + 1], (step, wide))
+
+    def line_of(x, j):
+        return jnp.broadcast_to(x[j : j + 1, :], (step, wide))
+
+    parts = [gram_twice[b * step : (b + 1) * step] for b in range(count)]
+    near = [jnp.where(col == row + b * step, parts[b], 0.0) for b in range(count)]
+    both = sum(jnp.where(col == row + (rank + b * step), parts[b], near[b]) for b in range(count))
+    across = lax.rsqrt(jnp.sum(both, axis=0, keepdims=True))
     a = []
     for b in range(count):
+        down = lax.rsqrt(jnp.sum(near[b], axis=1, keepdims=True))
         unit = (col == row + (rank + b * step)).astype(F32)
-        a.append(jnp.where(col < rank, gram_twice[b * step : (b + 1) * step], unit))
-
-    def spread(x, k):
-        return jnp.broadcast_to(x[:, k : k + 1], (step, wide))
-
-    def line_of(x, j):
-        return jnp.broadcast_to(x[j : j + 1, :], (step, wide))
+        a.append(jnp.where(col < rank, parts[b] * down * across, unit))
 
     done = []
     for p in range(count):
         panel = a[p]
         f = [spread(panel, p * step + j) for j in range(step)]
         pivots = jnp.ones((step, wide), F32)
-        lines, weight = [], []
-        for j in range(step):
-            pivot = line_of(f[j], j)
-            inverse = 1.0 / pivot
-            below = jnp.where(row > j, f[j], 0.0)
-            line = line_of(panel, j) * inverse
-            panel = panel - below * line
+        pairs = []
+        for j in range(0, step, 2):
+            x, z, y = line_of(f[j], j), line_of(f[j], j + 1), line_of(f[j + 1], j + 1)
+            det = x * y - z * z
+            inverse = 1.0 / det
+
+            def solve(v):
+                top, low = line_of(v, j), line_of(v, j + 1)
+                return (y * top - z * low) * inverse, (x * low - z * top) * inverse
+
+            below = [jnp.where(row > j + 1, f[j + i], 0.0) for i in range(2)]
             ahead = {}
-            for t in range(j + 1, step):
-                ahead[t] = line_of(f[t], j) * inverse
-                f[t] = f[t] - below * ahead[t]
-            pivots = jnp.where(row == j, pivot, pivots)
-            lines.append(line)
-            weight.append(ahead)
-        done.append(jnp.where(col < rank, 0.0, panel * lax.rsqrt(pivots)))
+            for t in range(j + 2, step):
+                ahead[t] = solve(f[t])
+                f[t] = f[t] - (below[0] * ahead[t][0] + below[1] * ahead[t][1])
+            line = solve(panel)
+            ratio = 1.0 / x
+            second = line_of(panel, j + 1) - (z * ratio) * line_of(panel, j)
+            panel = panel - (below[0] * line[0] + below[1] * line[1])
+            panel = jnp.where(row == j + 1, second, panel)
+            pivots = jnp.where(row == j, x, jnp.where(row == j + 1, det * ratio, pivots))
+            pairs.append((line, ahead))
+        done.append(jnp.where(col < rank, 0.0, panel * lax.rsqrt(pivots) * across))
         for b in range(p + 1, count):
             g = [spread(a[b], p * step + j) for j in range(step)]
-            for j in range(step):
-                for t in range(j + 1, step):
-                    g[t] = g[t] - g[j] * weight[j][t]
-                a[b] = a[b] - g[j] * lines[j]
+            for j, (line, ahead) in zip(range(0, step, 2), pairs):
+                for t in range(j + 2, step):
+                    g[t] = g[t] - (g[j] * ahead[t][0] + g[j + 1] * ahead[t][1])
+                a[b] = a[b] - (g[j] * line[0] + g[j + 1] * line[1])
     w = jnp.concatenate(done, axis=0)
     return w + pltpu.roll(w, rank, 1)
 
@@ -223,26 +237,16 @@
         out[2 * j + 1] = x[:, rows:]
 
 
-def first_kernel(scale, info, own, other, total, total_other, out, high_out, low_out, held, high, low, sems):
-    length = own.shape[0]
+def parts_kernel(info, total, total_other, high, low):
+    half = total.shape[0]
     for mine, blocks in ((True, total), (False, total_other)):
-        at = planes(info, length, mine)
+        at = planes(info, 2 * half, mine)
         core = info[1] if mine else 1 - info[1]
-        for j in range(length // 2):
+        for j in range(half):
             for stream in range(2):
                 side = core if stream == 0 else 1 - core
                 span = pl.ds(pl.multiple_of(at(j) + side * LANES, LANES), LANES)
                 high[:, span], low[:, span] = split2(blocks[j, stream])
-    stores = [
-        pltpu.make_async_copy(high, high_out, sems.at[0]),
-        pltpu.make_async_copy(low, low_out, sems.at[1]),
-    ]
-    for store in stores:
-        store.start()
-    second = orthonormal(info, own, other, held)
-    next_left(info, right_factor(scale, second, held, high, low), high, low, out)
-    for store in stores:
-        store.wait()
 
 
 def load_parts(high_in, low_in, high, low, sems):
@@ -289,20 +293,16 @@
     return [pltpu.VMEM((4 * rank, n), BF16)], [pltpu.VMEM((cut, n), BF16)] * 2
 
 
-def first(scale, info, own, other, total, total_other):
-    length, rank, rows = own.shape
-    cut = total.shape[2]
-    held, both = scratch(length, rank, cut)
-    whole = jax.ShapeDtypeStruct((cut, 2 * length * rows), BF16)
+def parts(info, total, total_other):
+    half, cores, cut, rows = total.shape
+    whole = jax.ShapeDtypeStruct((cut, 2 * half * cores * rows), BF16)
     return pl.pallas_call(
-        functools.partial(first_kernel, scale),
-        in_specs=[SMEM_SPEC] + [VMEM_SPEC] * 4,
-        out_specs=[VMEM_SPEC, HBM_SPEC, HBM_SPEC],
-        out_shape=[jax.ShapeDtypeStruct(own.shape, F32), whole, whole],
-        scratch_shapes=held + both + [pltpu.SemaphoreType.DMA((2,))],
+        parts_kernel,
+        in_specs=[SMEM_SPEC, VMEM_SPEC, VMEM_SPEC],
+        out_shape=[whole, whole],
         compiler_params=params(),
-        name="first",
-    )(info, own, other, total, total_other)
+        name="parts",
+    )(info, total, total_other)
 
 
 def step(scale, info, own, other, high, low):
@@ -438,11 +438,10 @@
     piece = jnp.where(core == 0, piece, piece[:, ::-1]).reshape(length * extra, rows)
     own = gather(piece, "rep", reps).reshape(reps, length, extra, rows)
     own = own.transpose(1, 0, 2, 3).reshape(length, rank, rows)
-    partial, high, low = first(scale, info, own, swap_cores(own), total, swap_cores(total))
+    high, low = parts(info, total, swap_cores(total))
     for turn in range(ITERS - 1):
+        partial = step(scale, info, own, swap_cores(own), high, low)
         own = gather(jnp.sum(exchange(partial, "rep"), axis=0), "rep", reps)
-        if turn < ITERS - 2:
-            partial = step(scale, info, own, swap_cores(own), high, low)
     part_q, basis = last(scale, info, own, swap_cores(own), high, low)
     own_q = gather(lax.dynamic_index_in_dim(part_q, core, 0, False), "rep", reps)
     new_errors, factor_q = finish(flag, grads, errors, own_q, swap_cores(own_q), basis)

time: 276 us -> 278 us (level)
  Pallas kernels: 44.9 us -> 49.4 us
    pallas_call x1 -> x2, Pallas kernels: 12.3 us -> 25.8 us  [step(): pl.pallas_call(functools.partial(step_kernel, scale), in_specs=[SMEM_SPEC...]
    pallas_call x1, Pallas kernels: 12.2 us -> 3.04 us  [parts(): pl.pallas_call(parts_kernel, in_specs=[SMEM_SPEC, VMEM_SPEC, VMEM_SPEC],...]
  transfers between devices with their start and end apart: 22 -> 22, of which waited for: 5 -> 4; matrix products, arithmetic and copies ran while one was open for 0% -> 0% of each run, Pallas kernels for 0% -> 1%
where the time goes in v6:
time: 278 us; the launch traced here: 277 us
  blocking collectives  120 us (43%)
  starting transfers between devices  91.7 us (33%)
  Pallas kernels  49.4 us (18%)
  waiting for transfers between devices  7.77 us (3%)
  local copies, waits for them, and re-layouts  6.21 us (2%)
    all_to_all x7, blocking collectives, exchange(): return lax.all_to_all(chunks, axis, 0, 0)  120 us
    ppermute x16, starting transfers between devices, ring(): lax.ppermute(blocks[-1], ('z', 'core'), up + down if s < half - 1 else down)  65 us
    ppermute x6, starting transfers between devices, swap_cores(): return lax.ppermute(block, 'core', [(0, 1), (1, 0)])  26.8 us
    pallas_call x2, Pallas kernels, step(): pl.pallas_call(functools.partial(step_kernel, scale), in_specs=[SMEM_SPEC...  25.8 us
    pallas_call x1, Pallas kernels, last(): pl.pallas_call(functools.partial(last_kernel, scale), in_specs=[SMEM_SPEC...  12.5 us
  transfers between devices with their start and end apart: 22, of which 4 were waited for; matrix products, arithmetic and copies ran while one was open for 0% of the time, Pallas kernels for 1%

profile of v6, /device:TPU:1, one launch (start us, length us, event | category | flops | bytes accessed | tf_op | source)
XLA Modules:
  0.0 276.8 jit_solution(3175360957814275032)
XLA Ops:
  0.6 5.0 %start.1 = f32[16,328,128]{2,1,0:T(8,128)} custom-call(bf16[128,5120]{1,0:T(8,128)(2,1)} %bitcast.76, bf16[128,5120]{1,0:T(8,128)(2,1)} %bitcast.78, f32[64,5120]{1,0:T(8,128)} %q_start.1), custom_call_target="tpu_custom_call" | custom-call | tf_op jit(solution)/shard_map/start/pallas_call | solution.py:76
  5.6 39.2 %all_to_all.35 = f32[16,328,128]{2,1,0:T(8,128)S(1)} all-to-all(f32[16,328,128]{2,1,0:T(8,128)} %start.1), channel_id=1, replica_groups=mesh['rep'=16,'z'=16,'core'=2] {'rep'}, dimensions={0} | all-to-all | bytes 5373952 | tf_op jit(solution)/shard_map/all_to_all | solution.py:399
  44.9 6.0 %collective-permute-start.1 = (f32[328,128]{1,0:T(8,128)S(1)}, f32[328,128]{1,0:T(8,128)S(1)}, u32[]{:S(2)}, u32[]{:S(2)}) collective-permute-start(f32[328,128]{1,0:T(8,128)S(1)} %reduce_sum.27), channel_id=1, source_target_pairs={{0,1},{1,0},{2,3},{3,2},{4,5},{5,4},{6,7},{7,6},{8,9},{9,8},{10,11... | collective-permute-start | bytes 503816 | tf_op jit(solution)/shard_map/ppermute | solution.py:407
  50.9 11.5 %collective-permute-start = (f32[328,128]{1,0:T(8,128)S(1)}, f32[328,128]{1,0:T(8,128)S(1)}, u32[]{:S(2)}, u32[]{:S(2)}) collective-permute-start(f32[328,128]{1,0:T(8,128)S(1)} %reduce_sum.27), channel_id=1, source_target_pairs={{0,2},{2,4},{4,6},{6,8},{8,10},{10,12},{12,14},{14,16},{16,18},{18... | collective-permute-start | bytes 503816 | tf_op jit(solution)/shard_map/ppermute | solution.py:416
  62.4 2.6 collective-permute-start.2
  65.1 4.6 %collective-permute-start.3 = (f32[328,128]{1,0:T(8,128)S(1)}, f32[328,128]{1,0:T(8,128)S(1)}, u32[]{:S(2)}, u32[]{:S(2)}) collective-permute-start(f32[328,128]{1,0:T(8,128)S(1)} %collective-permute-done), channel_id=1, source_target_pairs={{0,2},{2,4},{4,6},{6,8},{8,10},{10,12},{12,14},{14,16},{16,18},{18... | collective-permute-start | bytes 503816 | tf_op jit(solution)/shard_map/ppermute | solution.py:416
  69.7 2.6 collective-permute-start.4
  72.4 4.6 %collective-permute-start.5 = (f32[328,128]{1,0:T(8,128)S(1)}, f32[328,128]{1,0:T(8,128)S(1)}, u32[]{:S(2)}, u32[]{:S(2)}) collective-permute-start(f32[328,128]{1,0:T(8,128)S(1)} %collective-permute-done.3), channel_id=1, source_target_pairs={{0,2},{2,4},{4,6},{6,8},{8,10},{10,12},{12,14},{14,16},{16,18},{18... | collective-permute-start | bytes 503816 | tf_op jit(solution)/shard_map/ppermute | solution.py:416
  77.0 2.6 collective-permute-start.6
  79.7 4.6 %collective-permute-start.7 = (f32[328,128]{1,0:T(8,128)S(1)}, f32[328,128]{1,0:T(8,128)S(1)}, u32[]{:S(2)}, u32[]{:S(2)}) collective-permute-start(f32[328,128]{1,0:T(8,128)S(1)} %collective-permute-done.5), channel_id=1, source_target_pairs={{0,2},{2,4},{4,6},{6,8},{8,10},{10,12},{12,14},{14,16},{16,18},{18... | collective-permute-start | bytes 503816 | tf_op jit(solution)/shard_map/ppermute | solution.py:416
  84.3 2.6 collective-permute-start.8
  87.0 4.6 %collective-permute-start.9 = (f32[328,128]{1,0:T(8,128)S(1)}, f32[328,128]{1,0:T(8,128)S(1)}, u32[]{:S(2)}, u32[]{:S(2)}) collective-permute-start(f32[328,128]{1,0:T(8,128)S(1)} %collective-permute-done.7), channel_id=1, source_target_pairs={{0,2},{2,4},{4,6},{6,8},{8,10},{10,12},{12,14},{14,16},{16,18},{18... | collective-permute-start | bytes 503816 | tf_op jit(solution)/shard_map/ppermute | solution.py:416
  94.3 4.6 %collective-permute-start.11 = (f32[328,128]{1,0:T(8,128)S(1)}, f32[328,128]{1,0:T(8,128)S(1)}, u32[]{:S(2)}, u32[]{:S(2)}) collective-permute-start(f32[328,128]{1,0:T(8,128)S(1)} %collective-permute-done.9), channel_id=1, source_target_pairs={{0,2},{2,4},{4,6},{6,8},{8,10},{10,12},{12,14},{14,16},{16,18},{18... | collective-permute-start | bytes 503816 | tf_op jit(solution)/shard_map/ppermute | solution.py:416
  101.6 4.6 %collective-permute-start.13 = (f32[328,128]{1,0:T(8,128)S(1)}, f32[328,128]{1,0:T(8,128)S(1)}, u32[]{:S(2)}, u32[]{:S(2)}) collective-permute-start(f32[328,128]{1,0:T(8,128)S(1)} %collective-permute-done.11), channel_id=1, source_target_pairs={{0,2},{2,4},{4,6},{6,8},{8,10},{10,12},{12,14},{14,16},{16,18},{18... | collective-permute-start | bytes 503816 | tf_op jit(solution)/shard_map/ppermute | solution.py:416
  106.3 2.6 collective-permute-start.14
  108.9 4.6 %collective-permute-start.15 = (f32[328,128]{1,0:T(8,128)S(1)}, f32[328,128]{1,0:T(8,128)S(1)}, u32[]{:S(2)}, u32[]{:S(2)}) collective-permute-start(f32[328,128]{1,0:T(8,128)S(1)} %collective-permute-done.13), channel_id=1, source_target_pairs={{1,31},{3,1},{5,3},{7,5},{9,7},{11,9},{13,11},{15,13},{17,15},{19,... | collective-permute-start | bytes 503816 | tf_op jit(solution)/shard_map/ppermute | solution.py:416
  116.3 3.3 %collective-permute-done.16 = f32[328,128]{1,0:T(8,128)S(1)} collective-permute-done((f32[328,128]{1,0:T(8,128)S(1)}, f32[328,128]{1,0:T(8,128)S(1)}, u32[]{:S(2)}, u32[]{:S(2)}) %collective-permute-start.16) | collective-permute-done | bytes 167968 | tf_op jit(solution)/shard_map/ppermute | solution.py:416
  122.4 13.3 %all_to_all.36 = f32[16,64,128]{2,1,0:T(8,128)S(1)} all-to-all(f32[16,64,128]{2,1,0:T(8,128)S(1)} %broadcast_in_dim.15), channel_id=1, replica_groups=mesh['rep'=16,'z'=16,'core'=2] {'rep'}, dimensions={0} | all-to-all | bytes 1048576 | tf_op jit(solution)/shard_map/all_to_all | solution.py:399
  136.2 4.2 %collective-permute-start.17 = (f32[16,64,128]{2,1,0:T(8,128)S(1)}, f32[16,64,128]{2,1,0:T(8,128)}, u32[]{:S(2)}, u32[]{:S(2)}) collective-permute-start(f32[16,64,128]{2,1,0:T(8,128)S(1)} %bitcast.80), channel_id=1, source_target_pairs={{0,1},{1,0},{2,3},{3,2},{4,5},{5,4},{6,7},{7,6},{8,9},{9,8},{10,11... | collective-permute-start | bytes 1572872 | tf_op jit(solution)/shard_map/ppermute | solution.py:407
  142.2 3.0 %parts.1 = (bf16[320,4096]{1,0:T(8,128)(2,1)S(1)}, bf16[320,4096]{1,0:T(8,128)(2,1)S(1)}) custom-call(s32[2]{0:T(128)S(1)} %pad_add_fusion.info, f32[8,2,320,128]{3,2,1,0:T(8,128)S(1)} %copy-done.4, f32[8,2,320,128]{3,2,1,0:T(8,128)} %collective-permute-done.18.total_other), custom_call_target="tpu_custom_call" | custom-call | tf_op jit(solution)/shard_map/parts/pallas_call | solution.py:299
  145.3 13.4 %step.2 = f32[16,64,128]{2,1,0:T(8,128)S(1)} custom-call(s32[2]{0:T(128)S(1)} %pad_add_fusion.info, f32[16,64,128]{2,1,0:T(8,128)S(1)} %bitcast.81, f32[16,64,128]{2,1,0:T(8,128)} %collective-permute-done.17.other, bf16[320,4096]{1,0:T(8,128)(2,1)S(1)} %get-tuple-element.8.high_in, bf16[320,4096]{1,0:T(8,128)(2,1)S(1)} %get-tuple-element.9.low_in), custom_call_target="tpu_custom_call" | custom-call | tf_op jit(solution)/shard_map/step/pallas_call | solution.py:311
  158.7 13.2 %all_to_all.37 = f32[16,64,128]{2,1,0:T(8,128)S(1)} all-to-all(f32[16,64,128]{2,1,0:T(8,128)S(1)} %step.2), channel_id=1, replica_groups=mesh['rep'=16,'z'=16,'core'=2] {'rep'}, dimensions={0} | all-to-all | bytes 1048576 | tf_op jit(solution)/shard_map/all_to_all | solution.py:399
  172.0 13.2 %all_to_all.38.own = f32[16,64,128]{2,1,0:T(8,128)S(1)} all-to-all(f32[16,64,128]{2,1,0:T(8,128)S(1)} %broadcast_in_dim.32), channel_id=1, replica_groups=mesh['rep'=16,'z'=16,'core'=2] {'rep'}, dimensions={0} | all-to-all | bytes 1048576 | tf_op jit(solution)/shard_map/all_to_all | solution.py:399
  185.1 5.6 %collective-permute-start.19 = (f32[16,64,128]{2,1,0:T(8,128)S(1)}, f32[16,64,128]{2,1,0:T(8,128)S(1)}, u32[]{:S(2)}, u32[]{:S(2)}) collective-permute-start(f32[16,64,128]{2,1,0:T(8,128)S(1)} %all_to_all.38.own), channel_id=1, source_target_pairs={{0,1},{1,0},{2,3},{3,2},{4,5},{5,4},{6,7},{7,6},{8,9},{9,8},{10,11... | collective-permute-start | bytes 1572872 | tf_op jit(solution)/shard_map/ppermute | solution.py:407
  193.7 12.5 %step.3 = f32[16,64,128]{2,1,0:T(8,128)S(1)} custom-call(s32[2]{0:T(128)S(1)} %pad_add_fusion.info, f32[16,64,128]{2,1,0:T(8,128)S(1)} %all_to_all.38.own, f32[16,64,128]{2,1,0:T(8,128)S(1)} %collective-permute-done.19.other, bf16[320,4096]{1,0:T(8,128)(2,1)S(1)} %get-tuple-element.8.high_in, bf16[320,4096]{1,0:T(8,128)(2,1)S(1)} %copy-done.1), custom_call_target="tpu_custom_call" | custom-call | tf_op jit(solution)/shard_map/step/pallas_call | solution.py:311
  206.2 13.3 %all_to_all.39 = f32[16,64,128]{2,1,0:T(8,128)S(1)} all-to-all(f32[16,64,128]{2,1,0:T(8,128)S(1)} %step.3), channel_id=1, replica_groups=mesh['rep'=16,'z'=16,'core'=2] {'rep'}, dimensions={0} | all-to-all | bytes 1048576 | tf_op jit(solution)/shard_map/all_to_all | solution.py:399
  219.6 12.7 %all_to_all.40.own = f32[16,64,128]{2,1,0:T(8,128)S(1)} all-to-all(f32[16,64,128]{2,1,0:T(8,128)S(1)} %broadcast_in_dim.33), channel_id=1, replica_groups=mesh['rep'=16,'z'=16,'core'=2] {'rep'}, dimensions={0} | all-to-all | bytes 1048576 | tf_op jit(solution)/shard_map/all_to_all | solution.py:399
  232.4 5.4 %collective-permute-start.20 = (f32[16,64,128]{2,1,0:T(8,128)S(1)}, f32[16,64,128]{2,1,0:T(8,128)}, u32[]{:S(2)}, u32[]{:S(2)}) collective-permute-start(f32[16,64,128]{2,1,0:T(8,128)S(1)} %all_to_all.40.own), channel_id=1, source_target_pairs={{0,1},{1,0},{2,3},{3,2},{4,5},{5,4},{6,7},{7,6},{8,9},{9,8},{10,11... | collective-permute-start | bytes 1572872 | tf_op jit(solution)/shard_map/ppermute | solution.py:407
  240.9 12.5 %last.1 = (f32[2,80,128]{2,1,0:T(8,128)S(1)}, f32[64,128]{1,0:T(8,128)S(1)}) custom-call(s32[2]{0:T(128)S(1)} %pad_add_fusion.info, f32[16,64,128]{2,1,0:T(8,128)S(1)} %all_to_all.40.own, f32[16,64,128]{2,1,0:T(8,128)} %collective-permute-done.20.other, bf16[320,4096]{1,0:T(8,128)(2,1)S(1)} %get-tuple-element.8.high_in, bf16[320,4096]{1,0:T(8,128)(2,1)S(1)} %copy-done.2), custom_call_target="tpu_custom_call" | custom-call | tf_op jit(solution)/shard_map/last/pallas_call | solution.py:325
  253.5 14.9 %all_to_all.41.own = f32[16,80,128]{2,1,0:T(8,128)S(1)} all-to-all(f32[16,80,128]{2,1,0:T(8,128)S(1)} %broadcast_in_dim.35), channel_id=1, replica_groups=mesh['rep'=16,'z'=16,'core'=2] {'rep'}, dimensions={0} | all-to-all | bytes 1310720 | tf_op jit(solution)/shard_map/all_to_all | solution.py:399
  268.4 3.6 %collective-permute-start.21 = (f32[16,80,128]{2,1,0:T(8,128)S(1)}, f32[16,80,128]{2,1,0:T(8,128)S(1)}, u32[]{:S(2)}, u32[]{:S(2)}) collective-permute-start(f32[16,80,128]{2,1,0:T(8,128)S(1)} %all_to_all.41.own), channel_id=1, source_target_pairs={{0,1},{1,0},{2,3},{3,2},{4,5},{5,4},{6,7},{7,6},{8,9},{9,8},{10,11... | collective-permute-start | bytes 1966088 | tf_op jit(solution)/shard_map/ppermute | solution.py:407
  273.8 3.0 %finish.1 = (bf16[128,5120]{1,0:T(8,128)(2,1)}, f32[64,5120]{1,0:T(8,128)}) custom-call(s32[1]{0:T(128)} %bitcast.flag, bf16[128,5120]{1,0:T(8,128)(2,1)S(1)} %bitcast.77, bf16[128,5120]{1,0:T(8,128)(2,1)S(1)} %bitcast.79, f32[16,80,128]{2,1,0:T(8,128)S(1)} %all_to_all.41.own, f32[16,80,128]{2,1,0:T(8,128)S(1)} %collective-permute-done.21.other, ...), custom_call_target="tpu_custom_call" | custom-call | tf_op jit(solution)/shard_map/finish/pallas_call | solution.py:387
  (63 shorter events, 21.2 us)
Async XLA Ops:
  44.9 17.5 %collective-permute-start.1 = (f32[328,128]{1,0:T(8,128)S(1)}, f32[328,128]{1,0:T(8,128)S(1)}, u32[]{:S(2)}, u32[]{:S(2)}) collective-permute-start(f32[328,128]{1,0:T(8,128)S(1)} %reduce_sum.27), channel_id=1, source_target_pairs={{0,1},{1,0},{2,3},{3,2},{4,5},{5,4},{6,7},{7,6},{8,9},{9,8},{10,11... | collective-permute-start | bytes 503816 | tf_op jit(solution)/shard_map/ppermute | solution.py:407
  50.9 14.1 %collective-permute-start = (f32[328,128]{1,0:T(8,128)S(1)}, f32[328,128]{1,0:T(8,128)S(1)}, u32[]{:S(2)}, u32[]{:S(2)}) collective-permute-start(f32[328,128]{1,0:T(8,128)S(1)} %reduce_sum.27), channel_id=1, source_target_pairs={{0,2},{2,4},{4,6},{6,8},{8,10},{10,12},{12,14},{14,16},{16,18},{18... | collective-permute-start | bytes 503816 | tf_op jit(solution)/shard_map/ppermute | solution.py:416
  62.4 7.3 %collective-permute-start.2 = (f32[328,128]{1,0:T(8,128)S(1)}, f32[328,128]{1,0:T(8,128)S(1)}, u32[]{:S(2)}, u32[]{:S(2)}) collective-permute-start(f32[328,128]{1,0:T(8,128)S(1)} %collective-permute-done.1), channel_id=1, source_target_pairs={{0,2},{2,4},{4,6},{6,8},{8,10},{10,12},{12,14},{14,16},{16,18},{18... | collective-permute-start | bytes 503816 | tf_op jit(solution)/shard_map/ppermute | solution.py:416
  65.1 7.3 %collective-permute-start.3 = (f32[328,128]{1,0:T(8,128)S(1)}, f32[328,128]{1,0:T(8,128)S(1)}, u32[]{:S(2)}, u32[]{:S(2)}) collective-permute-start(f32[328,128]{1,0:T(8,128)S(1)} %collective-permute-done), channel_id=1, source_target_pairs={{0,2},{2,4},{4,6},{6,8},{8,10},{10,12},{12,14},{14,16},{16,18},{18... | collective-permute-start | bytes 503816 | tf_op jit(solution)/shard_map/ppermute | solution.py:416
  69.7 7.3 %collective-permute-start.4 = (f32[328,128]{1,0:T(8,128)S(1)}, f32[328,128]{1,0:T(8,128)S(1)}, u32[]{:S(2)}, u32[]{:S(2)}) collective-permute-start(f32[328,128]{1,0:T(8,128)S(1)} %collective-permute-done.2), channel_id=1, source_target_pairs={{0,2},{2,4},{4,6},{6,8},{8,10},{10,12},{12,14},{14,16},{16,18},{18... | collective-permute-start | bytes 503816 | tf_op jit(solution)/shard_map/ppermute | solution.py:416
  72.4 7.3 %collective-permute-start.5 = (f32[328,128]{1,0:T(8,128)S(1)}, f32[328,128]{1,0:T(8,128)S(1)}, u32[]{:S(2)}, u32[]{:S(2)}) collective-permute-start(f32[328,128]{1,0:T(8,128)S(1)} %collective-permute-done.3), channel_id=1, source_target_pairs={{0,2},{2,4},{4,6},{6,8},{8,10},{10,12},{12,14},{14,16},{16,18},{18... | collective-permute-start | bytes 503816 | tf_op jit(solution)/shard_map/ppermute | solution.py:416
  77.0 7.3 %collective-permute-start.6 = (f32[328,128]{1,0:T(8,128)S(1)}, f32[328,128]{1,0:T(8,128)S(1)}, u32[]{:S(2)}, u32[]{:S(2)}) collective-permute-start(f32[328,128]{1,0:T(8,128)S(1)} %collective-permute-done.4), channel_id=1, source_target_pairs={{0,2},{2,4},{4,6},{6,8},{8,10},{10,12},{12,14},{14,16},{16,18},{18... | collective-permute-start | bytes 503816 | tf_op jit(solution)/shard_map/ppermute | solution.py:416
  79.7 7.3 %collective-permute-start.7 = (f32[328,128]{1,0:T(8,128)S(1)}, f32[328,128]{1,0:T(8,128)S(1)}, u32[]{:S(2)}, u32[]{:S(2)}) collective-permute-start(f32[328,128]{1,0:T(8,128)S(1)} %collective-permute-done.5), channel_id=1, source_target_pairs={{0,2},{2,4},{4,6},{6,8},{8,10},{10,12},{12,14},{14,16},{16,18},{18... | collective-permute-start | bytes 503816 | tf_op jit(solution)/shard_map/ppermute | solution.py:416
  84.3 7.3 %collective-permute-start.8 = (f32[328,128]{1,0:T(8,128)S(1)}, f32[328,128]{1,0:T(8,128)S(1)}, u32[]{:S(2)}, u32[]{:S(2)}) collective-permute-start(f32[328,128]{1,0:T(8,128)S(1)} %collective-permute-done.6), channel_id=1, source_target_pairs={{0,2},{2,4},{4,6},{6,8},{8,10},{10,12},{12,14},{14,16},{16,18},{18... | collective-permute-start | bytes 503816 | tf_op jit(solution)/shard_map/ppermute | solution.py:416
  87.0 7.3 %collective-permute-start.9 = (f32[328,128]{1,0:T(8,128)S(1)}, f32[328,128]{1,0:T(8,128)S(1)}, u32[]{:S(2)}, u32[]{:S(2)}) collective-permute-start(f32[328,128]{1,0:T(8,128)S(1)} %collective-permute-done.7), channel_id=1, source_target_pairs={{0,2},{2,4},{4,6},{6,8},{8,10},{10,12},{12,14},{14,16},{16,18},{18... | collective-permute-start | bytes 503816 | tf_op jit(solution)/shard_map/ppermute | solution.py:416
  91.7 7.3 %collective-permute-start.10 = (f32[328,128]{1,0:T(8,128)S(1)}, f32[328,128]{1,0:T(8,128)S(1)}, u32[]{:S(2)}, u32[]{:S(2)}) collective-permute-start(f32[328,128]{1,0:T(8,128)S(1)} %collective-permute-done.8), channel_id=1, source_target_pairs={{0,2},{2,4},{4,6},{6,8},{8,10},{10,12},{12,14},{14,16},{16,18},{18... | collective-permute-start | bytes 503816 | tf_op jit(solution)/shard_map/ppermute | solution.py:416
  94.3 7.3 %collective-permute-start.11 = (f32[328,128]{1,0:T(8,128)S(1)}, f32[328,128]{1,0:T(8,128)S(1)}, u32[]{:S(2)}, u32[]{:S(2)}) collective-permute-start(f32[328,128]{1,0:T(8,128)S(1)} %collective-permute-done.9), channel_id=1, source_target_pairs={{0,2},{2,4},{4,6},{6,8},{8,10},{10,12},{12,14},{14,16},{16,18},{18... | collective-permute-start | bytes 503816 | tf_op jit(solution)/shard_map/ppermute | solution.py:416
  99.0 7.3 %collective-permute-start.12 = (f32[328,128]{1,0:T(8,128)S(1)}, f32[328,128]{1,0:T(8,128)S(1)}, u32[]{:S(2)}, u32[]{:S(2)}) collective-permute-start(f32[328,128]{1,0:T(8,128)S(1)} %collective-permute-done.10), channel_id=1, source_target_pairs={{0,2},{2,4},{4,6},{6,8},{8,10},{10,12},{12,14},{14,16},{16,18},{18... | collective-permute-start | bytes 503816 | tf_op jit(solution)/shard_map/ppermute | solution.py:416
  101.6 7.3 %collective-permute-start.13 = (f32[328,128]{1,0:T(8,128)S(1)}, f32[328,128]{1,0:T(8,128)S(1)}, u32[]{:S(2)}, u32[]{:S(2)}) collective-permute-start(f32[328,128]{1,0:T(8,128)S(1)} %collective-permute-done.11), channel_id=1, source_target_pairs={{0,2},{2,4},{4,6},{6,8},{8,10},{10,12},{12,14},{14,16},{16,18},{18... | collective-permute-start | bytes 503816 | tf_op jit(solution)/shard_map/ppermute | solution.py:416
  106.3 7.3 %collective-permute-start.14 = (f32[328,128]{1,0:T(8,128)S(1)}, f32[328,128]{1,0:T(8,128)S(1)}, u32[]{:S(2)}, u32[]{:S(2)}) collective-permute-start(f32[328,128]{1,0:T(8,128)S(1)} %collective-permute-done.12), channel_id=1, source_target_pairs={{0,2},{2,4},{4,6},{6,8},{8,10},{10,12},{12,14},{14,16},{16,18},{18... | collective-permute-start | bytes 503816 | tf_op jit(solution)/shard_map/ppermute | solution.py:416
  108.9 7.3 %collective-permute-start.15 = (f32[328,128]{1,0:T(8,128)S(1)}, f32[328,128]{1,0:T(8,128)S(1)}, u32[]{:S(2)}, u32[]{:S(2)}) collective-permute-start(f32[328,128]{1,0:T(8,128)S(1)} %collective-permute-done.13), channel_id=1, source_target_pairs={{1,31},{3,1},{5,3},{7,5},{9,7},{11,9},{13,11},{15,13},{17,15},{19,... | collective-permute-start | bytes 503816 | tf_op jit(solution)/shard_map/ppermute | solution.py:416
  113.6 6.1 %collective-permute-start.16 = (f32[328,128]{1,0:T(8,128)S(1)}, f32[328,128]{1,0:T(8,128)S(1)}, u32[]{:S(2)}, u32[]{:S(2)}) collective-permute-start(f32[328,128]{1,0:T(8,128)S(1)} %collective-permute-done.14), channel_id=1, source_target_pairs={{1,31},{3,1},{5,3},{7,5},{9,7},{11,9},{13,11},{15,13},{17,15},{19,... | collective-permute-start | bytes 503816 | tf_op jit(solution)/shard_map/ppermute | solution.py:416
  120.3 20.2 %copy-start.3 = (f32[8,2,320,128]{3,2,1,0:T(8,128)}, f32[8,2,320,128]{3,2,1,0:T(8,128)S(1)}, u32[]{:S(2)}) copy-start(f32[8,2,320,128]{3,2,1,0:T(8,128)S(1)} %slice.9.total) | copy-start | bytes 7864324
  120.3 20.1 %collective-permute-start.18 = (f32[8,2,320,128]{3,2,1,0:T(8,128)S(1)}, f32[8,2,320,128]{3,2,1,0:T(8,128)}, u32[]{:S(2)}, u32[]{:S(2)}) collective-permute-start(f32[8,2,320,128]{3,2,1,0:T(8,128)S(1)} %slice.9.total), channel_id=1, source_target_pairs={{0,1},{1,0},{2,3},{3,2},{4,5},{5,4},{6,7},{7,6},{8,9},{9,8},{10,11... | collective-permute-start | bytes 7864328 | tf_op jit(solution)/shard_map/ppermute | solution.py:407
  136.2 9.1 %collective-permute-start.17 = (f32[16,64,128]{2,1,0:T(8,128)S(1)}, f32[16,64,128]{2,1,0:T(8,128)}, u32[]{:S(2)}, u32[]{:S(2)}) collective-permute-start(f32[16,64,128]{2,1,0:T(8,128)S(1)} %bitcast.80), channel_id=1, source_target_pairs={{0,1},{1,0},{2,3},{3,2},{4,5},{5,4},{6,7},{7,6},{8,9},{9,8},{10,11... | collective-permute-start | bytes 1572872 | tf_op jit(solution)/shard_map/ppermute | solution.py:407
  140.5 1.7 copy-start.4
  145.3 13.4 %copy-start = (bf16[320,4096]{1,0:T(8,128)(2,1)}, bf16[320,4096]{1,0:T(8,128)(2,1)S(1)}, u32[]{:S(2)}) copy-start(bf16[320,4096]{1,0:T(8,128)(2,1)S(1)} %get-tuple-element.9.low_in) | copy-start | bytes 7864324
  185.1 6.9 %collective-permute-start.19 = (f32[16,64,128]{2,1,0:T(8,128)S(1)}, f32[16,64,128]{2,1,0:T(8,128)S(1)}, u32[]{:S(2)}, u32[]{:S(2)}) collective-permute-start(f32[16,64,128]{2,1,0:T(8,128)S(1)} %all_to_all.38.own), channel_id=1, source_target_pairs={{0,1},{1,0},{2,3},{3,2},{4,5},{5,4},{6,7},{7,6},{8,9},{9,8},{10,11... | collective-permute-start | bytes 1572872 | tf_op jit(solution)/shard_map/ppermute | solution.py:407
  192.0 1.7 copy-start.1
  232.4 6.8 %collective-permute-start.20 = (f32[16,64,128]{2,1,0:T(8,128)S(1)}, f32[16,64,128]{2,1,0:T(8,128)}, u32[]{:S(2)}, u32[]{:S(2)}) collective-permute-start(f32[16,64,128]{2,1,0:T(8,128)S(1)} %all_to_all.40.own), channel_id=1, source_target_pairs={{0,1},{1,0},{2,3},{3,2},{4,5},{5,4},{6,7},{7,6},{8,9},{9,8},{10,11... | collective-permute-start | bytes 1572872 | tf_op jit(solution)/shard_map/ppermute | solution.py:407
  239.2 1.7 copy-start.2
  240.9 32.9 %copy-start.5 = (bf16[1,128,5120]{2,1,0:T(8,128)(2,1)S(1)}, bf16[1,128,5120]{2,1,0:T(8,128)(2,1)}, u32[]{:S(2)}) copy-start(bf16[1,128,5120]{2,1,0:T(8,128)(2,1)} %param.3) | copy-start | bytes 3932164
  240.9 32.9 %copy-start.6 = (bf16[1,128,5120]{2,1,0:T(8,128)(2,1)S(1)}, bf16[1,128,5120]{2,1,0:T(8,128)(2,1)}, u32[]{:S(2)}) copy-start(bf16[1,128,5120]{2,1,0:T(8,128)(2,1)} %param.4) | copy-start | bytes 3932164
  268.4 5.3 %collective-permute-start.21 = (f32[16,80,128]{2,1,0:T(8,128)S(1)}, f32[16,80,128]{2,1,0:T(8,128)S(1)}, u32[]{:S(2)}, u32[]{:S(2)}) collective-permute-start(f32[16,80,128]{2,1,0:T(8,128)S(1)} %all_to_all.41.own), channel_id=1, source_target_pairs={{0,1},{1,0},{2,3},{3,2},{4,5},{5,4},{6,7},{7,6},{8,9},{9,8},{10,11... | collective-permute-start | bytes 1966088 | tf_op jit(solution)/shard_map/ppermute | solution.py:407

commit v7 on v6

--- a/solution.py
+++ b/solution.py
@@ -39,7 +39,7 @@
     return pltpu.CompilerParams(vmem_limit_bytes=limit)
 
 
-def start_kernel(grads, errors, q_start, out, g_held, e_held, q_held, sems):
+def start_kernel(grads, errors, q_start, result, g_held, e_held, q_held, out, sems, out_sems):
     reps, tall, rows = out.shape
     rank, width = q_start.shape
     cut = width // reps
@@ -54,6 +54,7 @@
         for load in loads[-1]:
             load.start()
     left = jnp.zeros((2 * rank, rows), F32)
+    stores = []
     for i, span in enumerate(spans):
         for load in loads[i]:
             load.wait()
@@ -61,6 +62,9 @@
         turned = (g.astype(F32) + e.astype(F32)).T
         out[2 * i, :cut, :] = turned[:cut]
         out[2 * i + 1, :cut, :] = turned[cut:]
+        block = (pl.ds(2 * i, 2), pl.ds(0, cut))
+        stores.append(pltpu.make_async_copy(out.at[block], result.at[block], out_sems.at[i]))
+        stores[-1].start()
         high, low = split2(q_held[:, span])
         both = jnp.concatenate([high, low], axis=0)
         left = left + (dot(both, g, NT) + dot(both, e, NT))
@@ -68,6 +72,11 @@
     for i in range(reps):
         out[i, cut : cut + extra, :] = left[extra * i : extra * (i + 1)]
         out[i, cut + extra :, :] = jnp.zeros((tall - cut - extra, rows), F32)
+    block = (pl.ds(0, reps), pl.ds(cut, tall - cut))
+    stores.append(pltpu.make_async_copy(out.at[block], result.at[block], out_sems.at[reps // 2]))
+    stores[-1].start()
+    for store in stores:
+        store.wait()
 
 
 def start(grads, errors, q_start, reps):
@@ -76,13 +85,15 @@
     return pl.pallas_call(
         start_kernel,
         in_specs=[HBM_SPEC] * 3,
-        out_specs=VMEM_SPEC,
+        out_specs=HBM_SPEC,
         out_shape=jax.ShapeDtypeStruct((reps, tall, rows), F32),
         scratch_shapes=[
             pltpu.VMEM(grads.shape, BF16),
             pltpu.VMEM(errors.shape, BF16),
             pltpu.VMEM(q_start.shape, F32),
+            pltpu.VMEM((reps, tall, rows), F32),
             pltpu.SemaphoreType.DMA((3, reps // 2)),
+            pltpu.SemaphoreType.DMA((reps // 2 + 1,)),
         ],
         compiler_params=params(3 * VMEM),
         name="start",
@@ -237,7 +248,7 @@
         out[2 * j + 1] = x[:, rows:]
 
 
-def parts_kernel(info, total, total_other, high, low):
+def first_kernel(scale, info, own, other, total, total_other, out, high, low, held):
     half = total.shape[0]
     for mine, blocks in ((True, total), (False, total_other)):
         at = planes(info, 2 * half, mine)
@@ -247,32 +258,18 @@
                 side = core if stream == 0 else 1 - core
                 span = pl.ds(pl.multiple_of(at(j) + side * LANES, LANES), LANES)
                 high[:, span], low[:, span] = split2(blocks[j, stream])
-
-
-def load_parts(high_in, low_in, high, low, sems):
-    loads = [
-        pltpu.make_async_copy(high_in, high, sems.at[0]),
-        pltpu.make_async_copy(low_in, low, sems.at[1]),
-    ]
-    for load in loads:
-        load.start()
-    return loads
-
-
-def step_kernel(scale, info, own, other, high_in, low_in, out, held, high, low, sems):
-    loads = load_parts(high_in, low_in, high, low, sems)
     second = orthonormal(info, own, other, held)
-    for load in loads:
-        load.wait()
     next_left(info, right_factor(scale, second, held, high, low), high, low, out)
 
 
-def last_kernel(scale, info, own, other, high_in, low_in, out, basis, held, high, low, sems):
-    loads = load_parts(high_in, low_in, high, low, sems)
+def step_kernel(scale, info, own, other, high, low, out, held):
+    second = orthonormal(info, own, other, held)
+    next_left(info, right_factor(scale, second, held, high, low), high, low, out)
+
+
+def last_kernel(scale, info, own, other, high, low, out, basis, held):
     length, rank, rows = own.shape
     second = orthonormal(info, own, other, held)
-    for load in loads:
-        load.wait()
     q = right_factor(scale, second, held, high, low)
     half = rank // 2
     quarter = half // 2
@@ -288,31 +285,30 @@
     basis[...] = y[:rank] + (y[rank : 2 * rank] + y[2 * rank :])
 
 
-def scratch(length, rank, cut):
-    n = 2 * length * LANES
-    return [pltpu.VMEM((4 * rank, n), BF16)], [pltpu.VMEM((cut, n), BF16)] * 2
-
-
-def parts(info, total, total_other):
-    half, cores, cut, rows = total.shape
-    whole = jax.ShapeDtypeStruct((cut, 2 * half * cores * rows), BF16)
+def held_scratch(own):
+    length, rank, rows = own.shape
+    return [pltpu.VMEM((4 * rank, 2 * length * rows), BF16)]
+
+
+def first(scale, info, own, other, total, total_other):
+    length, rank, rows = own.shape
+    whole = jax.ShapeDtypeStruct((total.shape[2], 2 * length * rows), BF16)
     return pl.pallas_call(
-        parts_kernel,
-        in_specs=[SMEM_SPEC, VMEM_SPEC, VMEM_SPEC],
-        out_shape=[whole, whole],
+        functools.partial(first_kernel, scale),
+        in_specs=[SMEM_SPEC] + [VMEM_SPEC] * 4,
+        out_shape=[jax.ShapeDtypeStruct(own.shape, F32), whole, whole],
+        scratch_shapes=held_scratch(own),
         compiler_params=params(),
-        name="parts",
-    )(info, total, total_other)
+        name="first",
+    )(info, own, other, total, total_other)
 
 
 def step(scale, info, own, other, high, low):
-    length, rank, rows = own.shape
-    held, both = scratch(length, rank, high.shape[0])
     return pl.pallas_call(
         functools.partial(step_kernel, scale),
-        in_specs=[SMEM_SPEC, VMEM_SPEC, VMEM_SPEC, HBM_SPEC, HBM_SPEC],
+        in_specs=[SMEM_SPEC] + [VMEM_SPEC] * 4,
         out_shape=jax.ShapeDtypeStruct(own.shape, F32),
-        scratch_shapes=held + both + [pltpu.SemaphoreType.DMA((2,))],
+        scratch_shapes=held_scratch(own),
         compiler_params=params(),
         name="step",
     )(info, own, other, high, low)
@@ -320,13 +316,12 @@
 
 def last(scale, info, own, other, high, low):
     length, rank, rows = own.shape
-    held, both = scratch(length, rank, high.shape[0])
     shapes = [(2, 5 * rank // 4, LANES), (rank, rows)]
     return pl.pallas_call(
         functools.partial(last_kernel, scale),
-        in_specs=[SMEM_SPEC, VMEM_SPEC, VMEM_SPEC, HBM_SPEC, HBM_SPEC],
+        in_specs=[SMEM_SPEC] + [VMEM_SPEC] * 4,
         out_shape=[jax.ShapeDtypeStruct(x, F32) for x in shapes],
-        scratch_shapes=held + both + [pltpu.SemaphoreType.DMA((2,))],
+        scratch_shapes=held_scratch(own),
         compiler_params=params(),
         name="last",
     )(info, own, other, high, low)
@@ -438,10 +433,11 @@
     piece = jnp.where(core == 0, piece, piece[:, ::-1]).reshape(length * extra, rows)
     own = gather(piece, "rep", reps).reshape(reps, length, extra, rows)
     own = own.transpose(1, 0, 2, 3).reshape(length, rank, rows)
-    high, low = parts(info, total, swap_cores(total))
+    partial, high, low = first(scale, info, own, swap_cores(own), total, swap_cores(total))
     for turn in range(ITERS - 1):
-        partial = step(scale, info, own, swap_cores(own), high, low)
         own = gather(jnp.sum(exchange(partial, "rep"), axis=0), "rep", reps)
+        if turn < ITERS - 2:
+            partial = step(scale, info, own, swap_cores(own), high, low)
     part_q, basis = last(scale, info, own, swap_cores(own), high, low)
     own_q = gather(lax.dynamic_index_in_dim(part_q, core, 0, False), "rep", reps)
     new_errors, factor_q = finish(flag, grads, errors, own_q, swap_cores(own_q), basis)

time: 278 us -> 269 us (0.968)
  Pallas kernels: 49.4 us -> 37.8 us
    pallas_call x2 -> x1, Pallas kernels: 25.8 us -> 9.19 us  [step(): pl.pallas_call(functools.partial(step_kernel, scale), in_specs=[SMEM_SPEC...]
    pallas_call x2, Pallas kernels: 8.05 us -> 16.5 us  [the longest x1 12.2 us: first(): pl.pallas_call(functools.partial(first_kernel, scale), in_specs=[SMEM_SPE...]
    pallas_call x1, Pallas kernels: 12.5 us -> 9.12 us  [last(): pl.pallas_call(functools.partial(last_kernel, scale), in_specs=[SMEM_SPEC...]
  transfers between devices with their start and end apart: 22 -> 22, of which waited for: 4 -> 5; matrix products, arithmetic and copies ran while one was open for 0% -> 0% of each run, Pallas kernels for 1% -> 0%
where the time goes in v7:
time: 269 us; the launch traced here: 268 us
  blocking collectives  120 us (45%)
  starting transfers between devices  91.3 us (34%)
  Pallas kernels  37.8 us (14%)
  waiting for transfers between devices  9.41 us (3%)
  local copies, waits for them, and re-layouts  7.71 us (3%)
    all_to_all x7, blocking collectives, exchange(): return lax.all_to_all(chunks, axis, 0, 0)  120 us
    ppermute x16, starting transfers between devices, ring(): lax.ppermute(blocks[-1], ('z', 'core'), up + down if s < half - 1 else down)  65 us
    ppermute x6, starting transfers between devices, swap_cores(): return lax.ppermute(block, 'core', [(0, 1), (1, 0)])  26.3 us
    pallas_call x1, Pallas kernels, first(): pl.pallas_call(functools.partial(first_kernel, scale), in_specs=[SMEM_SPE...  12.2 us
    pallas_call x1, Pallas kernels, step(): pl.pallas_call(functools.partial(step_kernel, scale), in_specs=[SMEM_SPEC...  9.19 us
    pallas_call x1, Pallas kernels, last(): pl.pallas_call(functools.partial(last_kernel, scale), in_specs=[SMEM_SPEC...  9.12 us
    unnamed x14, local copies, waits for them, and re-layouts  6.73 us
    ppermute x6, waiting for transfers between devices, swap_cores(): return lax.ppermute(block, 'core', [(0, 1), (1, 0)])  6.03 us
  transfers between devices with their start and end apart: 22, of which 5 were waited for; matrix products, arithmetic and copies ran while one was open for 0% of the time, Pallas kernels for 0%

profile of v7, /device:TPU:1, one launch (start us, length us, event | category | flops | bytes accessed | tf_op | source)
XLA Modules:
  0.0 267.6 jit_solution(8985701536704789098)
XLA Ops:
  0.6 4.3 %start.1 = f32[16,328,128]{2,1,0:T(8,128)} custom-call(bf16[128,5120]{1,0:T(8,128)(2,1)} %bitcast.76, bf16[128,5120]{1,0:T(8,128)(2,1)} %bitcast.78, f32[64,5120]{1,0:T(8,128)} %q_start.1), custom_call_target="tpu_custom_call" | custom-call | tf_op jit(solution)/shard_map/start/pallas_call | solution.py:85
  4.9 39.2 %all_to_all.35 = f32[16,328,128]{2,1,0:T(8,128)S(1)} all-to-all(f32[16,328,128]{2,1,0:T(8,128)} %start.1), channel_id=1, replica_groups=mesh['rep'=16,'z'=16,'core'=2] {'rep'}, dimensions={0} | all-to-all | bytes 5373952 | tf_op jit(solution)/shard_map/all_to_all | solution.py:394
  44.2 6.0 %collective-permute-start.1 = (f32[328,128]{1,0:T(8,128)S(1)}, f32[328,128]{1,0:T(8,128)S(1)}, u32[]{:S(2)}, u32[]{:S(2)}) collective-permute-start(f32[328,128]{1,0:T(8,128)S(1)} %reduce_sum.27), channel_id=1, source_target_pairs={{0,1},{1,0},{2,3},{3,2},{4,5},{5,4},{6,7},{7,6},{8,9},{9,8},{10,11... | collective-permute-start | bytes 503816 | tf_op jit(solution)/shard_map/ppermute | solution.py:402
  50.2 11.5 %collective-permute-start = (f32[328,128]{1,0:T(8,128)S(1)}, f32[328,128]{1,0:T(8,128)S(1)}, u32[]{:S(2)}, u32[]{:S(2)}) collective-permute-start(f32[328,128]{1,0:T(8,128)S(1)} %reduce_sum.27), channel_id=1, source_target_pairs={{0,2},{2,4},{4,6},{6,8},{8,10},{10,12},{12,14},{14,16},{16,18},{18... | collective-permute-start | bytes 503816 | tf_op jit(solution)/shard_map/ppermute | solution.py:411
  64.3 4.6 %collective-permute-start.3 = (f32[328,128]{1,0:T(8,128)S(1)}, f32[328,128]{1,0:T(8,128)S(1)}, u32[]{:S(2)}, u32[]{:S(2)}) collective-permute-start(f32[328,128]{1,0:T(8,128)S(1)} %collective-permute-done), channel_id=1, source_target_pairs={{0,2},{2,4},{4,6},{6,8},{8,10},{10,12},{12,14},{14,16},{16,18},{18... | collective-permute-start | bytes 503816 | tf_op jit(solution)/shard_map/ppermute | solution.py:411
  69.0 2.6 collective-permute-start.4
  71.6 4.6 %collective-permute-start.5 = (f32[328,128]{1,0:T(8,128)S(1)}, f32[328,128]{1,0:T(8,128)S(1)}, u32[]{:S(2)}, u32[]{:S(2)}) collective-permute-start(f32[328,128]{1,0:T(8,128)S(1)} %collective-permute-done.3), channel_id=1, source_target_pairs={{0,2},{2,4},{4,6},{6,8},{8,10},{10,12},{12,14},{14,16},{16,18},{18... | collective-permute-start | bytes 503816 | tf_op jit(solution)/shard_map/ppermute | solution.py:411
  76.3 2.6 collective-permute-start.6
  79.0 4.6 %collective-permute-start.7 = (f32[328,128]{1,0:T(8,128)S(1)}, f32[328,128]{1,0:T(8,128)S(1)}, u32[]{:S(2)}, u32[]{:S(2)}) collective-permute-start(f32[328,128]{1,0:T(8,128)S(1)} %collective-permute-done.5), channel_id=1, source_target_pairs={{0,2},{2,4},{4,6},{6,8},{8,10},{10,12},{12,14},{14,16},{16,18},{18... | collective-permute-start | bytes 503816 | tf_op jit(solution)/shard_map/ppermute | solution.py:411
  83.6 2.6 collective-permute-start.8
  86.3 4.6 %collective-permute-start.9 = (f32[328,128]{1,0:T(8,128)S(1)}, f32[328,128]{1,0:T(8,128)S(1)}, u32[]{:S(2)}, u32[]{:S(2)}) collective-permute-start(f32[328,128]{1,0:T(8,128)S(1)} %collective-permute-done.7), channel_id=1, source_target_pairs={{0,2},{2,4},{4,6},{6,8},{8,10},{10,12},{12,14},{14,16},{16,18},{18... | collective-permute-start | bytes 503816 | tf_op jit(solution)/shard_map/ppermute | solution.py:411
  90.9 2.6 collective-permute-start.10
  93.6 4.6 %collective-permute-start.11 = (f32[328,128]{1,0:T(8,128)S(1)}, f32[328,128]{1,0:T(8,128)S(1)}, u32[]{:S(2)}, u32[]{:S(2)}) collective-permute-start(f32[328,128]{1,0:T(8,128)S(1)} %collective-permute-done.9), channel_id=1, source_target_pairs={{0,2},{2,4},{4,6},{6,8},{8,10},{10,12},{12,14},{14,16},{16,18},{18... | collective-permute-start | bytes 503816 | tf_op jit(solution)/shard_map/ppermute | solution.py:411
  98.2 2.6 collective-permute-start.12
  100.9 4.6 %collective-permute-start.13 = (f32[328,128]{1,0:T(8,128)S(1)}, f32[328,128]{1,0:T(8,128)S(1)}, u32[]{:S(2)}, u32[]{:S(2)}) collective-permute-start(f32[328,128]{1,0:T(8,128)S(1)} %collective-permute-done.11), channel_id=1, source_target_pairs={{0,2},{2,4},{4,6},{6,8},{8,10},{10,12},{12,14},{14,16},{16,18},{18... | collective-permute-start | bytes 503816 | tf_op jit(solution)/shard_map/ppermute | solution.py:411
  105.5 2.6 collective-permute-start.14
  108.2 4.6 %collective-permute-start.15 = (f32[328,128]{1,0:T(8,128)S(1)}, f32[328,128]{1,0:T(8,128)S(1)}, u32[]{:S(2)}, u32[]{:S(2)}) collective-permute-start(f32[328,128]{1,0:T(8,128)S(1)} %collective-permute-done.13), channel_id=1, source_target_pairs={{1,31},{3,1},{5,3},{7,5},{9,7},{11,9},{13,11},{15,13},{17,15},{19,... | collective-permute-start | bytes 503816 | tf_op jit(solution)/shard_map/ppermute | solution.py:411
  115.6 3.3 %collective-permute-done.16 = f32[328,128]{1,0:T(8,128)S(1)} collective-permute-done((f32[328,128]{1,0:T(8,128)S(1)}, f32[328,128]{1,0:T(8,128)S(1)}, u32[]{:S(2)}, u32[]{:S(2)}) %collective-permute-start.16) | collective-permute-done | bytes 167968 | tf_op jit(solution)/shard_map/ppermute | solution.py:411
  121.6 13.3 %all_to_all.36 = f32[16,64,128]{2,1,0:T(8,128)S(1)} all-to-all(f32[16,64,128]{2,1,0:T(8,128)S(1)} %broadcast_in_dim.15), channel_id=1, replica_groups=mesh['rep'=16,'z'=16,'core'=2] {'rep'}, dimensions={0} | all-to-all | bytes 1048576 | tf_op jit(solution)/shard_map/all_to_all | solution.py:394
  135.4 4.2 %collective-permute-start.17 = (f32[16,64,128]{2,1,0:T(8,128)S(1)}, f32[16,64,128]{2,1,0:T(8,128)}, u32[]{:S(2)}, u32[]{:S(2)}) collective-permute-start(f32[16,64,128]{2,1,0:T(8,128)S(1)} %bitcast.80), channel_id=1, source_target_pairs={{0,1},{1,0},{2,3},{3,2},{4,5},{5,4},{6,7},{7,6},{8,9},{9,8},{10,11... | collective-permute-start | bytes 1572872 | tf_op jit(solution)/shard_map/ppermute | solution.py:402
  142.9 12.2 %first.1 = (f32[16,64,128]{2,1,0:T(8,128)S(1)}, bf16[320,4096]{1,0:T(8,128)(2,1)S(1)}, bf16[320,4096]{1,0:T(8,128)(2,1)S(1)}) custom-call(s32[2]{0:T(128)S(1)} %pad_add_fusion.info, f32[16,64,128]{2,1,0:T(8,128)S(1)} %bitcast.81, f32[16,64,128]{2,1,0:T(8,128)} %collective-permute-done.17.other, f32[8,2,320,128]{3,2,1,0:T(8,128)S(1)} %copy-done.4, ...), custom_call_target="tpu_custom_call" | custom-call | tf_op jit(solution)/shard_map/first/pallas_call | solution.py:296
  156.6 13.3 %all_to_all.37 = f32[16,64,128]{2,1,0:T(8,128)S(1)} all-to-all(f32[16,64,128]{2,1,0:T(8,128)S(1)} %get-tuple-element.9), channel_id=1, replica_groups=mesh['rep'=16,'z'=16,'core'=2] {'rep'}, dimensions={0} | all-to-all | bytes 1048576 | tf_op jit(solution)/shard_map/all_to_all | solution.py:394
  170.1 12.7 %all_to_all.38.own = f32[16,64,128]{2,1,0:T(8,128)S(1)} all-to-all(f32[16,64,128]{2,1,0:T(8,128)S(1)} %broadcast_in_dim.32), channel_id=1, replica_groups=mesh['rep'=16,'z'=16,'core'=2] {'rep'}, dimensions={0} | all-to-all | bytes 1048576 | tf_op jit(solution)/shard_map/all_to_all | solution.py:394
  182.8 5.4 %collective-permute-start.19 = (f32[16,64,128]{2,1,0:T(8,128)S(1)}, f32[16,64,128]{2,1,0:T(8,128)S(1)}, u32[]{:S(2)}, u32[]{:S(2)}) collective-permute-start(f32[16,64,128]{2,1,0:T(8,128)S(1)} %all_to_all.38.own), channel_id=1, source_target_pairs={{0,1},{1,0},{2,3},{3,2},{4,5},{5,4},{6,7},{7,6},{8,9},{9,8},{10,11... | collective-permute-start | bytes 1572872 | tf_op jit(solution)/shard_map/ppermute | solution.py:402
  191.2 9.2 %step.1 = f32[16,64,128]{2,1,0:T(8,128)S(1)} custom-call(s32[2]{0:T(128)S(1)} %pad_add_fusion.info, f32[16,64,128]{2,1,0:T(8,128)S(1)} %all_to_all.38.own, f32[16,64,128]{2,1,0:T(8,128)S(1)} %collective-permute-done.19.other, bf16[320,4096]{1,0:T(8,128)(2,1)S(1)} %get-tuple-element.10.high, bf16[320,4096]{1,0:T(8,128)(2,1)S(1)} %copy-done.1), custom_call_target="tpu_custom_call" | custom-call | tf_op jit(solution)/shard_map/step/pallas_call | solution.py:307
  200.4 13.3 %all_to_all.39 = f32[16,64,128]{2,1,0:T(8,128)S(1)} all-to-all(f32[16,64,128]{2,1,0:T(8,128)S(1)} %step.1), channel_id=1, replica_groups=mesh['rep'=16,'z'=16,'core'=2] {'rep'}, dimensions={0} | all-to-all | bytes 1048576 | tf_op jit(solution)/shard_map/all_to_all | solution.py:394
  213.8 12.7 %all_to_all.40.own = f32[16,64,128]{2,1,0:T(8,128)S(1)} all-to-all(f32[16,64,128]{2,1,0:T(8,128)S(1)} %broadcast_in_dim.33), channel_id=1, replica_groups=mesh['rep'=16,'z'=16,'core'=2] {'rep'}, dimensions={0} | all-to-all | bytes 1048576 | tf_op jit(solution)/shard_map/all_to_all | solution.py:394
  226.5 5.2 %collective-permute-start.20 = (f32[16,64,128]{2,1,0:T(8,128)S(1)}, f32[16,64,128]{2,1,0:T(8,128)}, u32[]{:S(2)}, u32[]{:S(2)}) collective-permute-start(f32[16,64,128]{2,1,0:T(8,128)S(1)} %all_to_all.40.own), channel_id=1, source_target_pairs={{0,1},{1,0},{2,3},{3,2},{4,5},{5,4},{6,7},{7,6},{8,9},{9,8},{10,11... | collective-permute-start | bytes 1572872 | tf_op jit(solution)/shard_map/ppermute | solution.py:402
  235.1 9.1 %last.1 = (f32[2,80,128]{2,1,0:T(8,128)S(1)}, f32[64,128]{1,0:T(8,128)S(1)}) custom-call(s32[2]{0:T(128)S(1)} %pad_add_fusion.info, f32[16,64,128]{2,1,0:T(8,128)S(1)} %all_to_all.40.own, f32[16,64,128]{2,1,0:T(8,128)} %collective-permute-done.20.other, bf16[320,4096]{1,0:T(8,128)(2,1)S(1)} %get-tuple-element.10.high, bf16[320,4096]{1,0:T(8,128)(2,1)S(1)} %copy-done.2), custom_call_target="tpu_custom_call" | custom-call | tf_op jit(solution)/shard_map/last/pallas_call | solution.py:320
  244.3 15.0 %all_to_all.41.own = f32[16,80,128]{2,1,0:T(8,128)S(1)} all-to-all(f32[16,80,128]{2,1,0:T(8,128)S(1)} %broadcast_in_dim.35), channel_id=1, replica_groups=mesh['rep'=16,'z'=16,'core'=2] {'rep'}, dimensions={0} | all-to-all | bytes 1310720 | tf_op jit(solution)/shard_map/all_to_all | solution.py:394
  259.2 3.6 %collective-permute-start.21 = (f32[16,80,128]{2,1,0:T(8,128)S(1)}, f32[16,80,128]{2,1,0:T(8,128)S(1)}, u32[]{:S(2)}, u32[]{:S(2)}) collective-permute-start(f32[16,80,128]{2,1,0:T(8,128)S(1)} %all_to_all.41.own), channel_id=1, source_target_pairs={{0,1},{1,0},{2,3},{3,2},{4,5},{5,4},{6,7},{7,6},{8,9},{9,8},{10,11... | collective-permute-start | bytes 1966088 | tf_op jit(solution)/shard_map/ppermute | solution.py:402
  264.5 3.0 %finish.1 = (bf16[128,5120]{1,0:T(8,128)(2,1)}, f32[64,5120]{1,0:T(8,128)}) custom-call(s32[1]{0:T(128)} %bitcast.flag, bf16[128,5120]{1,0:T(8,128)(2,1)S(1)} %bitcast.77, bf16[128,5120]{1,0:T(8,128)(2,1)S(1)} %bitcast.79, f32[16,80,128]{2,1,0:T(8,128)S(1)} %all_to_all.41.own, f32[16,80,128]{2,1,0:T(8,128)S(1)} %collective-permute-done.21.other, ...), custom_call_target="tpu_custom_call" | custom-call | tf_op jit(solution)/shard_map/finish/pallas_call | solution.py:382
  (62 shorter events, 21.7 us)
Async XLA Ops:
  44.2 17.5 %collective-permute-start.1 = (f32[328,128]{1,0:T(8,128)S(1)}, f32[328,128]{1,0:T(8,128)S(1)}, u32[]{:S(2)}, u32[]{:S(2)}) collective-permute-start(f32[328,128]{1,0:T(8,128)S(1)} %reduce_sum.27), channel_id=1, source_target_pairs={{0,1},{1,0},{2,3},{3,2},{4,5},{5,4},{6,7},{7,6},{8,9},{9,8},{10,11... | collective-permute-start | bytes 503816 | tf_op jit(solution)/shard_map/ppermute | solution.py:402
  50.2 14.1 %collective-permute-start = (f32[328,128]{1,0:T(8,128)S(1)}, f32[328,128]{1,0:T(8,128)S(1)}, u32[]{:S(2)}, u32[]{:S(2)}) collective-permute-start(f32[328,128]{1,0:T(8,128)S(1)} %reduce_sum.27), channel_id=1, source_target_pairs={{0,2},{2,4},{4,6},{6,8},{8,10},{10,12},{12,14},{14,16},{16,18},{18... | collective-permute-start | bytes 503816 | tf_op jit(solution)/shard_map/ppermute | solution.py:411
  61.7 7.3 %collective-permute-start.2 = (f32[328,128]{1,0:T(8,128)S(1)}, f32[328,128]{1,0:T(8,128)S(1)}, u32[]{:S(2)}, u32[]{:S(2)}) collective-permute-start(f32[328,128]{1,0:T(8,128)S(1)} %collective-permute-done.1), channel_id=1, source_target_pairs={{0,2},{2,4},{4,6},{6,8},{8,10},{10,12},{12,14},{14,16},{16,18},{18... | collective-permute-start | bytes 503816 | tf_op jit(solution)/shard_map/ppermute | solution.py:411
  64.3 7.3 %collective-permute-start.3 = (f32[328,128]{1,0:T(8,128)S(1)}, f32[328,128]{1,0:T(8,128)S(1)}, u32[]{:S(2)}, u32[]{:S(2)}) collective-permute-start(f32[328,128]{1,0:T(8,128)S(1)} %collective-permute-done), channel_id=1, source_target_pairs={{0,2},{2,4},{4,6},{6,8},{8,10},{10,12},{12,14},{14,16},{16,18},{18... | collective-permute-start | bytes 503816 | tf_op jit(solution)/shard_map/ppermute | solution.py:411
  69.0 7.3 %collective-permute-start.4 = (f32[328,128]{1,0:T(8,128)S(1)}, f32[328,128]{1,0:T(8,128)S(1)}, u32[]{:S(2)}, u32[]{:S(2)}) collective-permute-start(f32[328,128]{1,0:T(8,128)S(1)} %collective-permute-done.2), channel_id=1, source_target_pairs={{0,2},{2,4},{4,6},{6,8},{8,10},{10,12},{12,14},{14,16},{16,18},{18... | collective-permute-start | bytes 503816 | tf_op jit(solution)/shard_map/ppermute | solution.py:411
  71.6 7.3 %collective-permute-start.5 = (f32[328,128]{1,0:T(8,128)S(1)}, f32[328,128]{1,0:T(8,128)S(1)}, u32[]{:S(2)}, u32[]{:S(2)}) collective-permute-start(f32[328,128]{1,0:T(8,128)S(1)} %collective-permute-done.3), channel_id=1, source_target_pairs={{0,2},{2,4},{4,6},{6,8},{8,10},{10,12},{12,14},{14,16},{16,18},{18... | collective-permute-start | bytes 503816 | tf_op jit(solution)/shard_map/ppermute | solution.py:411
  76.3 7.3 %collective-permute-start.6 = (f32[328,128]{1,0:T(8,128)S(1)}, f32[328,128]{1,0:T(8,128)S(1)}, u32[]{:S(2)}, u32[]{:S(2)}) collective-permute-start(f32[328,128]{1,0:T(8,128)S(1)} %collective-permute-done.4), channel_id=1, source_target_pairs={{0,2},{2,4},{4,6},{6,8},{8,10},{10,12},{12,14},{14,16},{16,18},{18... | collective-permute-start | bytes 503816 | tf_op jit(solution)/shard_map/ppermute | solution.py:411
  79.0 7.3 %collective-permute-start.7 = (f32[328,128]{1,0:T(8,128)S(1)}, f32[328,128]{1,0:T(8,128)S(1)}, u32[]{:S(2)}, u32[]{:S(2)}) collective-permute-start(f32[328,128]{1,0:T(8,128)S(1)} %collective-permute-done.5), channel_id=1, source_target_pairs={{0,2},{2,4},{4,6},{6,8},{8,10},{10,12},{12,14},{14,16},{16,18},{18... | collective-permute-start | bytes 503816 | tf_op jit(solution)/shard_map/ppermute | solution.py:411
  83.6 7.3 %collective-permute-start.8 = (f32[328,128]{1,0:T(8,128)S(1)}, f32[328,128]{1,0:T(8,128)S(1)}, u32[]{:S(2)}, u32[]{:S(2)}) collective-permute-start(f32[328,128]{1,0:T(8,128)S(1)} %collective-permute-done.6), channel_id=1, source_target_pairs={{0,2},{2,4},{4,6},{6,8},{8,10},{10,12},{12,14},{14,16},{16,18},{18... | collective-permute-start | bytes 503816 | tf_op jit(solution)/shard_map/ppermute | solution.py:411
  86.3 7.3 %collective-permute-start.9 = (f32[328,128]{1,0:T(8,128)S(1)}, f32[328,128]{1,0:T(8,128)S(1)}, u32[]{:S(2)}, u32[]{:S(2)}) collective-permute-start(f32[328,128]{1,0:T(8,128)S(1)} %collective-permute-done.7), channel_id=1, source_target_pairs={{0,2},{2,4},{4,6},{6,8},{8,10},{10,12},{12,14},{14,16},{16,18},{18... | collective-permute-start | bytes 503816 | tf_op jit(solution)/shard_map/ppermute | solution.py:411
  90.9 7.3 %collective-permute-start.10 = (f32[328,128]{1,0:T(8,128)S(1)}, f32[328,128]{1,0:T(8,128)S(1)}, u32[]{:S(2)}, u32[]{:S(2)}) collective-permute-start(f32[328,128]{1,0:T(8,128)S(1)} %collective-permute-done.8), channel_id=1, source_target_pairs={{0,2},{2,4},{4,6},{6,8},{8,10},{10,12},{12,14},{14,16},{16,18},{18... | collective-permute-start | bytes 503816 | tf_op jit(solution)/shard_map/ppermute | solution.py:411
  93.6 7.3 %collective-permute-start.11 = (f32[328,128]{1,0:T(8,128)S(1)}, f32[328,128]{1,0:T(8,128)S(1)}, u32[]{:S(2)}, u32[]{:S(2)}) collective-permute-start(f32[328,128]{1,0:T(8,128)S(1)} %collective-permute-done.9), channel_id=1, source_target_pairs={{0,2},{2,4},{4,6},{6,8},{8,10},{10,12},{12,14},{14,16},{16,18},{18... | collective-permute-start | bytes 503816 | tf_op jit(solution)/shard_map/ppermute | solution.py:411
  98.2 7.3 %collective-permute-start.12 = (f32[328,128]{1,0:T(8,128)S(1)}, f32[328,128]{1,0:T(8,128)S(1)}, u32[]{:S(2)}, u32[]{:S(2)}) collective-permute-start(f32[328,128]{1,0:T(8,128)S(1)} %collective-permute-done.10), channel_id=1, source_target_pairs={{0,2},{2,4},{4,6},{6,8},{8,10},{10,12},{12,14},{14,16},{16,18},{18... | collective-permute-start | bytes 503816 | tf_op jit(solution)/shard_map/ppermute | solution.py:411
  100.9 7.3 %collective-permute-start.13 = (f32[328,128]{1,0:T(8,128)S(1)}, f32[328,128]{1,0:T(8,128)S(1)}, u32[]{:S(2)}, u32[]{:S(2)}) collective-permute-start(f32[328,128]{1,0:T(8,128)S(1)} %collective-permute-done.11), channel_id=1, source_target_pairs={{0,2},{2,4},{4,6},{6,8},{8,10},{10,12},{12,14},{14,16},{16,18},{18... | collective-permute-start | bytes 503816 | tf_op jit(solution)/shard_map/ppermute | solution.py:411
  105.5 7.3 %collective-permute-start.14 = (f32[328,128]{1,0:T(8,128)S(1)}, f32[328,128]{1,0:T(8,128)S(1)}, u32[]{:S(2)}, u32[]{:S(2)}) collective-permute-start(f32[328,128]{1,0:T(8,128)S(1)} %collective-permute-done.12), channel_id=1, source_target_pairs={{0,2},{2,4},{4,6},{6,8},{8,10},{10,12},{12,14},{14,16},{16,18},{18... | collective-permute-start | bytes 503816 | tf_op jit(solution)/shard_map/ppermute | solution.py:411
  108.2 7.3 %collective-permute-start.15 = (f32[328,128]{1,0:T(8,128)S(1)}, f32[328,128]{1,0:T(8,128)S(1)}, u32[]{:S(2)}, u32[]{:S(2)}) collective-permute-start(f32[328,128]{1,0:T(8,128)S(1)} %collective-permute-done.13), channel_id=1, source_target_pairs={{1,31},{3,1},{5,3},{7,5},{9,7},{11,9},{13,11},{15,13},{17,15},{19,... | collective-permute-start | bytes 503816 | tf_op jit(solution)/shard_map/ppermute | solution.py:411
  112.8 6.1 %collective-permute-start.16 = (f32[328,128]{1,0:T(8,128)S(1)}, f32[328,128]{1,0:T(8,128)S(1)}, u32[]{:S(2)}, u32[]{:S(2)}) collective-permute-start(f32[328,128]{1,0:T(8,128)S(1)} %collective-permute-done.14), channel_id=1, source_target_pairs={{1,31},{3,1},{5,3},{7,5},{9,7},{11,9},{13,11},{15,13},{17,15},{19,... | collective-permute-start | bytes 503816 | tf_op jit(solution)/shard_map/ppermute | solution.py:411
  119.6 21.5 %copy-start.3 = (f32[8,2,320,128]{3,2,1,0:T(8,128)}, f32[8,2,320,128]{3,2,1,0:T(8,128)S(1)}, u32[]{:S(2)}) copy-start(f32[8,2,320,128]{3,2,1,0:T(8,128)S(1)} %slice.9.total) | copy-start | bytes 7864324
  119.6 21.5 %collective-permute-start.18 = (f32[8,2,320,128]{3,2,1,0:T(8,128)S(1)}, f32[8,2,320,128]{3,2,1,0:T(8,128)}, u32[]{:S(2)}, u32[]{:S(2)}) collective-permute-start(f32[8,2,320,128]{3,2,1,0:T(8,128)S(1)} %slice.9.total), channel_id=1, source_target_pairs={{0,1},{1,0},{2,3},{3,2},{4,5},{5,4},{6,7},{7,6},{8,9},{9,8},{10,11... | collective-permute-start | bytes 7864328 | tf_op jit(solution)/shard_map/ppermute | solution.py:402
  135.4 5.7 %collective-permute-start.17 = (f32[16,64,128]{2,1,0:T(8,128)S(1)}, f32[16,64,128]{2,1,0:T(8,128)}, u32[]{:S(2)}, u32[]{:S(2)}) collective-permute-start(f32[16,64,128]{2,1,0:T(8,128)S(1)} %bitcast.80), channel_id=1, source_target_pairs={{0,1},{1,0},{2,3},{3,2},{4,5},{5,4},{6,7},{7,6},{8,9},{9,8},{10,11... | collective-permute-start | bytes 1572872 | tf_op jit(solution)/shard_map/ppermute | solution.py:402
  141.1 1.7 copy-start.4
  155.1 1.5 copy-start
  182.8 6.7 %collective-permute-start.19 = (f32[16,64,128]{2,1,0:T(8,128)S(1)}, f32[16,64,128]{2,1,0:T(8,128)S(1)}, u32[]{:S(2)}, u32[]{:S(2)}) collective-permute-start(f32[16,64,128]{2,1,0:T(8,128)S(1)} %all_to_all.38.own), channel_id=1, source_target_pairs={{0,1},{1,0},{2,3},{3,2},{4,5},{5,4},{6,7},{7,6},{8,9},{9,8},{10,11... | collective-permute-start | bytes 1572872 | tf_op jit(solution)/shard_map/ppermute | solution.py:402
  189.4 1.7 copy-start.1
  226.5 6.8 %collective-permute-start.20 = (f32[16,64,128]{2,1,0:T(8,128)S(1)}, f32[16,64,128]{2,1,0:T(8,128)}, u32[]{:S(2)}, u32[]{:S(2)}) collective-permute-start(f32[16,64,128]{2,1,0:T(8,128)S(1)} %all_to_all.40.own), channel_id=1, source_target_pairs={{0,1},{1,0},{2,3},{3,2},{4,5},{5,4},{6,7},{7,6},{8,9},{9,8},{10,11... | collective-permute-start | bytes 1572872 | tf_op jit(solution)/shard_map/ppermute | solution.py:402
  233.3 1.7 copy-start.2
  235.1 29.5 %copy-start.5 = (bf16[1,128,5120]{2,1,0:T(8,128)(2,1)S(1)}, bf16[1,128,5120]{2,1,0:T(8,128)(2,1)}, u32[]{:S(2)}) copy-start(bf16[1,128,5120]{2,1,0:T(8,128)(2,1)} %param.3) | copy-start | bytes 3932164
  235.1 29.5 %copy-start.6 = (bf16[1,128,5120]{2,1,0:T(8,128)(2,1)S(1)}, bf16[1,128,5120]{2,1,0:T(8,128)(2,1)}, u32[]{:S(2)}) copy-start(bf16[1,128,5120]{2,1,0:T(8,128)(2,1)} %param.4) | copy-start | bytes 3932164
  259.2 5.3 %collective-permute-start.21 = (f32[16,80,128]{2,1,0:T(8,128)S(1)}, f32[16,80,128]{2,1,0:T(8,128)S(1)}, u32[]{:S(2)}, u32[]{:S(2)}) collective-permute-start(f32[16,80,128]{2,1,0:T(8,128)S(1)} %all_to_all.41.own), channel_id=1, source_target_pairs={{0,1},{1,0},{2,3},{3,2},{4,5},{5,4},{6,7},{7,6},{8,9},{9,8},{10,11... | collective-permute-start | bytes 1966088 | tf_op jit(solution)/shard_map/ppermute | solution.py:402

commit v8 on v7

--- a/solution.py
+++ b/solution.py
@@ -100,7 +100,7 @@
     )(grads, errors, q_start)
 
 
-def inverse_factor(gram_twice):
+def inverse_factor(gram_twice, beside=None):
     rank, wide = gram_twice.shape
     step = 8
     count = rank // step
@@ -125,6 +125,8 @@
 
     done = []
     for p in range(count):
+        if beside is not None:
+            beside(p, count)
         panel = a[p]
         f = [spread(panel, p * step + j) for j in range(step)]
         pivots = jnp.ones((step, wide), F32)
@@ -193,16 +195,24 @@
 CHUNK = 512
 
 
-def right_of(held, high, low):
-    rank = held.shape[0] // 4
-    cut, n = high.shape
-    one = jnp.zeros((2 * rank, cut), F32)
-    two = jnp.zeros((rank, cut), F32)
-    for at in range(0, n, CHUNK):
-        x = held[: 2 * rank, at : at + CHUNK]
-        one = one + dot(x, high[:, at : at + CHUNK], NT)
-        two = two + dot(x[:rank], low[:, at : at + CHUNK], NT)
-    return one[:rank] + (one[rank:] + two)
+class Right:
+    def __init__(self, held, high, low):
+        rank = held.shape[0] // 4
+        self.refs = held, high, low
+        self.one = jnp.zeros((2 * rank, high.shape[0]), F32)
+        self.two = jnp.zeros((rank, high.shape[0]), F32)
+
+    def add(self, p, count):
+        held, high, low = self.refs
+        size = high.shape[1] // count
+        x = held[: 2 * self.two.shape[0], p * size : (p + 1) * size]
+        span = slice(p * size, (p + 1) * size)
+        self.one = self.one + dot(x, high[:, span], NT)
+        self.two = self.two + dot(x[: self.two.shape[0]], low[:, span], NT)
+
+    def total(self):
+        rank = self.two.shape[0]
+        return self.one[:rank] + (self.one[rank:] + self.two)
 
 
 def planes(info, length, mine):
@@ -216,22 +226,23 @@
     return at
 
 
-def orthonormal(info, own, other, held):
-    length = own.shape[0]
+def orthonormal(info, own, other, held, high, low, beside=None):
+    length, rank = own.shape[:2]
     for mine, blocks in ((True, own), (False, other)):
         at = planes(info, length, mine)
         for j in range(length // 2):
             put(held, at(j), jnp.concatenate([blocks[2 * j], blocks[2 * j + 1]], axis=1))
-    left = weights(inverse_factor(gram_of(held, CHUNK)))
+    left = weights(inverse_factor(gram_of(held, CHUNK), beside))
     for at in range(0, held.shape[1], CHUNK):
         y = dot(left, held[:, at : at + CHUNK], NN)
-        put(held, at, y[: y.shape[0] // 3] + (y[y.shape[0] // 3 : 2 * y.shape[0] // 3] + y[2 * y.shape[0] // 3 :]))
-    return inverse_factor(gram_of(held, CHUNK))
-
-
-def right_factor(scale, second, held, high, low):
+        put(held, at, y[:rank] + (y[rank : 2 * rank] + y[2 * rank :]))
+    right = Right(held, high, low)
+    second = inverse_factor(gram_of(held, CHUNK), right.add)
+    return second, right.total()
+
+
+def right_factor(scale, second, right):
     left = second[:, : second.shape[0]] * scale
-    right = right_of(held, high, low)
     return jnp.dot(left, right, precision=lax.Precision.HIGHEST, preferred_element_type=F32)
 
 
@@ -250,27 +261,30 @@
 
 def first_kernel(scale, info, own, other, total, total_other, out, high, low, held):
     half = total.shape[0]
-    for mine, blocks in ((True, total), (False, total_other)):
-        at = planes(info, 2 * half, mine)
-        core = info[1] if mine else 1 - info[1]
-        for j in range(half):
-            for stream in range(2):
-                side = core if stream == 0 else 1 - core
-                span = pl.ds(pl.multiple_of(at(j) + side * LANES, LANES), LANES)
-                high[:, span], low[:, span] = split2(blocks[j, stream])
-    second = orthonormal(info, own, other, held)
-    next_left(info, right_factor(scale, second, held, high, low), high, low, out)
+
+    def split(p, count):
+        for mine, blocks in ((True, total), (False, total_other)):
+            at = planes(info, 2 * half, mine)
+            core = info[1] if mine else 1 - info[1]
+            for j in range(p * half // count, (p + 1) * half // count):
+                for stream in range(2):
+                    side = core if stream == 0 else 1 - core
+                    span = pl.ds(pl.multiple_of(at(j) + side * LANES, LANES), LANES)
+                    high[:, span], low[:, span] = split2(blocks[j, stream])
+
+    second, right = orthonormal(info, own, other, held, high, low, split)
+    next_left(info, right_factor(scale, second, right), high, low, out)
 
 
 def step_kernel(scale, info, own, other, high, low, out, held):
-    second = orthonormal(info, own, other, held)
-    next_left(info, right_factor(scale, second, held, high, low), high, low, out)
+    second, right = orthonormal(info, own, other, held, high, low)
+    next_left(info, right_factor(scale, second, right), high, low, out)
 
 
 def last_kernel(scale, info, own, other, high, low, out, basis, held):
     length, rank, rows = own.shape
-    second = orthonormal(info, own, other, held)
-    q = right_factor(scale, second, held, high, low)
+    second, right = orthonormal(info, own, other, held, high, low)
+    q = right_factor(scale, second, right)
     half = rank // 2
     quarter = half // 2
     rest = jnp.concatenate([q[:, 2 * LANES :], jnp.zeros_like(q[:, 2 * LANES :])], axis=1)

time: 269 us -> 269 us (level)
  no operation moved by 1% of the time
where the time goes in v8:
time: 269 us; the launch traced here: 268 us
  blocking collectives  120 us (45%)
  starting transfers between devices  91.3 us (34%)
  Pallas kernels  37.8 us (14%)
  waiting for transfers between devices  9.41 us (3%)
  local copies, waits for them, and re-layouts  7.71 us (3%)
    all_to_all x7, blocking collectives, exchange(): return lax.all_to_all(chunks, axis, 0, 0)  120 us
    ppermute x16, starting transfers between devices, ring(): lax.ppermute(blocks[-1], ('z', 'core'), up + down if s < half - 1 else down)  65 us
    ppermute x6, starting transfers between devices, swap_cores(): return lax.ppermute(block, 'core', [(0, 1), (1, 0)])  26.3 us
    pallas_call x1, Pallas kernels, first(): pl.pallas_call(functools.partial(first_kernel, scale), in_specs=[SMEM_SPE...  12.2 us
    pallas_call x1, Pallas kernels, step(): pl.pallas_call(functools.partial(step_kernel, scale), in_specs=[SMEM_SPEC...  9.19 us
    pallas_call x1, Pallas kernels, last(): pl.pallas_call(functools.partial(last_kernel, scale), in_specs=[SMEM_SPEC...  9.12 us
    unnamed x14, local copies, waits for them, and re-layouts  6.73 us
    ppermute x6, waiting for transfers between devices, swap_cores(): return lax.ppermute(block, 'core', [(0, 1), (1, 0)])  6.03 us
  transfers between devices with their start and end apart: 22, of which 5 were waited for; matrix products, arithmetic and copies ran while one was open for 0% of the time, Pallas kernels for 0%

profile of v8, /device:TPU:1, one launch (start us, length us, event | category | flops | bytes accessed | tf_op | source)
XLA Modules:
  0.0 267.6 jit_solution(14978051713940997542)
XLA Ops:
  0.6 4.3 %start.1 = f32[16,328,128]{2,1,0:T(8,128)} custom-call(bf16[128,5120]{1,0:T(8,128)(2,1)} %bitcast.76, bf16[128,5120]{1,0:T(8,128)(2,1)} %bitcast.78, f32[64,5120]{1,0:T(8,128)} %q_start.1), custom_call_target="tpu_custom_call" | custom-call | tf_op jit(solution)/shard_map/start/pallas_call | solution.py:85
  4.9 39.2 %all_to_all.35 = f32[16,328,128]{2,1,0:T(8,128)S(1)} all-to-all(f32[16,328,128]{2,1,0:T(8,128)} %start.1), channel_id=1, replica_groups=mesh['rep'=16,'z'=16,'core'=2] {'rep'}, dimensions={0} | all-to-all | bytes 5373952 | tf_op jit(solution)/shard_map/all_to_all | solution.py:408
  44.2 6.0 %collective-permute-start.1 = (f32[328,128]{1,0:T(8,128)S(1)}, f32[328,128]{1,0:T(8,128)S(1)}, u32[]{:S(2)}, u32[]{:S(2)}) collective-permute-start(f32[328,128]{1,0:T(8,128)S(1)} %reduce_sum.27), channel_id=1, source_target_pairs={{0,1},{1,0},{2,3},{3,2},{4,5},{5,4},{6,7},{7,6},{8,9},{9,8},{10,11... | collective-permute-start | bytes 503816 | tf_op jit(solution)/shard_map/ppermute | solution.py:416
  50.2 11.5 %collective-permute-start = (f32[328,128]{1,0:T(8,128)S(1)}, f32[328,128]{1,0:T(8,128)S(1)}, u32[]{:S(2)}, u32[]{:S(2)}) collective-permute-start(f32[328,128]{1,0:T(8,128)S(1)} %reduce_sum.27), channel_id=1, source_target_pairs={{0,2},{2,4},{4,6},{6,8},{8,10},{10,12},{12,14},{14,16},{16,18},{18... | collective-permute-start | bytes 503816 | tf_op jit(solution)/shard_map/ppermute | solution.py:425
  64.3 4.6 %collective-permute-start.3 = (f32[328,128]{1,0:T(8,128)S(1)}, f32[328,128]{1,0:T(8,128)S(1)}, u32[]{:S(2)}, u32[]{:S(2)}) collective-permute-start(f32[328,128]{1,0:T(8,128)S(1)} %collective-permute-done), channel_id=1, source_target_pairs={{0,2},{2,4},{4,6},{6,8},{8,10},{10,12},{12,14},{14,16},{16,18},{18... | collective-permute-start | bytes 503816 | tf_op jit(solution)/shard_map/ppermute | solution.py:425
  69.0 2.6 collective-permute-start.4
  71.6 4.6 %collective-permute-start.5 = (f32[328,128]{1,0:T(8,128)S(1)}, f32[328,128]{1,0:T(8,128)S(1)}, u32[]{:S(2)}, u32[]{:S(2)}) collective-permute-start(f32[328,128]{1,0:T(8,128)S(1)} %collective-permute-done.3), channel_id=1, source_target_pairs={{0,2},{2,4},{4,6},{6,8},{8,10},{10,12},{12,14},{14,16},{16,18},{18... | collective-permute-start | bytes 503816 | tf_op jit(solution)/shard_map/ppermute | solution.py:425
  76.3 2.6 collective-permute-start.6
  79.0 4.6 %collective-permute-start.7 = (f32[328,128]{1,0:T(8,128)S(1)}, f32[328,128]{1,0:T(8,128)S(1)}, u32[]{:S(2)}, u32[]{:S(2)}) collective-permute-start(f32[328,128]{1,0:T(8,128)S(1)} %collective-permute-done.5), channel_id=1, source_target_pairs={{0,2},{2,4},{4,6},{6,8},{8,10},{10,12},{12,14},{14,16},{16,18},{18... | collective-permute-start | bytes 503816 | tf_op jit(solution)/shard_map/ppermute | solution.py:425
  83.6 2.6 collective-permute-start.8
  86.3 4.6 %collective-permute-start.9 = (f32[328,128]{1,0:T(8,128)S(1)}, f32[328,128]{1,0:T(8,128)S(1)}, u32[]{:S(2)}, u32[]{:S(2)}) collective-permute-start(f32[328,128]{1,0:T(8,128)S(1)} %collective-permute-done.7), channel_id=1, source_target_pairs={{0,2},{2,4},{4,6},{6,8},{8,10},{10,12},{12,14},{14,16},{16,18},{18... | collective-permute-start | bytes 503816 | tf_op jit(solution)/shard_map/ppermute | solution.py:425
  90.9 2.6 collective-permute-start.10
  93.6 4.6 %collective-permute-start.11 = (f32[328,128]{1,0:T(8,128)S(1)}, f32[328,128]{1,0:T(8,128)S(1)}, u32[]{:S(2)}, u32[]{:S(2)}) collective-permute-start(f32[328,128]{1,0:T(8,128)S(1)} %collective-permute-done.9), channel_id=1, source_target_pairs={{0,2},{2,4},{4,6},{6,8},{8,10},{10,12},{12,14},{14,16},{16,18},{18... | collective-permute-start | bytes 503816 | tf_op jit(solution)/shard_map/ppermute | solution.py:425
  98.2 2.6 collective-permute-start.12
  100.9 4.6 %collective-permute-start.13 = (f32[328,128]{1,0:T(8,128)S(1)}, f32[328,128]{1,0:T(8,128)S(1)}, u32[]{:S(2)}, u32[]{:S(2)}) collective-permute-start(f32[328,128]{1,0:T(8,128)S(1)} %collective-permute-done.11), channel_id=1, source_target_pairs={{0,2},{2,4},{4,6},{6,8},{8,10},{10,12},{12,14},{14,16},{16,18},{18... | collective-permute-start | bytes 503816 | tf_op jit(solution)/shard_map/ppermute | solution.py:425
  105.5 2.6 collective-permute-start.14
  108.2 4.6 %collective-permute-start.15 = (f32[328,128]{1,0:T(8,128)S(1)}, f32[328,128]{1,0:T(8,128)S(1)}, u32[]{:S(2)}, u32[]{:S(2)}) collective-permute-start(f32[328,128]{1,0:T(8,128)S(1)} %collective-permute-done.13), channel_id=1, source_target_pairs={{1,31},{3,1},{5,3},{7,5},{9,7},{11,9},{13,11},{15,13},{17,15},{19,... | collective-permute-start | bytes 503816 | tf_op jit(solution)/shard_map/ppermute | solution.py:425
  115.6 3.3 %collective-permute-done.16 = f32[328,128]{1,0:T(8,128)S(1)} collective-permute-done((f32[328,128]{1,0:T(8,128)S(1)}, f32[328,128]{1,0:T(8,128)S(1)}, u32[]{:S(2)}, u32[]{:S(2)}) %collective-permute-start.16) | collective-permute-done | bytes 167968 | tf_op jit(solution)/shard_map/ppermute | solution.py:425
  121.6 13.3 %all_to_all.36 = f32[16,64,128]{2,1,0:T(8,128)S(1)} all-to-all(f32[16,64,128]{2,1,0:T(8,128)S(1)} %broadcast_in_dim.15), channel_id=1, replica_groups=mesh['rep'=16,'z'=16,'core'=2] {'rep'}, dimensions={0} | all-to-all | bytes 1048576 | tf_op jit(solution)/shard_map/all_to_all | solution.py:408
  135.4 4.2 %collective-permute-start.17 = (f32[16,64,128]{2,1,0:T(8,128)S(1)}, f32[16,64,128]{2,1,0:T(8,128)}, u32[]{:S(2)}, u32[]{:S(2)}) collective-permute-start(f32[16,64,128]{2,1,0:T(8,128)S(1)} %bitcast.80), channel_id=1, source_target_pairs={{0,1},{1,0},{2,3},{3,2},{4,5},{5,4},{6,7},{7,6},{8,9},{9,8},{10,11... | collective-permute-start | bytes 1572872 | tf_op jit(solution)/shard_map/ppermute | solution.py:416
  142.9 12.2 %first.1 = (f32[16,64,128]{2,1,0:T(8,128)S(1)}, bf16[320,4096]{1,0:T(8,128)(2,1)S(1)}, bf16[320,4096]{1,0:T(8,128)(2,1)S(1)}) custom-call(s32[2]{0:T(128)S(1)} %pad_add_fusion.info, f32[16,64,128]{2,1,0:T(8,128)S(1)} %bitcast.81, f32[16,64,128]{2,1,0:T(8,128)} %collective-permute-done.17.other, f32[8,2,320,128]{3,2,1,0:T(8,128)S(1)} %copy-done.4, ...), custom_call_target="tpu_custom_call" | custom-call | tf_op jit(solution)/shard_map/first/pallas_call | solution.py:310
  156.6 13.3 %all_to_all.37 = f32[16,64,128]{2,1,0:T(8,128)S(1)} all-to-all(f32[16,64,128]{2,1,0:T(8,128)S(1)} %get-tuple-element.9), channel_id=1, replica_groups=mesh['rep'=16,'z'=16,'core'=2] {'rep'}, dimensions={0} | all-to-all | bytes 1048576 | tf_op jit(solution)/shard_map/all_to_all | solution.py:408
  170.1 12.7 %all_to_all.38.own = f32[16,64,128]{2,1,0:T(8,128)S(1)} all-to-all(f32[16,64,128]{2,1,0:T(8,128)S(1)} %broadcast_in_dim.32), channel_id=1, replica_groups=mesh['rep'=16,'z'=16,'core'=2] {'rep'}, dimensions={0} | all-to-all | bytes 1048576 | tf_op jit(solution)/shard_map/all_to_all | solution.py:408
  182.8 5.4 %collective-permute-start.19 = (f32[16,64,128]{2,1,0:T(8,128)S(1)}, f32[16,64,128]{2,1,0:T(8,128)S(1)}, u32[]{:S(2)}, u32[]{:S(2)}) collective-permute-start(f32[16,64,128]{2,1,0:T(8,128)S(1)} %all_to_all.38.own), channel_id=1, source_target_pairs={{0,1},{1,0},{2,3},{3,2},{4,5},{5,4},{6,7},{7,6},{8,9},{9,8},{10,11... | collective-permute-start | bytes 1572872 | tf_op jit(solution)/shard_map/ppermute | solution.py:416
  191.2 9.2 %step.1 = f32[16,64,128]{2,1,0:T(8,128)S(1)} custom-call(s32[2]{0:T(128)S(1)} %pad_add_fusion.info, f32[16,64,128]{2,1,0:T(8,128)S(1)} %all_to_all.38.own, f32[16,64,128]{2,1,0:T(8,128)S(1)} %collective-permute-done.19.other, bf16[320,4096]{1,0:T(8,128)(2,1)S(1)} %get-tuple-element.10.high, bf16[320,4096]{1,0:T(8,128)(2,1)S(1)} %copy-done.1), custom_call_target="tpu_custom_call" | custom-call | tf_op jit(solution)/shard_map/step/pallas_call | solution.py:321
  200.4 13.3 %all_to_all.39 = f32[16,64,128]{2,1,0:T(8,128)S(1)} all-to-all(f32[16,64,128]{2,1,0:T(8,128)S(1)} %step.1), channel_id=1, replica_groups=mesh['rep'=16,'z'=16,'core'=2] {'rep'}, dimensions={0} | all-to-all | bytes 1048576 | tf_op jit(solution)/shard_map/all_to_all | solution.py:408
  213.8 12.7 %all_to_all.40.own = f32[16,64,128]{2,1,0:T(8,128)S(1)} all-to-all(f32[16,64,128]{2,1,0:T(8,128)S(1)} %broadcast_in_dim.33), channel_id=1, replica_groups=mesh['rep'=16,'z'=16,'core'=2] {'rep'}, dimensions={0} | all-to-all | bytes 1048576 | tf_op jit(solution)/shard_map/all_to_all | solution.py:408
  226.5 5.2 %collective-permute-start.20 = (f32[16,64,128]{2,1,0:T(8,128)S(1)}, f32[16,64,128]{2,1,0:T(8,128)}, u32[]{:S(2)}, u32[]{:S(2)}) collective-permute-start(f32[16,64,128]{2,1,0:T(8,128)S(1)} %all_to_all.40.own), channel_id=1, source_target_pairs={{0,1},{1,0},{2,3},{3,2},{4,5},{5,4},{6,7},{7,6},{8,9},{9,8},{10,11... | collective-permute-start | bytes 1572872 | tf_op jit(solution)/shard_map/ppermute | solution.py:416
  235.1 9.1 %last.1 = (f32[2,80,128]{2,1,0:T(8,128)S(1)}, f32[64,128]{1,0:T(8,128)S(1)}) custom-call(s32[2]{0:T(128)S(1)} %pad_add_fusion.info, f32[16,64,128]{2,1,0:T(8,128)S(1)} %all_to_all.40.own, f32[16,64,128]{2,1,0:T(8,128)} %collective-permute-done.20.other, bf16[320,4096]{1,0:T(8,128)(2,1)S(1)} %get-tuple-element.10.high, bf16[320,4096]{1,0:T(8,128)(2,1)S(1)} %copy-done.2), custom_call_target="tpu_custom_call" | custom-call | tf_op jit(solution)/shard_map/last/pallas_call | solution.py:334
  244.3 15.0 %all_to_all.41.own = f32[16,80,128]{2,1,0:T(8,128)S(1)} all-to-all(f32[16,80,128]{2,1,0:T(8,128)S(1)} %broadcast_in_dim.35), channel_id=1, replica_groups=mesh['rep'=16,'z'=16,'core'=2] {'rep'}, dimensions={0} | all-to-all | bytes 1310720 | tf_op jit(solution)/shard_map/all_to_all | solution.py:408
  259.2 3.6 %collective-permute-start.21 = (f32[16,80,128]{2,1,0:T(8,128)S(1)}, f32[16,80,128]{2,1,0:T(8,128)S(1)}, u32[]{:S(2)}, u32[]{:S(2)}) collective-permute-start(f32[16,80,128]{2,1,0:T(8,128)S(1)} %all_to_all.41.own), channel_id=1, source_target_pairs={{0,1},{1,0},{2,3},{3,2},{4,5},{5,4},{6,7},{7,6},{8,9},{9,8},{10,11... | collective-permute-start | bytes 1966088 | tf_op jit(solution)/shard_map/ppermute | solution.py:416
  264.6 3.0 %finish.1 = (bf16[128,5120]{1,0:T(8,128)(2,1)}, f32[64,5120]{1,0:T(8,128)}) custom-call(s32[1]{0:T(128)} %bitcast.flag, bf16[128,5120]{1,0:T(8,128)(2,1)S(1)} %bitcast.77, bf16[128,5120]{1,0:T(8,128)(2,1)S(1)} %bitcast.79, f32[16,80,128]{2,1,0:T(8,128)S(1)} %all_to_all.41.own, f32[16,80,128]{2,1,0:T(8,128)S(1)} %collective-permute-done.21.other, ...), custom_call_target="tpu_custom_call" | custom-call | tf_op jit(solution)/shard_map/finish/pallas_call | solution.py:396
  (62 shorter events, 21.7 us)
Async XLA Ops:
  44.2 17.5 %collective-permute-start.1 = (f32[328,128]{1,0:T(8,128)S(1)}, f32[328,128]{1,0:T(8,128)S(1)}, u32[]{:S(2)}, u32[]{:S(2)}) collective-permute-start(f32[328,128]{1,0:T(8,128)S(1)} %reduce_sum.27), channel_id=1, source_target_pairs={{0,1},{1,0},{2,3},{3,2},{4,5},{5,4},{6,7},{7,6},{8,9},{9,8},{10,11... | collective-permute-start | bytes 503816 | tf_op jit(solution)/shard_map/ppermute | solution.py:416
  50.2 14.1 %collective-permute-start = (f32[328,128]{1,0:T(8,128)S(1)}, f32[328,128]{1,0:T(8,128)S(1)}, u32[]{:S(2)}, u32[]{:S(2)}) collective-permute-start(f32[328,128]{1,0:T(8,128)S(1)} %reduce_sum.27), channel_id=1, source_target_pairs={{0,2},{2,4},{4,6},{6,8},{8,10},{10,12},{12,14},{14,16},{16,18},{18... | collective-permute-start | bytes 503816 | tf_op jit(solution)/shard_map/ppermute | solution.py:425
  61.7 7.3 %collective-permute-start.2 = (f32[328,128]{1,0:T(8,128)S(1)}, f32[328,128]{1,0:T(8,128)S(1)}, u32[]{:S(2)}, u32[]{:S(2)}) collective-permute-start(f32[328,128]{1,0:T(8,128)S(1)} %collective-permute-done.1), channel_id=1, source_target_pairs={{0,2},{2,4},{4,6},{6,8},{8,10},{10,12},{12,14},{14,16},{16,18},{18... | collective-permute-start | bytes 503816 | tf_op jit(solution)/shard_map/ppermute | solution.py:425
  64.3 7.3 %collective-permute-start.3 = (f32[328,128]{1,0:T(8,128)S(1)}, f32[328,128]{1,0:T(8,128)S(1)}, u32[]{:S(2)}, u32[]{:S(2)}) collective-permute-start(f32[328,128]{1,0:T(8,128)S(1)} %collective-permute-done), channel_id=1, source_target_pairs={{0,2},{2,4},{4,6},{6,8},{8,10},{10,12},{12,14},{14,16},{16,18},{18... | collective-permute-start | bytes 503816 | tf_op jit(solution)/shard_map/ppermute | solution.py:425
  69.0 7.3 %collective-permute-start.4 = (f32[328,128]{1,0:T(8,128)S(1)}, f32[328,128]{1,0:T(8,128)S(1)}, u32[]{:S(2)}, u32[]{:S(2)}) collective-permute-start(f32[328,128]{1,0:T(8,128)S(1)} %collective-permute-done.2), channel_id=1, source_target_pairs={{0,2},{2,4},{4,6},{6,8},{8,10},{10,12},{12,14},{14,16},{16,18},{18... | collective-permute-start | bytes 503816 | tf_op jit(solution)/shard_map/ppermute | solution.py:425
  71.6 7.3 %collective-permute-start.5 = (f32[328,128]{1,0:T(8,128)S(1)}, f32[328,128]{1,0:T(8,128)S(1)}, u32[]{:S(2)}, u32[]{:S(2)}) collective-permute-start(f32[328,128]{1,0:T(8,128)S(1)} %collective-permute-done.3), channel_id=1, source_target_pairs={{0,2},{2,4},{4,6},{6,8},{8,10},{10,12},{12,14},{14,16},{16,18},{18... | collective-permute-start | bytes 503816 | tf_op jit(solution)/shard_map/ppermute | solution.py:425
  76.3 7.3 %collective-permute-start.6 = (f32[328,128]{1,0:T(8,128)S(1)}, f32[328,128]{1,0:T(8,128)S(1)}, u32[]{:S(2)}, u32[]{:S(2)}) collective-permute-start(f32[328,128]{1,0:T(8,128)S(1)} %collective-permute-done.4), channel_id=1, source_target_pairs={{0,2},{2,4},{4,6},{6,8},{8,10},{10,12},{12,14},{14,16},{16,18},{18... | collective-permute-start | bytes 503816 | tf_op jit(solution)/shard_map/ppermute | solution.py:425
  79.0 7.3 %collective-permute-start.7 = (f32[328,128]{1,0:T(8,128)S(1)}, f32[328,128]{1,0:T(8,128)S(1)}, u32[]{:S(2)}, u32[]{:S(2)}) collective-permute-start(f32[328,128]{1,0:T(8,128)S(1)} %collective-permute-done.5), channel_id=1, source_target_pairs={{0,2},{2,4},{4,6},{6,8},{8,10},{10,12},{12,14},{14,16},{16,18},{18... | collective-permute-start | bytes 503816 | tf_op jit(solution)/shard_map/ppermute | solution.py:425
  83.6 7.3 %collective-permute-start.8 = (f32[328,128]{1,0:T(8,128)S(1)}, f32[328,128]{1,0:T(8,128)S(1)}, u32[]{:S(2)}, u32[]{:S(2)}) collective-permute-start(f32[328,128]{1,0:T(8,128)S(1)} %collective-permute-done.6), channel_id=1, source_target_pairs={{0,2},{2,4},{4,6},{6,8},{8,10},{10,12},{12,14},{14,16},{16,18},{18... | collective-permute-start | bytes 503816 | tf_op jit(solution)/shard_map/ppermute | solution.py:425
  86.3 7.3 %collective-permute-start.9 = (f32[328,128]{1,0:T(8,128)S(1)}, f32[328,128]{1,0:T(8,128)S(1)}, u32[]{:S(2)}, u32[]{:S(2)}) collective-permute-start(f32[328,128]{1,0:T(8,128)S(1)} %collective-permute-done.7), channel_id=1, source_target_pairs={{0,2},{2,4},{4,6},{6,8},{8,10},{10,12},{12,14},{14,16},{16,18},{18... | collective-permute-start | bytes 503816 | tf_op jit(solution)/shard_map/ppermute | solution.py:425
  90.9 7.3 %collective-permute-start.10 = (f32[328,128]{1,0:T(8,128)S(1)}, f32[328,128]{1,0:T(8,128)S(1)}, u32[]{:S(2)}, u32[]{:S(2)}) collective-permute-start(f32[328,128]{1,0:T(8,128)S(1)} %collective-permute-done.8), channel_id=1, source_target_pairs={{0,2},{2,4},{4,6},{6,8},{8,10},{10,12},{12,14},{14,16},{16,18},{18... | collective-permute-start | bytes 503816 | tf_op jit(solution)/shard_map/ppermute | solution.py:425
  93.6 7.3 %collective-permute-start.11 = (f32[328,128]{1,0:T(8,128)S(1)}, f32[328,128]{1,0:T(8,128)S(1)}, u32[]{:S(2)}, u32[]{:S(2)}) collective-permute-start(f32[328,128]{1,0:T(8,128)S(1)} %collective-permute-done.9), channel_id=1, source_target_pairs={{0,2},{2,4},{4,6},{6,8},{8,10},{10,12},{12,14},{14,16},{16,18},{18... | collective-permute-start | bytes 503816 | tf_op jit(solution)/shard_map/ppermute | solution.py:425
  98.2 7.3 %collective-permute-start.12 = (f32[328,128]{1,0:T(8,128)S(1)}, f32[328,128]{1,0:T(8,128)S(1)}, u32[]{:S(2)}, u32[]{:S(2)}) collective-permute-start(f32[328,128]{1,0:T(8,128)S(1)} %collective-permute-done.10), channel_id=1, source_target_pairs={{0,2},{2,4},{4,6},{6,8},{8,10},{10,12},{12,14},{14,16},{16,18},{18... | collective-permute-start | bytes 503816 | tf_op jit(solution)/shard_map/ppermute | solution.py:425
  100.9 7.3 %collective-permute-start.13 = (f32[328,128]{1,0:T(8,128)S(1)}, f32[328,128]{1,0:T(8,128)S(1)}, u32[]{:S(2)}, u32[]{:S(2)}) collective-permute-start(f32[328,128]{1,0:T(8,128)S(1)} %collective-permute-done.11), channel_id=1, source_target_pairs={{0,2},{2,4},{4,6},{6,8},{8,10},{10,12},{12,14},{14,16},{16,18},{18... | collective-permute-start | bytes 503816 | tf_op jit(solution)/shard_map/ppermute | solution.py:425
  105.5 7.3 %collective-permute-start.14 = (f32[328,128]{1,0:T(8,128)S(1)}, f32[328,128]{1,0:T(8,128)S(1)}, u32[]{:S(2)}, u32[]{:S(2)}) collective-permute-start(f32[328,128]{1,0:T(8,128)S(1)} %collective-permute-done.12), channel_id=1, source_target_pairs={{0,2},{2,4},{4,6},{6,8},{8,10},{10,12},{12,14},{14,16},{16,18},{18... | collective-permute-start | bytes 503816 | tf_op jit(solution)/shard_map/ppermute | solution.py:425
  108.2 7.3 %collective-permute-start.15 = (f32[328,128]{1,0:T(8,128)S(1)}, f32[328,128]{1,0:T(8,128)S(1)}, u32[]{:S(2)}, u32[]{:S(2)}) collective-permute-start(f32[328,128]{1,0:T(8,128)S(1)} %collective-permute-done.13), channel_id=1, source_target_pairs={{1,31},{3,1},{5,3},{7,5},{9,7},{11,9},{13,11},{15,13},{17,15},{19,... | collective-permute-start | bytes 503816 | tf_op jit(solution)/shard_map/ppermute | solution.py:425
  112.8 6.1 %collective-permute-start.16 = (f32[328,128]{1,0:T(8,128)S(1)}, f32[328,128]{1,0:T(8,128)S(1)}, u32[]{:S(2)}, u32[]{:S(2)}) collective-permute-start(f32[328,128]{1,0:T(8,128)S(1)} %collective-permute-done.14), channel_id=1, source_target_pairs={{1,31},{3,1},{5,3},{7,5},{9,7},{11,9},{13,11},{15,13},{17,15},{19,... | collective-permute-start | bytes 503816 | tf_op jit(solution)/shard_map/ppermute | solution.py:425
  119.6 21.5 %copy-start.3 = (f32[8,2,320,128]{3,2,1,0:T(8,128)}, f32[8,2,320,128]{3,2,1,0:T(8,128)S(1)}, u32[]{:S(2)}) copy-start(f32[8,2,320,128]{3,2,1,0:T(8,128)S(1)} %slice.9.total) | copy-start | bytes 7864324
  119.6 21.5 %collective-permute-start.18 = (f32[8,2,320,128]{3,2,1,0:T(8,128)S(1)}, f32[8,2,320,128]{3,2,1,0:T(8,128)}, u32[]{:S(2)}, u32[]{:S(2)}) collective-permute-start(f32[8,2,320,128]{3,2,1,0:T(8,128)S(1)} %slice.9.total), channel_id=1, source_target_pairs={{0,1},{1,0},{2,3},{3,2},{4,5},{5,4},{6,7},{7,6},{8,9},{9,8},{10,11... | collective-permute-start | bytes 7864328 | tf_op jit(solution)/shard_map/ppermute | solution.py:416
  135.4 5.7 %collective-permute-start.17 = (f32[16,64,128]{2,1,0:T(8,128)S(1)}, f32[16,64,128]{2,1,0:T(8,128)}, u32[]{:S(2)}, u32[]{:S(2)}) collective-permute-start(f32[16,64,128]{2,1,0:T(8,128)S(1)} %bitcast.80), channel_id=1, source_target_pairs={{0,1},{1,0},{2,3},{3,2},{4,5},{5,4},{6,7},{7,6},{8,9},{9,8},{10,11... | collective-permute-start | bytes 1572872 | tf_op jit(solution)/shard_map/ppermute | solution.py:416
  141.1 1.7 copy-start.4
  155.1 1.5 copy-start
  182.8 6.7 %collective-permute-start.19 = (f32[16,64,128]{2,1,0:T(8,128)S(1)}, f32[16,64,128]{2,1,0:T(8,128)S(1)}, u32[]{:S(2)}, u32[]{:S(2)}) collective-permute-start(f32[16,64,128]{2,1,0:T(8,128)S(1)} %all_to_all.38.own), channel_id=1, source_target_pairs={{0,1},{1,0},{2,3},{3,2},{4,5},{5,4},{6,7},{7,6},{8,9},{9,8},{10,11... | collective-permute-start | bytes 1572872 | tf_op jit(solution)/shard_map/ppermute | solution.py:416
  189.5 1.7 copy-start.1
  226.5 6.8 %collective-permute-start.20 = (f32[16,64,128]{2,1,0:T(8,128)S(1)}, f32[16,64,128]{2,1,0:T(8,128)}, u32[]{:S(2)}, u32[]{:S(2)}) collective-permute-start(f32[16,64,128]{2,1,0:T(8,128)S(1)} %all_to_all.40.own), channel_id=1, source_target_pairs={{0,1},{1,0},{2,3},{3,2},{4,5},{5,4},{6,7},{7,6},{8,9},{9,8},{10,11... | collective-permute-start | bytes 1572872 | tf_op jit(solution)/shard_map/ppermute | solution.py:416
  233.3 1.7 copy-start.2
  235.1 29.5 %copy-start.5 = (bf16[1,128,5120]{2,1,0:T(8,128)(2,1)S(1)}, bf16[1,128,5120]{2,1,0:T(8,128)(2,1)}, u32[]{:S(2)}) copy-start(bf16[1,128,5120]{2,1,0:T(8,128)(2,1)} %param.3) | copy-start | bytes 3932164
  235.1 29.5 %copy-start.6 = (bf16[1,128,5120]{2,1,0:T(8,128)(2,1)S(1)}, bf16[1,128,5120]{2,1,0:T(8,128)(2,1)}, u32[]{:S(2)}) copy-start(bf16[1,128,5120]{2,1,0:T(8,128)(2,1)} %param.4) | copy-start | bytes 3932164
  259.2 5.3 %collective-permute-start.21 = (f32[16,80,128]{2,1,0:T(8,128)S(1)}, f32[16,80,128]{2,1,0:T(8,128)S(1)}, u32[]{:S(2)}, u32[]{:S(2)}) collective-permute-start(f32[16,80,128]{2,1,0:T(8,128)S(1)} %all_to_all.41.own), channel_id=1, source_target_pairs={{0,1},{1,0},{2,3},{3,2},{4,5},{5,4},{6,7},{7,6},{8,9},{9,8},{10,11... | collective-permute-start | bytes 1966088 | tf_op jit(solution)/shard_map/ppermute | solution.py:416
